TPU v7x, 512 devices: a whole 4x8x8 slice. The times are simulated.
512 devices in a mesh: ctx: 64 (over z, x, core), hd: 8 (over y).
Axes of the slice: x: 4, y: 8, z: 8, core: 2. Of those that a mesh axis runs over, the one named last changes fastest.
Arguments:
- query_rows: bfloat16 [16384, 4096], P('ctx', 'hd'), may hold values from -240 to 240
- key_rows: bfloat16 [16384, 1024], P('ctx', 'hd'), may hold values from -3.5 to 3.5
- value_rows: bfloat16 [16384, 1024], P('ctx', 'hd'), may hold values from -6 to 6
- doc_ids: int32 [256], P('ctx'), may hold values from 0 to 17, never falling along the last dimension, each value on 1 to 160 neighbouring positions
- out_weight: bfloat16 [4096, 4096], P('hd'), may hold values from -0.125 to 0.125
Outputs:
- attended: bfloat16 [16384, 4096], P('ctx', 'hd')
- projected: bfloat16 [16384, 4096], P('ctx', 'hd')
Inputs may be any that keep to these rules, and one draw needn't show every extreme that they name: `doc_ids`: ids never fall along the stretch; each of the 18 documents spans 1 to 160 whole blocks, and one spans exactly 160.
All inputs are finite; a program needn't handle non-finite values.
Results may differ from a plain program's by a relative error of at most 0.019.
Values may be sent and summed in bfloat16 or wider, within the bound.
No kernel may reach another device: no remote copies, remote signals or barrier semaphores. Data moves between devices by JAX's collectives and lax.ppermute only.
A program may use at most 64 MiB of HBM per device.

v0:
```python
from functools import partial
import math

import jax
import jax.numpy as jnp
from jax import lax
from jax.sharding import PartitionSpec as P

HDIM = 128
BLOCK = 64


NEG_BIG = -1e30


def attend_part(
    softmax_state, shard_part, leading_row, query_heads, query_pos, query_doc, score_scale
):
    key_part, value_part, doc_part = shard_part
    row_count = key_part.shape[0]
    block_len = 256
    kv_local = query_heads.shape[1]
    key_blocks = key_part.reshape(row_count // block_len, block_len, kv_local, HDIM)
    value_blocks = value_part.reshape(row_count // block_len, block_len, kv_local, HDIM)
    doc_blocks = doc_part.reshape(row_count // block_len, block_len)

    def one_block(block_index, running):
        block_keys = key_blocks[block_index]
        block_values = value_blocks[block_index]
        key_pos = block_index * block_len + jnp.arange(block_len, dtype=jnp.int32)
        visible = (key_pos[None, :] <= query_pos[:, None]) & (key_pos[None, :] >= 0)
        visible = visible & (doc_blocks[block_index][None, :] == query_doc[:, None])

        def compute(inner_state):
            old_max, old_sum, old_weighted = inner_state
            scores = (
                jnp.einsum(
                    "tkgd,skd->kgts", query_heads, block_keys, preferred_element_type=jnp.float32
                )
                * score_scale
            )
            scores = jnp.where(visible[None, None], scores, NEG_BIG)
            new_max = jnp.maximum(old_max, jnp.max(scores, axis=-1))
            factor = jnp.exp(old_max - new_max)
            weights = jnp.where(visible[None, None], jnp.exp(scores - new_max[..., None]), 0.0)
            new_sum = old_sum * factor + jnp.sum(weights, axis=-1)
            update = jnp.einsum(
                "kgts,skd->kgtd",
                weights.astype(jnp.bfloat16),
                block_values,
                preferred_element_type=jnp.float32,
            )
            return (new_max, new_sum, old_weighted * factor[..., None] + update)

        return lax.cond(jnp.any(visible), compute, lambda inner_state: inner_state, running)

    return lax.fori_loop(0, row_count // block_len, one_block, softmax_state)


def attention_part(query_rows, key_rows, value_rows, doc_ids):
    tokens_here = query_rows.shape[0]
    kv_local = key_rows.shape[1] // HDIM
    group_size = query_rows.shape[1] // key_rows.shape[1]
    position = lax.axis_index("ctx")
    query_heads = query_rows.reshape(tokens_here, kv_local, group_size, HDIM)
    query_pos = position * tokens_here + jnp.arange(tokens_here, dtype=jnp.int32)
    token_docs = jnp.repeat(doc_ids, BLOCK)
    fold_part = partial(
        attend_part,
        query_heads=query_heads,
        query_pos=query_pos,
        query_doc=token_docs,
        score_scale=1.0 / math.sqrt(HDIM),
    )
    start_state = (
        jnp.full((kv_local, group_size, tokens_here), NEG_BIG, jnp.float32),
        jnp.zeros((kv_local, group_size, tokens_here), jnp.float32),
        jnp.zeros((kv_local, group_size, tokens_here, HDIM), jnp.float32),
    )
    softmax_state = fold_part(
        start_state,
        (
            lax.all_gather(key_rows, "ctx", axis=0, tiled=True),
            lax.all_gather(value_rows, "ctx", axis=0, tiled=True),
            lax.all_gather(token_docs, "ctx", axis=0, tiled=True),
        ),
        jnp.int32(0),
    )
    final_max, final_sum, final_weighted = softmax_state
    attended = final_weighted / final_sum[..., None]
    return (
        attended.transpose(2, 0, 1, 3)
        .reshape(tokens_here, kv_local * group_size * HDIM)
        .astype(jnp.bfloat16)
    )


def per_device(query_rows, key_rows, value_rows, doc_ids, out_weight):
    attended = attention_part(query_rows, key_rows, value_rows, doc_ids)
    partial_proj = jnp.dot(attended, out_weight, preferred_element_type=jnp.float32)
    projected = lax.psum_scatter(
        partial_proj.astype(jnp.bfloat16), "hd", scatter_dimension=1, tiled=True
    )
    return (attended, projected)


def solution(mesh):
    in_specs = (P("ctx", "hd"), P("ctx", "hd"), P("ctx", "hd"), P("ctx"), P("hd", None))
    out_specs = (P("ctx", "hd"), P("ctx", "hd"))
    return jax.shard_map(
        per_device, mesh=mesh, in_specs=in_specs, out_specs=out_specs, check_vma=False
    )
```

profile of v0, /device:TPU:6, one launch (start us, length us, event | category | flops | bytes accessed | tf_op | source)
XLA Modules:
  0.0 503.7 jit_solution(16923461428096324373)
XLA Ops:
  8.7 1.1 copy.14
  10.8 49.5 %all-gather = s32[64,1,256]{2,1,0:T(1,128)S(1)} all-gather(s32[1,1,256]{2,1,0:T(1,128)S(1)} %reshape.90), channel_id=1, replica_groups=mesh['ctx'=64,'hd'=8] {'ctx'}, dimensions={0}, use_global_device_ids=true | all-gather | bytes 66560 | tf_op jit(solution)/shard_map/all_gather | solution.py:85
  60.2 39.9 %all-gather.4.cloned.1.call-done = bf16[16384,128]{1,0:T(8,128)(2,1)} async-done(((bf16[256,128]{1,0:T(8,128)(2,1)}), bf16[16384,128]{1,0:T(8,128)(2,1)}) %all-gather.4.cloned.1.call-update) | async-done | bytes 4194320 | tf_op jit(solution)/shard_map/all_gather | solution.py:83
  100.1 85.3 %all-gather.6.cloned.1.call-done = bf16[16384,128]{1,0:T(8,128)(2,1)} async-done(((bf16[256,128]{1,0:T(8,128)(2,1)}), bf16[16384,128]{1,0:T(8,128)(2,1)}) %all-gather.6.cloned.1.call-update) | async-done | bytes 4194320 | tf_op jit(solution)/shard_map/all_gather | solution.py:84
  185.5 154.3 %while.18 = (s32[]{:T(128)}, f32[1,4,256]{2,1,0:T(4,128)S(1)}, f32[1,4,256]{2,1,0:T(4,128)S(1)}, f32[1,4,256,128]{3,2,1,0:T(8,128)S(1)}, s32[64,256]{1,0:T(8,128...) while((s32[]{:T(128)}, f32[1,4,256]{2,1,0:T(4,128)S(1)}, ...), condition=%wide.region_6.7_spmd.clone, body=%wide.region_0.6_spmd.clone.sunk | while | flops 137170944 | bytes 4928287 | solution.py:57
  186.4 0.8 fusion.29
  188.7 0.8 fusion.29
  191.1 0.8 fusion.29
  193.5 0.8 fusion.29
  202.0 2.8 conditional.3
  202.0 1.2 fusion.25
  203.2 1.3 fusion.6
  205.7 0.8 fusion.29
  219.9 0.8 fusion.29
  222.3 0.8 fusion.29
  224.6 0.8 fusion.29
  227.0 0.8 fusion.29
  243.6 0.8 fusion.29
  245.9 0.8 fusion.29
  248.3 0.8 fusion.29
  250.7 0.8 fusion.29
  264.9 0.8 fusion.29
  267.2 0.8 fusion.29
  269.6 0.8 fusion.29
  272.0 0.8 fusion.29
  288.6 0.8 fusion.29
  290.9 0.8 fusion.29
  293.3 0.8 fusion.29
  295.7 0.8 fusion.29
  309.9 0.8 fusion.29
  340.2 4.9 convolution_convert_fusion
  345.2 152.0 %reduce-scatter.2.cloned.1.call-done = bf16[256,512]{1,0:T(8,128)(2,1)} async-done(((bf16[256,4096]{1,0:T(8,128)(2,1)}), bf16[256,512]{1,0:T(8,128)(2,1)}) %reduce-scatter.2.cloned.1.call-update) | async-done | bytes 262160 | tf_op jit(solution)/shard_map/reduce_scatter | solution.py:101
  (447 shorter events, 92.6 us)
Async XLA Ops:
  7.2 92.9 %all-gather.4.cloned.1.call-start = ((), (), s32[]{:S(2)}) async-start(), calls=%async_computation.1 | async-start | bytes 4259840 | tf_op jit(solution)/shard_map/all_gather | solution.py:83
  7.9 177.5 %all-gather.6.cloned.1.call-start = ((), (), s32[]{:S(2)}) async-start(), calls=%async_computation.2 | async-start | bytes 4259840 | tf_op jit(solution)/shard_map/all_gather | solution.py:84
  8.6 488.5 %reduce-scatter.2.cloned.1.call-start = ((), (), s32[]{:S(2)}) async-start(), calls=%async_computation.3 | async-start | bytes 2359296 | tf_op jit(solution)/shard_map/reduce_scatter | solution.py:101
  340.2 4.9 copy-start
Sparse Core Ops, SparseCore 0:
  11.3 88.7 all-gather.3
  103.4 81.9 all-gather.5
  345.3 151.8 reduce-scatter.1
where the time goes:
time: 509 us; the launch traced here: 504 us
  waiting for transfers between devices  279 us (55%)
  local copies, waits for them, and re-layouts  55 us (11%)
  other arithmetic  54.5 us (11%)
  blocking collectives  49.5 us (10%)
  loops' own time  44.8 us (9%)
  between operations  13.8 us (3%)
  matrix products  7.41 us (1%)
    reduce_scatter x1, waiting for transfers between devices, per_device(): lax.psum_scatter(partial_proj.astype(jnp.bfloat16), 'hd', scatter_dimensi...  152 us
    all_gather x1, waiting for transfers between devices, attention_part(): lax.all_gather(value_rows, 'ctx', axis=0, tiled=True)  85.3 us
    reduce_or x64, other arithmetic, one_block(): jnp.any(visible)  53 us
    all_gather x1, blocking collectives, attention_part(): lax.all_gather(token_docs, 'ctx', axis=0, tiled=True)  49.5 us
    broadcast_in_dim x65, local copies, waits for them, and re-layouts, attention_part(): token_docs = jnp.repeat(doc_ids, BLOCK)  47.2 us
    another operation x1, loops' own time, attend_part(): return lax.fori_loop(0, row_count // block_len, one_block, softmax_state)  43.9 us
    all_gather x1, waiting for transfers between devices, attention_part(): lax.all_gather(key_rows, 'ctx', axis=0, tiled=True)  39.9 us
  transfers between devices with their start and end apart: 3, of which 3 were waited for; matrix products, arithmetic and copies ran while one was open for 0% of the time, Pallas kernels for 0%

commit v1 on v0

v1 whole, which is shorter than its diff:
```python
import functools
import math

import jax
import jax.numpy as jnp
from jax import lax
from jax.experimental import pallas as pl
from jax.experimental.pallas import tpu as pltpu
from jax.sharding import PartitionSpec as P

HDIM = 128
BLOCK = 64
ROWS = 256
GROUP = 4
NZ, NX, NC = 8, 4, 2
QCOLS = GROUP * ROWS
PAD = 16
NEG_BIG = -1e30
SCALE = math.log2(math.e) / math.sqrt(HDIM)

X_GROUPS = [[(z * NX + x) * NC + c for x in range(NX)] for z in range(NZ) for c in range(NC)]
Z_GROUPS = [[(z * NX + x) * NC + c for z in range(NZ)] for x in range(NX) for c in range(NC)]


def ctx_perm(move):
    pairs = []
    for index in range(NZ * NX * NC):
        z, x, c = index // (NX * NC), (index // NC) % NX, index % NC
        z, x, c = move(z, x, c)
        pairs.append((index, ((z % NZ) * NX + x % NX) * NC + c % NC))
    return pairs


def attend_kernel(
    place, q_ids, own_ids, other_ids, q0, q1, q2, q3, kv_own, kv_other,
    out, v_turned, total, high, norm,
):
    index = place[0]
    z, x, c = lax.div(index, NX * NC), lax.rem(lax.div(index, NC), NX), lax.rem(index, NC)
    queries = (q0, q1, q2, q3)

    def turn(zk, carry):
        v_turned[zk, :, 0:ROWS] = kv_own[zk, ROWS : 2 * ROWS, :].T
        v_turned[zk, :, ROWS : 2 * ROWS] = kv_other[zk, ROWS : 2 * ROWS, :].T
        return carry

    lax.fori_loop(0, z + 1, turn, 0)

    for r in range(NX):
        q_ref = queries[r]
        xq = lax.rem(x - r + NX, NX)
        q_first = ((z * NX + xq) * NC + c) * ROWS
        total[...] = jnp.zeros_like(total)
        high[...] = jnp.full_like(high, NEG_BIG)
        norm[...] = jnp.zeros_like(norm)

        def fold(zk, masked):
            if masked:
                key_first = (zk * NX + x) * (NC * ROWS)
                q_block = lax.broadcasted_iota(jnp.int32, (1, ROWS), 1)
                low = jnp.zeros((1, ROWS), jnp.int32)
                for b in range(ROWS // BLOCK):
                    before = jnp.int32(0)
                    for kb in range(ROWS // BLOCK):
                        before += jnp.where(own_ids[zk, kb] < q_ids[r, b], 1, 0)
                        before += jnp.where(other_ids[zk, kb] < q_ids[r, b], 1, 0)
                    low = jnp.where(q_block >= b * BLOCK, key_first + before * BLOCK, low)
                q_pos = q_first + q_block
                rows = lax.broadcasted_iota(jnp.int32, (ROWS, ROWS), 0)
                pos_own = rows + (key_first + c * ROWS)
                pos_other = rows + (key_first + (1 - c) * ROWS)
                seen_own = (pos_own >= low) & (pos_own <= q_pos)
                seen_other = (pos_other >= low) & (pos_other <= q_pos)
            k_own = kv_own[zk, 0:ROWS, :]
            k_other = kv_other[zk, 0:ROWS, :]
            for h in range(GROUP):
                cols = slice(h * ROWS, (h + 1) * ROWS)
                q_head = q_ref[0:ROWS, h * HDIM : (h + 1) * HDIM]
                dims = (((1,), (1,)), ((), ()))
                s_own = lax.dot_general(k_own, q_head, dims, preferred_element_type=jnp.float32)
                s_other = lax.dot_general(k_other, q_head, dims, preferred_element_type=jnp.float32)
                if masked:
                    s_own = jnp.where(seen_own, s_own, NEG_BIG)
                    s_other = jnp.where(seen_other, s_other, NEG_BIG)
                old = high[0:1, cols]
                new = jnp.maximum(
                    jnp.max(jnp.maximum(s_own, s_other), axis=0, keepdims=True), old
                )
                factor = jnp.exp2((old - new) * SCALE)
                p_own = jnp.exp2((s_own - new) * SCALE)
                p_other = jnp.exp2((s_other - new) * SCALE)
                if masked:
                    p_own = jnp.where(seen_own, p_own, 0.0)
                    p_other = jnp.where(seen_other, p_other, 0.0)
                high[0:1, cols] = new
                norm[0:1, cols] = norm[0:1, cols] * factor + jnp.sum(
                    p_own + p_other, axis=0, keepdims=True
                )
                update = jnp.dot(
                    v_turned[zk, :, 0:ROWS],
                    p_own.astype(jnp.bfloat16),
                    preferred_element_type=jnp.float32,
                ) + jnp.dot(
                    v_turned[zk, :, ROWS : 2 * ROWS],
                    p_other.astype(jnp.bfloat16),
                    preferred_element_type=jnp.float32,
                )
                total[:, cols] = total[:, cols] * factor + update

        def step(zk, carry):
            key_first = (zk * NX + x) * (NC * ROWS)
            k_low = jnp.minimum(own_ids[zk, 0], other_ids[zk, 0])
            k_top = jnp.maximum(own_ids[zk, 3], other_ids[zk, 3])
            q_low, q_top = q_ids[r, 0], q_ids[r, 3]
            some = (key_first <= q_first + ROWS - 1) & (k_top >= q_low)
            whole = (key_first + NC * ROWS - 1 <= q_first) & (k_low == q_top)

            @pl.when(some & whole)
            def _():
                fold(zk, False)

            @pl.when(some & jnp.logical_not(whole))
            def _():
                fold(zk, True)

            return carry

        lax.fori_loop(0, z + 1, step, 0)

        sums = norm[0:1, :]
        seen = sums > 0.0
        safe = jnp.where(seen, sums, 1.0)
        level = jnp.where(seen, high[0:1, :] * SCALE + jnp.log2(safe), NEG_BIG)
        first = level.astype(jnp.bfloat16).astype(jnp.float32)
        rest = level - first
        second = rest.astype(jnp.bfloat16).astype(jnp.float32)
        third = rest - second
        row = lax.broadcasted_iota(jnp.int32, (PAD, QCOLS), 0)
        stats = jnp.where(row == 0, first, jnp.where(row == 1, second, jnp.where(row == 2, third, 0.0)))
        out[xq, 0:HDIM, :] = (total[...] * (1.0 / safe)).astype(jnp.bfloat16)
        out[xq, HDIM : HDIM + PAD, :] = stats.astype(jnp.bfloat16)


def attend(place, q_ids, own_ids, other_ids, blocks, kv_own, kv_other):
    smem = pl.BlockSpec(memory_space=pltpu.SMEM)
    vmem = pl.BlockSpec(memory_space=pltpu.VMEM)
    return pl.pallas_call(
        attend_kernel,
        out_shape=jax.ShapeDtypeStruct((NX, HDIM + PAD, QCOLS), jnp.bfloat16),
        in_specs=[smem] * 4 + [vmem] * 6,
        out_specs=vmem,
        scratch_shapes=[
            pltpu.VMEM((NZ, HDIM, NC * ROWS), jnp.bfloat16),
            pltpu.VMEM((HDIM, QCOLS), jnp.float32),
            pltpu.VMEM((8, QCOLS), jnp.float32),
            pltpu.VMEM((8, QCOLS), jnp.float32),
        ],
        compiler_params=pltpu.CompilerParams(vmem_limit_bytes=24 * 1024 * 1024),
    )(place, q_ids, own_ids, other_ids, *blocks, kv_own, kv_other)


def project_kernel(parts, weight, attended, partial):
    levels = []
    for s in range(NX):
        stats = parts[s, HDIM : HDIM + PAD, :].astype(jnp.float32)
        levels.append(stats[0:1, :] + stats[1:2, :] + stats[2:3, :])
    top = functools.reduce(jnp.maximum, levels)
    shares = [jnp.exp2(level - top) for level in levels]
    inverse = 1.0 / sum(shares)
    mixed = sum(
        parts[s, 0:HDIM, :].astype(jnp.float32) * (shares[s] * inverse) for s in range(NX)
    )
    for h in range(GROUP):
        block = mixed[:, h * ROWS : (h + 1) * ROWS]
        attended[:, h * HDIM : (h + 1) * HDIM] = block.T.astype(jnp.bfloat16)
    width = 512
    for n in range(partial.shape[1] // width):
        cols = slice(n * width, (n + 1) * width)
        partial[:, cols] = jnp.dot(
            attended[...], weight[:, cols], preferred_element_type=jnp.float32
        ).astype(jnp.bfloat16)


def project(parts, weight):
    vmem = pl.BlockSpec(memory_space=pltpu.VMEM)
    return pl.pallas_call(
        project_kernel,
        out_shape=(
            jax.ShapeDtypeStruct((ROWS, GROUP * HDIM), jnp.bfloat16),
            jax.ShapeDtypeStruct((ROWS, weight.shape[1]), jnp.bfloat16),
        ),
        in_specs=[vmem] * 2,
        out_specs=(vmem, vmem),
        compiler_params=pltpu.CompilerParams(vmem_limit_bytes=24 * 1024 * 1024),
    )(parts, weight)


def per_device(query_rows, key_rows, value_rows, doc_ids, out_weight):
    place = lax.axis_index("ctx").reshape(1)
    ids = doc_ids.astype(jnp.bfloat16)[None, :]

    q_packed = jnp.concatenate(
        [query_rows, jnp.pad(ids, ((0, PAD - 1), (0, query_rows.shape[1] - 4)))], axis=0
    )
    q_blocks = [q_packed] + [
        lax.ppermute(q_packed, "ctx", ctx_perm(lambda z, x, c, r=r: (z, x + r, c)))
        for r in range(1, NX)
    ]
    kv_packed = jnp.concatenate(
        [key_rows, value_rows, jnp.pad(ids, ((0, PAD - 1), (0, HDIM - 4)))], axis=0
    )
    kv_own = lax.all_to_all(
        jnp.broadcast_to(kv_packed[None], (NZ,) + kv_packed.shape),
        "ctx",
        0,
        0,
        axis_index_groups=Z_GROUPS,
    )
    kv_other = lax.ppermute(kv_own, "ctx", ctx_perm(lambda z, x, c: (z, x, 1 - c)))

    q_ids = jnp.stack([block[ROWS, 0:4] for block in q_blocks]).astype(jnp.int32)
    own_ids = kv_own[:, 2 * ROWS, 0:4].astype(jnp.int32)
    other_ids = kv_other[:, 2 * ROWS, 0:4].astype(jnp.int32)
    parts = attend(place, q_ids, own_ids, other_ids, q_blocks, kv_own, kv_other)
    parts = lax.all_to_all(parts, "ctx", 0, 0, axis_index_groups=X_GROUPS)
    attended, partial = project(parts, out_weight)
    projected = lax.psum_scatter(partial, "hd", scatter_dimension=1, tiled=True)
    return attended, projected


def solution(mesh):
    in_specs = (P("ctx", "hd"), P("ctx", "hd"), P("ctx", "hd"), P("ctx"), P("hd", None))
    out_specs = (P("ctx", "hd"), P("ctx", "hd"))
    return jax.shard_map(
        per_device, mesh=mesh, in_specs=in_specs, out_specs=out_specs, check_vma=False
    )
```

time: 509 us -> 175 us (0.34)
  waiting for transfers between devices: 279 us -> 79.3 us
  local copies, waits for them, and re-layouts: 55 us -> 0.16 us
  other arithmetic: 54.5 us -> 1.59 us
  loops' own time: 44.8 us -> 0 us
  blocking collectives: 49.5 us -> 61.3 us
  starting transfers between devices: 0.11 us -> 11.7 us
  matrix products: 7.41 us -> 0 us
  Pallas kernels: 0 us -> 6.19 us
    all_gather x2 -> x0, waiting for transfers between devices: 125 us -> none  [the longest x1 85.3 us: attention_part(): lax.all_gather(value_rows, 'ctx', axis=0, tiled=True)]
    reduce_scatter x1, waiting for transfers between devices: 152 us -> 68.4 us  [per_device(): projected = lax.psum_scatter(partial, 'hd', scatter_dimension=1, tiled=True)]
    all_to_all x0 -> x2, blocking collectives: none -> 61.3 us  [the longest x1 39.7 us: per_device(): lax.all_to_all(jnp.broadcast_to(kv_packed[None], (NZ,) + kv_packed.shape)...]
    reduce_or x64 -> x0, other arithmetic: 53 us -> none  [one_block(): jnp.any(visible)]
    all_gather x1 -> x0, blocking collectives: 49.5 us -> none  [attention_part(): lax.all_gather(token_docs, 'ctx', axis=0, tiled=True)]
    broadcast_in_dim x68 -> x1, local copies, waits for them, and re-layouts: 47.3 us -> 0.14 us  [per_device(): jnp.broadcast_to(kv_packed[None], (NZ,) + kv_packed.shape)]
    another operation x65 -> x0, loops' own time: 44.8 us -> none  [the longest x1 43.9 us: attend_part(): return lax.fori_loop(0, row_count // block_len, one_block, softmax_state)]
    ppermute x0 -> x4, starting transfers between devices: none -> 11.7 us  [the longest x3 9.76 us: per_device(): lax.ppermute(q_packed, 'ctx', ctx_perm(lambda z, x, c, r=r: (z, x + r, c)))]
  transfers between devices with their start and end apart: 3 -> 5, of which waited for: 3 -> 3; matrix products, arithmetic and copies ran while one was open for 0% -> 0% of each run, Pallas kernels for 0% -> 0%
where the time goes in v1:
time: 175 us; the launch traced here: 174 us
  waiting for transfers between devices  79.3 us (45%)
  blocking collectives  61.3 us (35%)
  between operations  14.1 us (8%)
  starting transfers between devices  11.7 us (7%)
  Pallas kernels  6.19 us (4%)
    reduce_scatter x1, waiting for transfers between devices, per_device(): projected = lax.psum_scatter(partial, 'hd', scatter_dimension=1, tiled=True)  68.4 us
    all_to_all x1, blocking collectives, per_device(): lax.all_to_all(jnp.broadcast_to(kv_packed[None], (NZ,) + kv_packed.shape)...  39.7 us
    all_to_all x1, blocking collectives, per_device(): parts = lax.all_to_all(parts, 'ctx', 0, 0, axis_index_groups=X_GROUPS)  21.6 us
    ppermute x3, waiting for transfers between devices, per_device(): lax.ppermute(q_packed, 'ctx', ctx_perm(lambda z, x, c, r=r: (z, x + r, c)))  10.9 us
    ppermute x3, starting transfers between devices, per_device(): lax.ppermute(q_packed, 'ctx', ctx_perm(lambda z, x, c, r=r: (z, x + r, c)))  9.76 us
  transfers between devices with their start and end apart: 5, of which 3 were waited for; matrix products, arithmetic and copies ran while one was open for 0% of the time, Pallas kernels for 0%

profile of v1, /device:TPU:6, one launch (start us, length us, event | category | flops | bytes accessed | tf_op | source)
XLA Modules:
  0.0 174.4 jit_solution(5650366477415159042)
XLA Ops:
  7.2 0.0 reduce-scatter.2.cloned.1.call-start
  7.2 0.7 convert_bitcast_fusion
  7.9 0.9 fusion.3
  8.8 0.1 broadcast_in_dim.10
  8.9 0.0 copy-start.1
  8.9 39.7 %all_to_all.10.kv_own = bf16[8,528,128]{2,1,0:T(8,128)(2,1)S(1)} all-to-all(bf16[8,528,128]{2,1,0:T(8,128)(2,1)S(1)} %broadcast_in_dim.10), channel_id=1, replica_groups={{0,64,128,192,256,320,384,448},{8,72,136,200,264,328,392,456},{16,80,14..., dimensions={0} | all-to-all | bytes 2162688 | tf_op jit(solution)/shard_map/all_to_all | solution.py:212
  48.6 1.9 %collective-permute-start.3 = (bf16[8,528,128]{2,1,0:T(8,128)(2,1)S(1)}, bf16[8,528,128]{2,1,0:T(8,128)(2,1)S(1)}, u32[]{:S(2)}, u32[]{:S(2)}) collective-permute-start(bf16[8,528,128]{2,1,0:T(8,128)(2,1)S(1)} %all_to_all.10.kv_own), channel_id=1, source_target_pairs={{0,8},{8,0},{16,24},{24,16},{32,40},{40,32},{48,56},{56,48},{64,72... | collective-permute-start | bytes 3244040 | tf_op jit(solution)/shard_map/ppermute | solution.py:219
  50.5 0.0 copy-done.1
  50.5 2.7 %collective-permute-start.2 = (bf16[272,512]{1,0:T(8,128)(2,1)S(1)}, bf16[272,512]{1,0:T(8,128)(2,1)S(1)}, u32[]{:S(2)}, u32[]{:S(2)}) collective-permute-start(bf16[272,512]{1,0:T(8,128)(2,1)S(1)} %fusion.1.q0), channel_id=1, source_target_pairs={{0,48},{8,56},{16,0},{24,8},{32,16},{40,24},{48,32},{56,40},{64,11... | collective-permute-start | bytes 835592 | tf_op jit(solution)/shard_map/ppermute | solution.py:206
  53.3 3.0 %collective-permute-start.1 = (bf16[272,512]{1,0:T(8,128)(2,1)S(1)}, bf16[272,512]{1,0:T(8,128)(2,1)S(1)}, u32[]{:S(2)}, u32[]{:S(2)}) collective-permute-start(bf16[272,512]{1,0:T(8,128)(2,1)S(1)} %fusion.1.q0), channel_id=1, source_target_pairs={{0,32},{8,40},{16,48},{24,56},{32,0},{40,8},{48,16},{56,24},{64,96... | collective-permute-start | bytes 835592 | tf_op jit(solution)/shard_map/ppermute | solution.py:206
  56.3 4.0 %collective-permute-start = (bf16[272,512]{1,0:T(8,128)(2,1)S(1)}, bf16[272,512]{1,0:T(8,128)(2,1)S(1)}, u32[]{:S(2)}, u32[]{:S(2)}) collective-permute-start(bf16[272,512]{1,0:T(8,128)(2,1)S(1)} %fusion.1.q0), channel_id=1, source_target_pairs={{0,16},{8,24},{16,32},{24,40},{32,48},{40,56},{48,0},{56,8},{64,80... | collective-permute-start | bytes 835592 | tf_op jit(solution)/shard_map/ppermute | solution.py:206
  60.3 8.3 %collective-permute-done.2.q3 = bf16[272,512]{1,0:T(8,128)(2,1)S(1)} collective-permute-done((bf16[272,512]{1,0:T(8,128)(2,1)S(1)}, bf16[272,512]{1,0:T(8,128)(2,1)S(1)}, u32[]{:S(2)}, u32[]{:S(2)}) %collective-permute-start.2) | collective-permute-done | bytes 278560 | tf_op jit(solution)/shard_map/ppermute | solution.py:206
  68.7 0.0 collective-permute-done.1.q2
  68.7 2.5 %collective-permute-done.q1 = bf16[272,512]{1,0:T(8,128)(2,1)S(1)} collective-permute-done((bf16[272,512]{1,0:T(8,128)(2,1)S(1)}, bf16[272,512]{1,0:T(8,128)(2,1)S(1)}, u32[]{:S(2)}, u32[]{:S(2)}) %collective-permute-start) | collective-permute-done | bytes 278560 | tf_op jit(solution)/shard_map/ppermute | solution.py:206
  71.2 0.0 collective-permute-done.3.kv_other
  71.3 0.0 copy-start
  71.3 3.3 %shard_map.68 = bf16[4,144,1024]{2,1,0:T(8,128)(2,1)S(1)} custom-call(s32[1]{0:T(128)} %bitcast.place, s32[4,4]{1,0:T(4,128)S(1)} %maximum_convert_fusion.q_ids, s32[8,4]{1,0:T(8,128)S(1)} %bitcast.5, s32[8,4]{1,0:T(8,128)S(1)} %bitcast.6, bf16[272,512]{1,0:T(8,128)(2,1)S(1)} %fusion.1.q0, bf16[272,512]{1,0:T(8,128)(2,1)S(1)} %collective-permute-done.q1, ...), custom_call_target="tpu_custom_call" | custom-call | tf_op jit(solution)/shard_map/pallas_call | solution.py:147
  74.6 21.6 %all_to_all.11.parts = bf16[4,144,1024]{2,1,0:T(8,128)(2,1)S(1)} all-to-all(bf16[4,144,1024]{2,1,0:T(8,128)(2,1)S(1)} %shard_map.68), channel_id=1, replica_groups={{0,16,32,48},{8,24,40,56},{64,80,96,112},{72,88,104,120},{128,144,160,1..., dimensions={0} | all-to-all | bytes 2359296 | tf_op jit(solution)/shard_map/all_to_all | solution.py:225
  96.2 0.0 copy-done
  96.2 2.9 %shard_map.69 = (bf16[256,512]{1,0:T(8,128)(2,1)}, bf16[256,4096]{1,0:T(8,128)(2,1)}) custom-call(bf16[4,144,1024]{2,1,0:T(8,128)(2,1)S(1)} %all_to_all.11.parts, bf16[512,4096]{1,0:T(8,128)(2,1)S(1)} %copy-done), custom_call_target="tpu_custom_call" | custom-call | tf_op jit(solution)/shard_map/pallas_call | solution.py:186
  99.1 0.0 reduce-scatter.2.cloned.1.call-update
  99.1 68.4 %reduce-scatter.2.cloned.1.call-done = bf16[256,512]{1,0:T(8,128)(2,1)} async-done(((bf16[256,4096]{1,0:T(8,128)(2,1)}), bf16[256,512]{1,0:T(8,128)(2,1)}) %reduce-scatter.2.cloned.1.call-update) | async-done | bytes 262160 | tf_op jit(solution)/shard_map/reduce_scatter | solution.py:227
  (7 shorter events, 0.1 us)
Async XLA Ops:
  7.2 160.4 %reduce-scatter.2.cloned.1.call-start = ((), (), s32[]{:S(2)}) async-start(), calls=%async_computation.3 | async-start | bytes 2359296 | tf_op jit(solution)/shard_map/reduce_scatter | solution.py:227
  8.9 41.6 %copy-start.1 = (bf16[256,512]{1,0:T(8,128)(2,1)S(1)}, bf16[256,512]{1,0:T(8,128)(2,1)}, u32[]{:S(2)}) copy-start(bf16[256,512]{1,0:T(8,128)(2,1)} %param.5) | copy-start | bytes 786436
  48.6 22.7 %collective-permute-start.3 = (bf16[8,528,128]{2,1,0:T(8,128)(2,1)S(1)}, bf16[8,528,128]{2,1,0:T(8,128)(2,1)S(1)}, u32[]{:S(2)}, u32[]{:S(2)}) collective-permute-start(bf16[8,528,128]{2,1,0:T(8,128)(2,1)S(1)} %all_to_all.10.kv_own), channel_id=1, source_target_pairs={{0,8},{8,0},{16,24},{24,16},{32,40},{40,32},{48,56},{56,48},{64,72... | collective-permute-start | bytes 3244040 | tf_op jit(solution)/shard_map/ppermute | solution.py:219
  50.5 18.1 %collective-permute-start.2 = (bf16[272,512]{1,0:T(8,128)(2,1)S(1)}, bf16[272,512]{1,0:T(8,128)(2,1)S(1)}, u32[]{:S(2)}, u32[]{:S(2)}) collective-permute-start(bf16[272,512]{1,0:T(8,128)(2,1)S(1)} %fusion.1.q0), channel_id=1, source_target_pairs={{0,48},{8,56},{16,0},{24,8},{32,16},{40,24},{48,32},{56,40},{64,11... | collective-permute-start | bytes 835592 | tf_op jit(solution)/shard_map/ppermute | solution.py:206
  53.3 15.4 %collective-permute-start.1 = (bf16[272,512]{1,0:T(8,128)(2,1)S(1)}, bf16[272,512]{1,0:T(8,128)(2,1)S(1)}, u32[]{:S(2)}, u32[]{:S(2)}) collective-permute-start(bf16[272,512]{1,0:T(8,128)(2,1)S(1)} %fusion.1.q0), channel_id=1, source_target_pairs={{0,32},{8,40},{16,48},{24,56},{32,0},{40,8},{48,16},{56,24},{64,96... | collective-permute-start | bytes 835592 | tf_op jit(solution)/shard_map/ppermute | solution.py:206
  56.3 14.9 %collective-permute-start = (bf16[272,512]{1,0:T(8,128)(2,1)S(1)}, bf16[272,512]{1,0:T(8,128)(2,1)S(1)}, u32[]{:S(2)}, u32[]{:S(2)}) collective-permute-start(bf16[272,512]{1,0:T(8,128)(2,1)S(1)} %fusion.1.q0), channel_id=1, source_target_pairs={{0,16},{8,24},{16,32},{24,40},{32,48},{40,56},{48,0},{56,8},{64,80... | collective-permute-start | bytes 835592 | tf_op jit(solution)/shard_map/ppermute | solution.py:206
  71.3 24.9 %copy-start = (bf16[512,4096]{1,0:T(8,128)(2,1)S(1)}, bf16[512,4096]{1,0:T(8,128)(2,1)}, u32[]{:S(2)}) copy-start(bf16[512,4096]{1,0:T(8,128)(2,1)} %weight.1) | copy-start | bytes 12582916
Sparse Core Ops, SparseCore 0:
  99.3 68.2 reduce-scatter.1

commit v2 on v1

v2 whole, which is shorter than its diff:
```python
import functools
import math

import jax
import jax.numpy as jnp
from jax import lax
from jax.experimental import pallas as pl
from jax.experimental.pallas import tpu as pltpu
from jax.sharding import PartitionSpec as P

HDIM = 128
BLOCK = 64
ROWS = 256
GROUP = 4
NZ, NX, NC = 8, 4, 2
QCOLS = GROUP * ROWS
PAD = 16
NEG_BIG = -1e30
SCALE = math.log2(math.e) / math.sqrt(HDIM)

X_GROUPS = [[(z * NX + x) * NC + c for x in range(NX)] for z in range(NZ) for c in range(NC)]
Z_GROUPS = [[(z * NX + x) * NC + c for z in range(NZ)] for x in range(NX) for c in range(NC)]


def ctx_perm(move):
    pairs = []
    for index in range(NZ * NX * NC):
        z, x, c = index // (NX * NC), (index // NC) % NX, index % NC
        z, x, c = move(z, x, c)
        pairs.append((index, ((z % NZ) * NX + x % NX) * NC + c % NC))
    return pairs


def attend_kernel(
    place, q_ids, own_ids, other_ids, q0, q1, q2, q3, kv_own, kv_other,
    out, q_held, k_held, v_turned, scores, total, high, norm,
):
    index = place[0]
    z, x, c = lax.div(index, NX * NC), lax.rem(lax.div(index, NC), NX), lax.rem(index, NC)
    own_at, other_at = pl.multiple_of(c * ROWS, ROWS), pl.multiple_of((1 - c) * ROWS, ROWS)

    for r, q_ref in enumerate((q0, q1, q2, q3)):
        for h in range(GROUP):
            q_held[r, h * ROWS : (h + 1) * ROWS, :] = q_ref[0:ROWS, h * HDIM : (h + 1) * HDIM]

    def hold(zk, carry):
        k_held[zk, pl.ds(own_at, ROWS), :] = kv_own[zk, 0:ROWS, :]
        k_held[zk, pl.ds(other_at, ROWS), :] = kv_other[zk, 0:ROWS, :]
        v_turned[zk, :, pl.ds(own_at, ROWS)] = kv_own[zk, ROWS : 2 * ROWS, :].T
        v_turned[zk, :, pl.ds(other_at, ROWS)] = kv_other[zk, ROWS : 2 * ROWS, :].T
        return carry

    lax.fori_loop(0, z + 1, hold, 0)

    def multiply(r, zk):
        return lax.dot_general(
            k_held[zk], q_held[r], (((1,), (1,)), ((), ())), preferred_element_type=jnp.float32
        )

    def one_block(r, carry):
        xq = lax.rem(x - r + NX, NX)
        q_first = ((z * NX + xq) * NC + c) * ROWS
        q_low, q_top = q_ids[r, 0], q_ids[r, ROWS // BLOCK - 1]
        total[...] = jnp.zeros_like(total)
        high[...] = jnp.full_like(high, NEG_BIG)
        norm[...] = jnp.zeros_like(norm)

        start = jnp.int32(0)
        for zk in range(NZ):
            k_top = jnp.maximum(own_ids[zk, 3], other_ids[zk, 3])
            start += jnp.where((k_top < q_low) & (zk < z), 1, 0)
        stop = jnp.where(xq < x, z, z + 1)

        def fold(slot, zk, masked):
            if masked:
                key_first = (zk * NX + x) * (NC * ROWS)
                token = lax.rem(lax.broadcasted_iota(jnp.int32, (1, QCOLS), 1), ROWS)
                low = jnp.zeros((1, QCOLS), jnp.int32)
                for b in range(ROWS // BLOCK):
                    before = jnp.int32(0)
                    for kb in range(ROWS // BLOCK):
                        before += jnp.where(own_ids[zk, kb] < q_ids[r, b], 1, 0)
                        before += jnp.where(other_ids[zk, kb] < q_ids[r, b], 1, 0)
                    low = jnp.where(token >= b * BLOCK, before * BLOCK, low)
                last = token + (q_first - key_first)
            scores[1 - slot] = multiply(r, jnp.minimum(zk + 1, z))
            now = scores[slot]
            if masked:
                row = lax.broadcasted_iota(jnp.int32, (NC * ROWS, QCOLS), 0)
                now = jnp.where((row >= low) & (row <= last), now, NEG_BIG)
            old = high[0:1, :]
            new = jnp.maximum(jnp.max(now, axis=0, keepdims=True), old)
            factor = jnp.exp2((old - new) * SCALE)
            weights = jnp.exp2((now - new) * SCALE)
            high[0:1, :] = new
            norm[0:1, :] = norm[0:1, :] * factor + jnp.sum(weights, axis=0, keepdims=True)
            total[...] = total[...] * factor + jnp.dot(
                v_turned[zk], weights.astype(jnp.bfloat16), preferred_element_type=jnp.float32
            )

        def turn(slot, zk):
            at = jnp.minimum(zk, NZ - 1)
            k_low = jnp.minimum(own_ids[at, 0], other_ids[at, 0])
            whole = (k_low == q_top) & ((zk < z) | (xq > x))

            @pl.when((zk < stop) & whole)
            def _():
                fold(slot, zk, False)

            @pl.when((zk < stop) & jnp.logical_not(whole))
            def _():
                fold(slot, zk, True)

        def two_turns(i, inner):
            turn(0, start + 2 * i)
            turn(1, start + 2 * i + 1)
            return inner

        @pl.when(start < stop)
        def _():
            scores[0] = multiply(r, start)

        lax.fori_loop(0, lax.div(jnp.maximum(stop - start, 0) + 1, 2), two_turns, 0)

        seen = high[0:1, :] > NEG_BIG
        safe = jnp.where(seen, norm[0:1, :], 1.0)
        share = jnp.where(seen, 1.0 / safe, 0.0)
        level = jnp.where(seen, high[0:1, :] * SCALE + jnp.log2(safe), NEG_BIG)
        first = level.astype(jnp.bfloat16).astype(jnp.float32)
        rest = level - first
        second = rest.astype(jnp.bfloat16).astype(jnp.float32)
        third = rest - second
        row = lax.broadcasted_iota(jnp.int32, (PAD, QCOLS), 0)
        stats = jnp.where(row == 0, first, jnp.where(row == 1, second, jnp.where(row == 2, third, 0.0)))
        out[xq, 0:HDIM, :] = (total[...] * share).astype(jnp.bfloat16)
        out[xq, HDIM : HDIM + PAD, :] = stats.astype(jnp.bfloat16)
        return carry

    lax.fori_loop(0, NX, one_block, 0)


def attend(place, q_ids, own_ids, other_ids, blocks, kv_own, kv_other):
    smem = pl.BlockSpec(memory_space=pltpu.SMEM)
    vmem = pl.BlockSpec(memory_space=pltpu.VMEM)
    return pl.pallas_call(
        attend_kernel,
        out_shape=jax.ShapeDtypeStruct((NX, HDIM + PAD, QCOLS), jnp.bfloat16),
        in_specs=[smem] * 4 + [vmem] * 6,
        out_specs=vmem,
        scratch_shapes=[
            pltpu.VMEM((NX, QCOLS, HDIM), jnp.bfloat16),
            pltpu.VMEM((NZ, NC * ROWS, HDIM), jnp.bfloat16),
            pltpu.VMEM((NZ, HDIM, NC * ROWS), jnp.bfloat16),
            pltpu.VMEM((2, NC * ROWS, QCOLS), jnp.float32),
            pltpu.VMEM((HDIM, QCOLS), jnp.float32),
            pltpu.VMEM((8, QCOLS), jnp.float32),
            pltpu.VMEM((8, QCOLS), jnp.float32),
        ],
        compiler_params=pltpu.CompilerParams(vmem_limit_bytes=32 * 1024 * 1024),
    )(place, q_ids, own_ids, other_ids, *blocks, kv_own, kv_other)


def project_kernel(parts, weight, attended, partial):
    levels = []
    for s in range(NX):
        stats = parts[s, HDIM : HDIM + PAD, :].astype(jnp.float32)
        levels.append(stats[0:1, :] + stats[1:2, :] + stats[2:3, :])
    top = functools.reduce(jnp.maximum, levels)
    shares = [jnp.exp2(level - top) for level in levels]
    inverse = 1.0 / sum(shares)
    mixed = sum(
        parts[s, 0:HDIM, :].astype(jnp.float32) * (shares[s] * inverse) for s in range(NX)
    )
    for h in range(GROUP):
        block = mixed[:, h * ROWS : (h + 1) * ROWS]
        attended[:, h * HDIM : (h + 1) * HDIM] = block.T.astype(jnp.bfloat16)
    width = 512
    for n in range(partial.shape[1] // width):
        cols = slice(n * width, (n + 1) * width)
        partial[:, cols] = jnp.dot(
            attended[...], weight[:, cols], preferred_element_type=jnp.float32
        ).astype(jnp.bfloat16)


def project(parts, weight):
    vmem = pl.BlockSpec(memory_space=pltpu.VMEM)
    return pl.pallas_call(
        project_kernel,
        out_shape=(
            jax.ShapeDtypeStruct((ROWS, GROUP * HDIM), jnp.bfloat16),
            jax.ShapeDtypeStruct((ROWS, weight.shape[1]), jnp.bfloat16),
        ),
        in_specs=[vmem] * 2,
        out_specs=(vmem, vmem),
        compiler_params=pltpu.CompilerParams(vmem_limit_bytes=24 * 1024 * 1024),
    )(parts, weight)


def per_device(query_rows, key_rows, value_rows, doc_ids, out_weight):
    place = lax.axis_index("ctx").reshape(1)
    ids = doc_ids.astype(jnp.bfloat16)[None, :]

    q_packed = jnp.concatenate(
        [query_rows, jnp.pad(ids, ((0, PAD - 1), (0, query_rows.shape[1] - 4)))], axis=0
    )
    q_blocks = [q_packed] + [
        lax.ppermute(q_packed, "ctx", ctx_perm(lambda z, x, c, r=r: (z, x + r, c)))
        for r in range(1, NX)
    ]
    kv_packed = jnp.concatenate(
        [key_rows, value_rows, jnp.pad(ids, ((0, PAD - 1), (0, HDIM - 4)))], axis=0
    )
    kv_own = lax.all_to_all(
        jnp.broadcast_to(kv_packed[None], (NZ,) + kv_packed.shape),
        "ctx",
        0,
        0,
        axis_index_groups=Z_GROUPS,
    )
    *q_blocks, kv_own = lax.optimization_barrier((*q_blocks, kv_own))
    kv_other = lax.ppermute(kv_own, "ctx", ctx_perm(lambda z, x, c: (z, x, 1 - c)))

    q_ids = jnp.stack([block[ROWS, 0:4] for block in q_blocks]).astype(jnp.int32)
    own_ids = kv_own[:, 2 * ROWS, 0:4].astype(jnp.int32)
    other_ids = kv_other[:, 2 * ROWS, 0:4].astype(jnp.int32)
    parts = attend(place, q_ids, own_ids, other_ids, q_blocks, kv_own, kv_other)
    parts = lax.all_to_all(parts, "ctx", 0, 0, axis_index_groups=X_GROUPS)
    attended, partial = project(parts, out_weight)
    projected = lax.psum_scatter(partial, "hd", scatter_dimension=1, tiled=True)
    return attended, projected


def solution(mesh):
    in_specs = (P("ctx", "hd"), P("ctx", "hd"), P("ctx", "hd"), P("ctx"), P("hd", None))
    out_specs = (P("ctx", "hd"), P("ctx", "hd"))
    return jax.shard_map(
        per_device, mesh=mesh, in_specs=in_specs, out_specs=out_specs, check_vma=False
    )
```

time: 175 us -> 142 us (0.81)
  blocking collectives: 61.3 us -> 23.3 us
  starting transfers between devices: 11.7 us -> 22.2 us
  waiting for transfers between devices: 79.3 us -> 72.6 us
    all_to_all x1 -> x0, blocking collectives: 39.7 us -> none  [per_device(): lax.all_to_all(jnp.broadcast_to(kv_packed[None], (NZ,) + kv_packed.shape)...]
    reduce_scatter x1, waiting for transfers between devices: 68.4 us -> 50.4 us  [per_device(): projected = lax.psum_scatter(partial, 'hd', scatter_dimension=1, tiled=True)]
    all_to_all x0 -> x1, starting transfers between devices: none -> 10.4 us  [per_device(): lax.all_to_all(jnp.broadcast_to(kv_packed[None], (NZ,) + kv_packed.shape)...]
    all_to_all x0 -> x1, waiting for transfers between devices: none -> 9.64 us  [per_device(): lax.all_to_all(jnp.broadcast_to(kv_packed[None], (NZ,) + kv_packed.shape)...]
    ppermute x1, waiting for transfers between devices: 0.01 us -> 2.59 us  [per_device(): lax.ppermute(kv_own, 'ctx', ctx_perm(lambda z, x, c: (z, x, 1 - c)))]
  transfers between devices with their start and end apart: 5 -> 6, of which waited for: 3 -> 5; matrix products, arithmetic and copies ran while one was open for 0% -> 0% of each run, Pallas kernels for 0% -> 0%
where the time goes in v2:
time: 142 us; the launch traced here: 141 us
  waiting for transfers between devices  72.6 us (51%)
  blocking collectives  23.3 us (16%)
  starting transfers between devices  22.2 us (16%)
  between operations  14.1 us (10%)
  Pallas kernels  6.11 us (4%)
  other arithmetic  1.59 us (1%)
    reduce_scatter x1, waiting for transfers between devices, per_device(): projected = lax.psum_scatter(partial, 'hd', scatter_dimension=1, tiled=True)  50.4 us
    all_to_all x1, blocking collectives, per_device(): parts = lax.all_to_all(parts, 'ctx', 0, 0, axis_index_groups=X_GROUPS)  23.3 us
    all_to_all x1, starting transfers between devices, per_device(): lax.all_to_all(jnp.broadcast_to(kv_packed[None], (NZ,) + kv_packed.shape)...  10.4 us
    ppermute x3, waiting for transfers between devices, per_device(): lax.ppermute(q_packed, 'ctx', ctx_perm(lambda z, x, c, r=r: (z, x + r, c)))  9.94 us
    ppermute x3, starting transfers between devices, per_device(): lax.ppermute(q_packed, 'ctx', ctx_perm(lambda z, x, c, r=r: (z, x + r, c)))  9.76 us
    all_to_all x1, waiting for transfers between devices, per_device(): lax.all_to_all(jnp.broadcast_to(kv_packed[None], (NZ,) + kv_packed.shape)...  9.64 us
    pallas_call x1, Pallas kernels, attend(): pl.pallas_call(attend_kernel, out_shape=jax.ShapeDtypeStruct((NX, HDIM +...  3.22 us
    pallas_call x1, Pallas kernels, project(): pl.pallas_call(project_kernel, out_shape=(jax.ShapeDtypeStruct((ROWS, GRO...  2.89 us
  transfers between devices with their start and end apart: 6, of which 5 were waited for; matrix products, arithmetic and copies ran while one was open for 0% of the time, Pallas kernels for 0%

profile of v2, /device:TPU:6, one launch (start us, length us, event | category | flops | bytes accessed | tf_op | source)
XLA Modules:
  0.0 141.1 jit_solution(3260450464837060463)
XLA Ops:
  7.2 0.7 convert_bitcast_fusion
  7.8 0.9 fusion.3
  8.7 1.1 broadcast_in_dim.10
  9.8 0.0 copy-start.1
  9.8 10.4 %all-to-all-start = ((bf16[8,528,128]{2,1,0:T(8,128)(2,1)}), bf16[8,528,128]{2,1,0:T(8,128)(2,1)S(1)}, u32[]{:S(2)}, u32[]{:S(2)}) async-start(bf16[8,528,128]{2,1,0:T(8,128)(2,1)} %broadcast_in_dim.10), calls=%async_computation | async-start | bytes 2162688 | tf_op jit(solution)/shard_map/all_to_all | solution.py:213
  20.3 0.0 reduce-scatter.2.cloned.1.call-start
  20.3 0.0 copy-done.1
  20.4 2.7 %collective-permute-start.2 = (bf16[272,512]{1,0:T(8,128)(2,1)S(1)}, bf16[272,512]{1,0:T(8,128)(2,1)S(1)}, u32[]{:S(2)}, u32[]{:S(2)}) collective-permute-start(bf16[272,512]{1,0:T(8,128)(2,1)S(1)} %fusion.1.q0), channel_id=1, source_target_pairs={{0,48},{8,56},{16,0},{24,8},{32,16},{40,24},{48,32},{56,40},{64,11... | collective-permute-start | bytes 835592 | tf_op jit(solution)/shard_map/ppermute | solution.py:207
  23.1 3.0 %collective-permute-start.1 = (bf16[272,512]{1,0:T(8,128)(2,1)S(1)}, bf16[272,512]{1,0:T(8,128)(2,1)S(1)}, u32[]{:S(2)}, u32[]{:S(2)}) collective-permute-start(bf16[272,512]{1,0:T(8,128)(2,1)S(1)} %fusion.1.q0), channel_id=1, source_target_pairs={{0,32},{8,40},{16,48},{24,56},{32,0},{40,8},{48,16},{56,24},{64,96... | collective-permute-start | bytes 835592 | tf_op jit(solution)/shard_map/ppermute | solution.py:207
  26.1 4.0 %collective-permute-start = (bf16[272,512]{1,0:T(8,128)(2,1)S(1)}, bf16[272,512]{1,0:T(8,128)(2,1)S(1)}, u32[]{:S(2)}, u32[]{:S(2)}) collective-permute-start(bf16[272,512]{1,0:T(8,128)(2,1)S(1)} %fusion.1.q0), channel_id=1, source_target_pairs={{0,16},{8,24},{16,32},{24,40},{32,48},{40,56},{48,0},{56,8},{64,80... | collective-permute-start | bytes 835592 | tf_op jit(solution)/shard_map/ppermute | solution.py:207
  30.1 7.4 %collective-permute-done.2.q3 = bf16[272,512]{1,0:T(8,128)(2,1)S(1)} collective-permute-done((bf16[272,512]{1,0:T(8,128)(2,1)S(1)}, bf16[272,512]{1,0:T(8,128)(2,1)S(1)}, u32[]{:S(2)}, u32[]{:S(2)}) %collective-permute-start.2) | collective-permute-done | bytes 278560 | tf_op jit(solution)/shard_map/ppermute | solution.py:207
  37.6 0.0 collective-permute-done.1.q2
  37.6 2.5 %collective-permute-done.q1 = bf16[272,512]{1,0:T(8,128)(2,1)S(1)} collective-permute-done((bf16[272,512]{1,0:T(8,128)(2,1)S(1)}, bf16[272,512]{1,0:T(8,128)(2,1)S(1)}, u32[]{:S(2)}, u32[]{:S(2)}) %collective-permute-start) | collective-permute-done | bytes 278560 | tf_op jit(solution)/shard_map/ppermute | solution.py:207
  40.1 9.6 %all-to-all-done.kv_own = bf16[8,528,128]{2,1,0:T(8,128)(2,1)S(1)} async-done(((bf16[8,528,128]{2,1,0:T(8,128)(2,1)}), bf16[8,528,128]{2,1,0:T(8,128)(2,1)S(1)}, u32[]{:S(2)}, u32[]{:S(2)}) %all-to-all-start) | async-done | bytes 1081376 | tf_op jit(solution)/shard_map/all_to_all | solution.py:213
  49.7 1.9 %collective-permute-start.3 = (bf16[8,528,128]{2,1,0:T(8,128)(2,1)S(1)}, bf16[8,528,128]{2,1,0:T(8,128)(2,1)S(1)}, u32[]{:S(2)}, u32[]{:S(2)}) collective-permute-start(bf16[8,528,128]{2,1,0:T(8,128)(2,1)S(1)} %all-to-all-done.kv_own), channel_id=1, source_target_pairs={{0,8},{8,0},{16,24},{24,16},{32,40},{40,32},{48,56},{56,48},{64,72... | collective-permute-start | bytes 3244040 | tf_op jit(solution)/shard_map/ppermute | solution.py:221
  51.7 2.6 %collective-permute-done.3.kv_other = bf16[8,528,128]{2,1,0:T(8,128)(2,1)S(1)} collective-permute-done((bf16[8,528,128]{2,1,0:T(8,128)(2,1)S(1)}, bf16[8,528,128]{2,1,0:T(8,128)(2,1)S(1)}, u32[]{:S(2)}, u32[]{:S(2)}) %collective-permute-start.3) | collective-permute-done | bytes 1081376 | tf_op jit(solution)/shard_map/ppermute | solution.py:221
  54.3 0.0 copy-start
  54.3 3.2 %shard_map.68 = bf16[4,144,1024]{2,1,0:T(8,128)(2,1)S(1)} custom-call(s32[1]{0:T(128)} %bitcast.place, s32[4,4]{1,0:T(4,128)S(1)} %maximum_convert_fusion.q_ids, s32[8,4]{1,0:T(8,128)S(1)} %bitcast.5, s32[8,4]{1,0:T(8,128)S(1)} %bitcast.6, bf16[272,512]{1,0:T(8,128)(2,1)S(1)} %fusion.1.q0, bf16[272,512]{1,0:T(8,128)(2,1)S(1)} %collective-permute-done.q1, ...), custom_call_target="tpu_custom_call" | custom-call | tf_op jit(solution)/shard_map/pallas_call | solution.py:145
  57.6 23.3 %all_to_all.10.parts = bf16[4,144,1024]{2,1,0:T(8,128)(2,1)S(1)} all-to-all(bf16[4,144,1024]{2,1,0:T(8,128)(2,1)S(1)} %shard_map.68), channel_id=1, replica_groups={{0,16,32,48},{8,24,40,56},{64,80,96,112},{72,88,104,120},{128,144,160,1..., dimensions={0} | all-to-all | bytes 2359296 | tf_op jit(solution)/shard_map/all_to_all | solution.py:227
  80.9 0.0 copy-done
  80.9 2.9 %shard_map.69 = (bf16[256,512]{1,0:T(8,128)(2,1)}, bf16[256,4096]{1,0:T(8,128)(2,1)}) custom-call(bf16[4,144,1024]{2,1,0:T(8,128)(2,1)S(1)} %all_to_all.10.parts, bf16[512,4096]{1,0:T(8,128)(2,1)S(1)} %copy-done), custom_call_target="tpu_custom_call" | custom-call | tf_op jit(solution)/shard_map/pallas_call | solution.py:187
  83.8 0.0 reduce-scatter.2.cloned.1.call-update
  83.8 50.4 %reduce-scatter.2.cloned.1.call-done = bf16[256,512]{1,0:T(8,128)(2,1)} async-done(((bf16[256,4096]{1,0:T(8,128)(2,1)}), bf16[256,512]{1,0:T(8,128)(2,1)}) %reduce-scatter.2.cloned.1.call-update) | async-done | bytes 262160 | tf_op jit(solution)/shard_map/reduce_scatter | solution.py:229
  (8 shorter events, 0.1 us)
Async XLA Ops:
  9.8 10.5 %copy-start.1 = (bf16[256,512]{1,0:T(8,128)(2,1)S(1)}, bf16[256,512]{1,0:T(8,128)(2,1)}, u32[]{:S(2)}) copy-start(bf16[256,512]{1,0:T(8,128)(2,1)} %param.5) | copy-start | bytes 786436
  9.8 39.9 %all-to-all-start = ((bf16[8,528,128]{2,1,0:T(8,128)(2,1)}), bf16[8,528,128]{2,1,0:T(8,128)(2,1)S(1)}, u32[]{:S(2)}, u32[]{:S(2)}) async-start(bf16[8,528,128]{2,1,0:T(8,128)(2,1)} %broadcast_in_dim.10), calls=%async_computation | async-start | bytes 2162688 | tf_op jit(solution)/shard_map/all_to_all | solution.py:213
  20.3 114.0 %reduce-scatter.2.cloned.1.call-start = ((), (), s32[]{:S(2)}) async-start(), calls=%async_computation.3 | async-start | bytes 2359296 | tf_op jit(solution)/shard_map/reduce_scatter | solution.py:229
  20.4 17.2 %collective-permute-start.2 = (bf16[272,512]{1,0:T(8,128)(2,1)S(1)}, bf16[272,512]{1,0:T(8,128)(2,1)S(1)}, u32[]{:S(2)}, u32[]{:S(2)}) collective-permute-start(bf16[272,512]{1,0:T(8,128)(2,1)S(1)} %fusion.1.q0), channel_id=1, source_target_pairs={{0,48},{8,56},{16,0},{24,8},{32,16},{40,24},{48,32},{56,40},{64,11... | collective-permute-start | bytes 835592 | tf_op jit(solution)/shard_map/ppermute | solution.py:207
  23.1 14.4 %collective-permute-start.1 = (bf16[272,512]{1,0:T(8,128)(2,1)S(1)}, bf16[272,512]{1,0:T(8,128)(2,1)S(1)}, u32[]{:S(2)}, u32[]{:S(2)}) collective-permute-start(bf16[272,512]{1,0:T(8,128)(2,1)S(1)} %fusion.1.q0), channel_id=1, source_target_pairs={{0,32},{8,40},{16,48},{24,56},{32,0},{40,8},{48,16},{56,24},{64,96... | collective-permute-start | bytes 835592 | tf_op jit(solution)/shard_map/ppermute | solution.py:207
  26.1 14.0 %collective-permute-start = (bf16[272,512]{1,0:T(8,128)(2,1)S(1)}, bf16[272,512]{1,0:T(8,128)(2,1)S(1)}, u32[]{:S(2)}, u32[]{:S(2)}) collective-permute-start(bf16[272,512]{1,0:T(8,128)(2,1)S(1)} %fusion.1.q0), channel_id=1, source_target_pairs={{0,16},{8,24},{16,32},{24,40},{32,48},{40,56},{48,0},{56,8},{64,80... | collective-permute-start | bytes 835592 | tf_op jit(solution)/shard_map/ppermute | solution.py:207
  49.7 4.6 %collective-permute-start.3 = (bf16[8,528,128]{2,1,0:T(8,128)(2,1)S(1)}, bf16[8,528,128]{2,1,0:T(8,128)(2,1)S(1)}, u32[]{:S(2)}, u32[]{:S(2)}) collective-permute-start(bf16[8,528,128]{2,1,0:T(8,128)(2,1)S(1)} %all-to-all-done.kv_own), channel_id=1, source_target_pairs={{0,8},{8,0},{16,24},{24,16},{32,40},{40,32},{48,56},{56,48},{64,72... | collective-permute-start | bytes 3244040 | tf_op jit(solution)/shard_map/ppermute | solution.py:221
  54.3 26.6 %copy-start = (bf16[512,4096]{1,0:T(8,128)(2,1)S(1)}, bf16[512,4096]{1,0:T(8,128)(2,1)}, u32[]{:S(2)}) copy-start(bf16[512,4096]{1,0:T(8,128)(2,1)} %weight.1) | copy-start | bytes 12582916
Sparse Core Ops, SparseCore 0:
  83.9 50.2 reduce-scatter.1

commit v3 on v2

v3 whole, which is shorter than its diff:
```python
import functools
import math

import jax
import jax.numpy as jnp
from jax import lax
from jax.experimental import pallas as pl
from jax.experimental.pallas import tpu as pltpu
from jax.sharding import PartitionSpec as P

HDIM = 128
BLOCK = 64
ROWS = 256
GROUP = 4
NZ, NX, NC = 8, 4, 2
NY = 8
QCOLS = GROUP * ROWS
PAD = 16
NEG_BIG = -1e30
SCALE = math.log2(math.e) / math.sqrt(HDIM)

X_GROUPS = [[(z * NX + x) * NC + c for x in range(NX)] for z in range(NZ) for c in range(NC)]
Z_GROUPS = [[(z * NX + x) * NC + c for z in range(NZ)] for x in range(NX) for c in range(NC)]


def ctx_perm(move):
    pairs = []
    for index in range(NZ * NX * NC):
        z, x, c = index // (NX * NC), (index // NC) % NX, index % NC
        z, x, c = move(z, x, c)
        pairs.append((index, ((z % NZ) * NX + x % NX) * NC + c % NC))
    return pairs


def hold_kernel(place, kv_own, kv_other, k_held, v_turned):
    index = place[0]
    z, c = lax.div(index, NX * NC), lax.rem(index, NC)
    own_at, other_at = pl.multiple_of(c * ROWS, ROWS), pl.multiple_of((1 - c) * ROWS, ROWS)

    def hold(zk, carry):
        k_held[zk, pl.ds(own_at, ROWS), :] = kv_own[zk, 0:ROWS, :]
        k_held[zk, pl.ds(other_at, ROWS), :] = kv_other[zk, 0:ROWS, :]
        v_turned[zk, :, pl.ds(own_at, ROWS)] = kv_own[zk, ROWS : 2 * ROWS, :].T
        v_turned[zk, :, pl.ds(other_at, ROWS)] = kv_other[zk, ROWS : 2 * ROWS, :].T
        return carry

    lax.fori_loop(0, z + 1, hold, 0)


def attend_kernel(
    shifts, place, q_ids, own_ids, other_ids, *refs
):
    count = len(shifts)
    q_refs, (k_held, v_turned, out, q_held, bounds, scores, total, high, norm) = refs[:count], refs[count:]
    index = place[0]
    z, x, c = lax.div(index, NX * NC), lax.rem(lax.div(index, NC), NX), lax.rem(index, NC)

    for n, q_ref in enumerate(q_refs):
        for h in range(GROUP):
            q_held[n, h * ROWS : (h + 1) * ROWS, :] = q_ref[0:ROWS, h * HDIM : (h + 1) * HDIM]
        start = jnp.int32(0)
        for zk in range(NZ):
            k_top = jnp.maximum(own_ids[zk, 3], other_ids[zk, 3])
            start += jnp.where((k_top < q_ids[shifts[n], 0]) & (zk < z), 1, 0)
        xq = lax.rem(x - shifts[n] + NX, NX)
        bounds[n, 0] = start
        bounds[n, 1] = jnp.maximum(jnp.where(xq < x, z, z + 1), start + 1)
        bounds[n, 2] = xq
        bounds[n, 3] = shifts[n]
    for k in range(4):
        bounds[count, k] = bounds[count - 1, k]

    def multiply(n, zk):
        return lax.dot_general(
            k_held[zk], q_held[n], (((1,), (1,)), ((), ())), preferred_element_type=jnp.float32
        )

    def fold(slot, n, zk, next_n, next_zk, masked):
        r, xq = bounds[n, 3], bounds[n, 2]
        if masked:
            q_first = ((z * NX + xq) * NC + c) * ROWS
            key_first = (zk * NX + x) * (NC * ROWS)
            token = lax.rem(lax.broadcasted_iota(jnp.int32, (1, QCOLS), 1), ROWS)
            low = jnp.zeros((1, QCOLS), jnp.int32)
            for b in range(ROWS // BLOCK):
                before = jnp.int32(0)
                for kb in range(ROWS // BLOCK):
                    before += jnp.where(own_ids[zk, kb] < q_ids[r, b], 1, 0)
                    before += jnp.where(other_ids[zk, kb] < q_ids[r, b], 1, 0)
                low = jnp.where(token >= b * BLOCK, before * BLOCK, low)
            last = token + (q_first - key_first)
        scores[1 - slot] = multiply(next_n, next_zk)
        now = scores[slot]
        if masked:
            row = lax.broadcasted_iota(jnp.int32, (NC * ROWS, QCOLS), 0)
            now = jnp.where((row >= low) & (row <= last), now, NEG_BIG)
        old = high[0:1, :]
        new = jnp.maximum(jnp.max(now, axis=0, keepdims=True), old)
        factor = jnp.exp2((old - new) * SCALE)
        weights = jnp.exp2((now - new) * SCALE)
        high[0:1, :] = new
        norm[0:1, :] = norm[0:1, :] * factor + jnp.sum(weights, axis=0, keepdims=True)
        total[...] = total[...] * factor + jnp.dot(
            v_turned[zk], weights.astype(jnp.bfloat16), preferred_element_type=jnp.float32
        )

    def clear():
        total[...] = jnp.zeros_like(total)
        high[...] = jnp.full_like(high, NEG_BIG)
        norm[...] = jnp.zeros_like(norm)

    def write(n):
        seen = high[0:1, :] > NEG_BIG
        safe = jnp.where(seen, norm[0:1, :], 1.0)
        share = jnp.where(seen, 1.0 / safe, 0.0)
        level = jnp.where(seen, high[0:1, :] * SCALE + jnp.log2(safe), NEG_BIG)
        first = level.astype(jnp.bfloat16).astype(jnp.float32)
        rest = level - first
        second = rest.astype(jnp.bfloat16).astype(jnp.float32)
        third = rest - second
        row = lax.broadcasted_iota(jnp.int32, (PAD, QCOLS), 0)
        stats = jnp.where(row == 0, first, jnp.where(row == 1, second, jnp.where(row == 2, third, 0.0)))
        at = bounds[n, 2]
        out[at, 0:HDIM, :] = (total[...] * share).astype(jnp.bfloat16)
        out[at, HDIM : HDIM + PAD, :] = stats.astype(jnp.bfloat16)

    def turn(slot, n, zk):
        live = n < count
        at = jnp.minimum(n, count - 1)
        ends = zk + 1 >= bounds[at, 1]
        next_n = jnp.where(ends, n + 1, n)
        next_zk = jnp.where(ends, bounds[jnp.minimum(n + 1, count), 0], zk + 1)
        ready_n = jnp.minimum(next_n, count - 1)
        k_low = jnp.minimum(own_ids[zk, 0], other_ids[zk, 0])
        whole = (k_low == q_ids[bounds[at, 3], ROWS // BLOCK - 1]) & ((zk < z) | (bounds[at, 2] > x))

        @pl.when(live & whole)
        def _():
            fold(slot, at, zk, ready_n, next_zk, False)

        @pl.when(live & jnp.logical_not(whole))
        def _():
            fold(slot, at, zk, ready_n, next_zk, True)

        @pl.when(live & ends)
        def _():
            write(at)
            clear()

        return jnp.where(live, next_n, n), jnp.where(live, next_zk, zk)

    def two_turns(i, carry):
        return turn(1, *turn(0, *carry))

    clear()
    scores[0] = multiply(0, bounds[0, 0])
    tiles = jnp.int32(0)
    for n in range(count):
        tiles += bounds[n, 1] - bounds[n, 0]
    lax.fori_loop(0, lax.div(tiles + 1, 2), two_turns, (jnp.int32(0), bounds[0, 0]))


SMEM = pl.BlockSpec(memory_space=pltpu.SMEM)
VMEM = pl.BlockSpec(memory_space=pltpu.VMEM)


def hold(place, kv_own, kv_other):
    return pl.pallas_call(
        hold_kernel,
        out_shape=(
            jax.ShapeDtypeStruct((NZ, NC * ROWS, HDIM), jnp.bfloat16),
            jax.ShapeDtypeStruct((NZ, HDIM, NC * ROWS), jnp.bfloat16),
        ),
        in_specs=[SMEM, VMEM, VMEM],
        out_specs=(VMEM, VMEM),
        compiler_params=pltpu.CompilerParams(vmem_limit_bytes=24 * 1024 * 1024),
    )(place, kv_own, kv_other)


def attend(shifts, place, q_ids, own_ids, other_ids, q_blocks, k_held, v_turned):
    count = len(shifts)
    pairs = count * NZ * NC * ROWS * QCOLS // 2
    return pl.pallas_call(
        functools.partial(attend_kernel, shifts),
        out_shape=jax.ShapeDtypeStruct((NX, HDIM + PAD, QCOLS), jnp.bfloat16),
        in_specs=[SMEM] * 4 + [VMEM] * (count + 2),
        out_specs=VMEM,
        scratch_shapes=[
            pltpu.VMEM((count, QCOLS, HDIM), jnp.bfloat16),
            pltpu.SMEM((count + 1, 4), jnp.int32),
            pltpu.VMEM((2, NC * ROWS, QCOLS), jnp.float32),
            pltpu.VMEM((HDIM, QCOLS), jnp.float32),
            pltpu.VMEM((8, QCOLS), jnp.float32),
            pltpu.VMEM((8, QCOLS), jnp.float32),
        ],
        compiler_params=pltpu.CompilerParams(vmem_limit_bytes=24 * 1024 * 1024),
        cost_estimate=pl.CostEstimate(
            flops=4 * HDIM * pairs, bytes_accessed=4 * NZ * NC * ROWS * HDIM, transcendentals=pairs
        ),
    )(place, q_ids, own_ids, other_ids, *[q_blocks[r] for r in shifts], k_held, v_turned)


def column_share(attended, weight, y, step, columns):
    width = weight.shape[1] // NY
    at = pl.multiple_of(lax.rem(y + step + NY, NY) * width, width)
    picked = weight[:, pl.ds(at, width)][:, columns]
    return jnp.dot(attended[...], picked, preferred_element_type=jnp.float32).astype(jnp.bfloat16)


def far_kernel(y, parts, weight, attended, ahead3, behind3, ahead4, behind4):
    levels = []
    for s in range(NX):
        stats = parts[s, HDIM : HDIM + PAD, :].astype(jnp.float32)
        levels.append(stats[0:1, :] + stats[1:2, :] + stats[2:3, :])
    top = functools.reduce(jnp.maximum, levels)
    shares = [jnp.exp2(level - top) for level in levels]
    inverse = 1.0 / sum(shares)
    mixed = sum(
        parts[s, 0:HDIM, :].astype(jnp.float32) * (shares[s] * inverse) for s in range(NX)
    )
    for h in range(GROUP):
        block = mixed[:, h * ROWS : (h + 1) * ROWS]
        attended[:, h * HDIM : (h + 1) * HDIM] = block.T.astype(jnp.bfloat16)
    half = ahead4.shape[1]
    everything = slice(0, 2 * half)
    ahead3[...] = column_share(attended, weight, y[0], 3, everything)
    behind3[...] = column_share(attended, weight, y[0], -3, everything)
    ahead4[...] = column_share(attended, weight, y[0], 4, slice(0, half))
    behind4[...] = column_share(attended, weight, y[0], 4, slice(half, 2 * half))


def near_kernel(y, attended, weight, ahead1, behind1, ahead2, behind2, here):
    everything = slice(0, here.shape[1])
    for out, step in ((ahead2, 2), (behind2, -2), (ahead1, 1), (behind1, -1), (here, 0)):
        out[...] = column_share(attended, weight, y[0], step, everything)


def project_far(y, parts, weight):
    width = weight.shape[1] // NY
    whole = jax.ShapeDtypeStruct((ROWS, width), jnp.bfloat16)
    half = jax.ShapeDtypeStruct((ROWS, width // 2), jnp.bfloat16)
    return pl.pallas_call(
        far_kernel,
        out_shape=(
            jax.ShapeDtypeStruct((ROWS, GROUP * HDIM), jnp.bfloat16), whole, whole, half, half,
        ),
        in_specs=[SMEM, VMEM, VMEM],
        out_specs=(VMEM,) * 5,
        compiler_params=pltpu.CompilerParams(vmem_limit_bytes=24 * 1024 * 1024),
        cost_estimate=pl.CostEstimate(
            flops=ROWS * weight.size, bytes_accessed=weight.size, transcendentals=0
        ),
    )(y, parts, weight)


def project_near(y, attended, weight):
    whole = jax.ShapeDtypeStruct((ROWS, weight.shape[1] // NY), jnp.bfloat16)
    return pl.pallas_call(
        near_kernel,
        out_shape=(whole,) * 5,
        in_specs=[SMEM, VMEM, VMEM],
        out_specs=(VMEM,) * 5,
        compiler_params=pltpu.CompilerParams(vmem_limit_bytes=24 * 1024 * 1024),
        cost_estimate=pl.CostEstimate(
            flops=ROWS * weight.size, bytes_accessed=weight.size, transcendentals=0
        ),
    )(y, attended, weight)


def sum_over_hd(far, near):
    ahead3, behind3, ahead4, behind4 = far
    ahead1, behind1, ahead2, behind2, here = near

    def move(rows, step):
        return lax.ppermute(rows, "hd", [(i, (i + step) % NY) for i in range(NY)])

    def wide(rows):
        return rows.astype(jnp.float32)

    half = ahead4.shape[1]
    from3, from_far3 = move(ahead3, 1), move(behind3, -1)
    from4, from_far4 = move(ahead4, 2), move(behind4, -2)
    onward = wide(ahead2) + wide(from3) + jnp.pad(wide(from4), ((0, 0), (0, half)))
    backward = wide(behind2) + wide(from_far3) + jnp.pad(wide(from_far4), ((0, 0), (half, 0)))
    from2 = move(onward.astype(jnp.bfloat16), 2)
    from_far2 = move(backward.astype(jnp.bfloat16), -2)
    from1, from_far1 = move(ahead1, 1), move(behind1, -1)
    total = wide(here) + wide(from1) + wide(from_far1) + wide(from2) + wide(from_far2)
    return total.astype(jnp.bfloat16)


def per_device(query_rows, key_rows, value_rows, doc_ids, out_weight):
    place = lax.axis_index("ctx").reshape(1)
    ids = doc_ids.astype(jnp.bfloat16)[None, :]

    q_packed = jnp.concatenate(
        [query_rows, jnp.pad(ids, ((0, PAD - 1), (0, query_rows.shape[1] - 4)))], axis=0
    )
    q_blocks = [q_packed] + [
        lax.ppermute(q_packed, "ctx", ctx_perm(lambda z, x, c, r=r: (z, x + r, c)))
        for r in range(1, NX)
    ]
    kv_packed = jnp.concatenate(
        [key_rows, value_rows, jnp.pad(ids, ((0, PAD - 1), (0, HDIM - 4)))], axis=0
    )
    kv_own = lax.all_to_all(
        jnp.broadcast_to(kv_packed[None], (NZ,) + kv_packed.shape),
        "ctx",
        0,
        0,
        axis_index_groups=Z_GROUPS,
    )
    *q_blocks, kv_own = lax.optimization_barrier((*q_blocks, kv_own))
    kv_other = lax.ppermute(kv_own, "ctx", ctx_perm(lambda z, x, c: (z, x, 1 - c)))

    q_ids = jnp.stack([block[ROWS, 0:4] for block in q_blocks]).astype(jnp.int32)
    own_ids = kv_own[:, 2 * ROWS, 0:4].astype(jnp.int32)
    other_ids = kv_other[:, 2 * ROWS, 0:4].astype(jnp.int32)
    k_held, v_turned = hold(place, kv_own, kv_other)
    made = attend((0, 1, 2, 3), place, q_ids, own_ids, other_ids, q_blocks, k_held, v_turned)
    parts = lax.all_to_all(made, "ctx", 0, 0, axis_index_groups=X_GROUPS)
    y = lax.axis_index("hd").reshape(1)
    attended, *far = project_far(y, parts, out_weight)
    near = project_near(y, attended, out_weight)
    return attended, sum_over_hd(far, near)


def solution(mesh):
    in_specs = (P("ctx", "hd"), P("ctx", "hd"), P("ctx", "hd"), P("ctx"), P("hd", None))
    out_specs = (P("ctx", "hd"), P("ctx", "hd"))
    return jax.shard_map(
        per_device, mesh=mesh, in_specs=in_specs, out_specs=out_specs, check_vma=False
    )
```

time: 142 us -> 131 us (0.923)
  the two profiles are of different devices: /device:TPU:6 before, /device:TPU:449 now
where the time goes in v3:
time: 131 us; the launch traced here: 130 us
  starting transfers between devices  52.7 us (40%)
  waiting for transfers between devices  44.1 us (34%)
  Pallas kernels  25.8 us (20%)
  local copies, waits for them, and re-layouts  4.29 us (3%)
  other arithmetic  2.63 us (2%)
    ppermute x8, starting transfers between devices, move(): return lax.ppermute(rows, 'hd', [(i, (i + step) % NY) for i in range(NY)])  26.3 us
    pallas_call x1, Pallas kernels, attend(): pl.pallas_call(functools.partial(attend_kernel, shifts), out_shape=jax.Sh...  22.7 us
    all_to_all x1, waiting for transfers between devices, per_device(): parts = lax.all_to_all(made, 'ctx', 0, 0, axis_index_groups=X_GROUPS)  15.7 us
    ppermute x8, waiting for transfers between devices, move(): return lax.ppermute(rows, 'hd', [(i, (i + step) % NY) for i in range(NY)])  14.5 us
    ppermute x3, starting transfers between devices, per_device(): lax.ppermute(q_packed, 'ctx', ctx_perm(lambda z, x, c, r=r: (z, x + r, c)))  10.5 us
    ppermute x3, waiting for transfers between devices, per_device(): lax.ppermute(q_packed, 'ctx', ctx_perm(lambda z, x, c, r=r: (z, x + r, c)))  7.63 us
    all_to_all x1, starting transfers between devices, per_device(): parts = lax.all_to_all(made, 'ctx', 0, 0, axis_index_groups=X_GROUPS)  6.25 us
    ppermute x1, starting transfers between devices, per_device(): lax.ppermute(kv_own, 'ctx', ctx_perm(lambda z, x, c: (z, x, 1 - c)))  5.46 us
  transfers between devices with their start and end apart: 14, of which 9 were waited for; matrix products, arithmetic and copies ran while one was open for 0% of the time, Pallas kernels for 1%

profile of v3, /device:TPU:449, one launch (start us, length us, event | category | flops | bytes accessed | tf_op | source)
XLA Modules:
  0.0 130.3 jit_solution(3613157078592186420)
XLA Ops:
  0.6 0.7 convert_bitcast_fusion
  1.3 0.9 fusion.3
  2.2 1.1 broadcast_in_dim.10
  3.3 4.1 %all-to-all-start = ((bf16[8,528,128]{2,1,0:T(8,128)(2,1)}), bf16[8,528,128]{2,1,0:T(8,128)(2,1)S(1)}, u32[]{:S(2)}, u32[]{:S(2)}) async-start(bf16[8,528,128]{2,1,0:T(8,128)(2,1)} %broadcast_in_dim.10), calls=%async_computation | async-start | bytes 2162688 | tf_op jit(solution)/shard_map/all_to_all | solution.py:306
  7.4 3.1 %collective-permute-start = (bf16[272,512]{1,0:T(8,128)(2,1)S(1)}, bf16[272,512]{1,0:T(8,128)(2,1)S(1)}, u32[]{:S(2)}, u32[]{:S(2)}) collective-permute-start(bf16[272,512]{1,0:T(8,128)(2,1)S(1)} %fusion.1.refs_0_), channel_id=1, source_target_pairs={{0,16},{8,24},{16,32},{24,40},{32,48},{40,56},{48,0},{56,8},{64,80... | collective-permute-start | bytes 835592 | tf_op jit(solution)/shard_map/ppermute | solution.py:300
  10.6 4.4 %collective-permute-start.1 = (bf16[272,512]{1,0:T(8,128)(2,1)S(1)}, bf16[272,512]{1,0:T(8,128)(2,1)S(1)}, u32[]{:S(2)}, u32[]{:S(2)}) collective-permute-start(bf16[272,512]{1,0:T(8,128)(2,1)S(1)} %fusion.1.refs_0_), channel_id=1, source_target_pairs={{0,32},{8,40},{16,48},{24,56},{32,0},{40,8},{48,16},{56,24},{64,96... | collective-permute-start | bytes 835592 | tf_op jit(solution)/shard_map/ppermute | solution.py:300
  14.9 3.1 %collective-permute-start.2 = (bf16[272,512]{1,0:T(8,128)(2,1)S(1)}, bf16[272,512]{1,0:T(8,128)(2,1)S(1)}, u32[]{:S(2)}, u32[]{:S(2)}) collective-permute-start(bf16[272,512]{1,0:T(8,128)(2,1)S(1)} %fusion.1.refs_0_), channel_id=1, source_target_pairs={{0,48},{8,56},{16,0},{24,8},{32,16},{40,24},{48,32},{56,40},{64,11... | collective-permute-start | bytes 835592 | tf_op jit(solution)/shard_map/ppermute | solution.py:300
  18.0 6.4 %collective-permute-done.1.refs_2_ = bf16[272,512]{1,0:T(8,128)(2,1)S(1)} collective-permute-done((bf16[272,512]{1,0:T(8,128)(2,1)S(1)}, bf16[272,512]{1,0:T(8,128)(2,1)S(1)}, u32[]{:S(2)}, u32[]{:S(2)}) %collective-permute-start.1) | collective-permute-done | bytes 278560 | tf_op jit(solution)/shard_map/ppermute | solution.py:300
  24.4 1.2 collective-permute-done.2.refs_3_
  25.6 4.0 %all-to-all-done.kv_own = bf16[8,528,128]{2,1,0:T(8,128)(2,1)S(1)} async-done(((bf16[8,528,128]{2,1,0:T(8,128)(2,1)}), bf16[8,528,128]{2,1,0:T(8,128)(2,1)S(1)}, u32[]{:S(2)}, u32[]{:S(2)}) %all-to-all-start) | async-done | bytes 1081376 | tf_op jit(solution)/shard_map/all_to_all | solution.py:306
  29.7 5.5 %collective-permute-start.3 = (bf16[8,528,128]{2,1,0:T(8,128)(2,1)S(1)}, bf16[8,528,128]{2,1,0:T(8,128)(2,1)S(1)}, u32[]{:S(2)}, u32[]{:S(2)}) collective-permute-start(bf16[8,528,128]{2,1,0:T(8,128)(2,1)S(1)} %all-to-all-done.kv_own), channel_id=1, source_target_pairs={{0,8},{8,0},{16,24},{24,16},{32,40},{40,32},{48,56},{56,48},{64,72... | collective-permute-start | bytes 3244040 | tf_op jit(solution)/shard_map/ppermute | solution.py:314
  35.2 2.2 %collective-permute-done.3.kv_other = bf16[8,528,128]{2,1,0:T(8,128)(2,1)S(1)} collective-permute-done((bf16[8,528,128]{2,1,0:T(8,128)(2,1)S(1)}, bf16[8,528,128]{2,1,0:T(8,128)(2,1)S(1)}, u32[]{:S(2)}, u32[]{:S(2)}) %collective-permute-start.3) | collective-permute-done | bytes 1081376 | tf_op jit(solution)/shard_map/ppermute | solution.py:314
  37.4 0.7 shard_map.68
  38.1 22.7 %shard_map.69 = bf16[4,144,1024]{2,1,0:T(8,128)(2,1)} custom-call(s32[1]{0:T(128)} %bitcast.1.place, s32[4,4]{1,0:T(4,128)S(1)} %maximum_convert_fusion.q_ids, s32[8,4]{1,0:T(8,128)S(1)} %bitcast.6, s32[8,4]{1,0:T(8,128)S(1)} %bitcast.7, bf16[272,512]{1,0:T(8,128)(2,1)S(1)} %fusion.1.refs_0_, bf16[272,512]{1,0:T(8,128)(2,1)S(1)} %collective-permute-done.refs_1_, ...), custom_call_target="tpu_custom_call" | custom-call | flops 4294967296 | bytes 2097152 | tf_op jit(solution)/shard_map/pallas_call | solution.py:183
  60.9 6.3 %all-to-all-start.1 = ((bf16[4,144,1024]{2,1,0:T(8,128)(2,1)}), bf16[4,144,1024]{2,1,0:T(8,128)(2,1)S(1)}, u32[]{:S(2)}, u32[]{:S(2)}) async-start(bf16[4,144,1024]{2,1,0:T(8,128)(2,1)} %shard_map.69), calls=%async_computation.1 | async-start | bytes 2359296 | tf_op jit(solution)/shard_map/all_to_all | solution.py:321
  67.1 15.7 %all-to-all-done.1.parts = bf16[4,144,1024]{2,1,0:T(8,128)(2,1)S(1)} async-done(((bf16[4,144,1024]{2,1,0:T(8,128)(2,1)}), bf16[4,144,1024]{2,1,0:T(8,128)(2,1)S(1)}, u32[]{:S(2)}, u32[]{:S(2)}) %all-to-all-start.1) | async-done | bytes 1179680 | tf_op jit(solution)/shard_map/all_to_all | solution.py:321
  82.9 2.2 %copy-done = bf16[512,4096]{1,0:T(8,128)(2,1)S(1)} copy-done((bf16[512,4096]{1,0:T(8,128)(2,1)S(1)}, bf16[512,4096]{1,0:T(8,128)(2,1)}, u32[]{:S(2)}) %copy-start) | copy-done | bytes 4194328
  85.1 1.5 %shard_map.70 = (bf16[256,512]{1,0:T(8,128)(2,1)}, bf16[256,512]{1,0:T(8,128)(2,1)S(1)}, bf16[256,512]{1,0:T(8,128)(2,1)S(1)}, bf16[256,256]{1,0:T(8,128)(2,1)S(1)}, bf16[256,256]{1,0:T(8,128)(2,1)S(1)}) custom-call(s32[1]{0:T(128)} %bitcast.y, bf16[4,144,1024]{2,1,0:T(8,128)(2,1)S(1)} %all-to-all-done.1.parts, bf16[512,4096]{1,0:T(8,128)(2,1)S(1)} %copy-done), custom_call_target="tpu_custom_call" | custom-call | flops 536870912 | bytes 2097152 | tf_op jit(solution)/shard_map/pallas_call | solution.py:242
  86.5 3.2 %collective-permute-start.6 = (bf16[256,512]{1,0:T(8,128)(2,1)S(1)}, bf16[256,512]{1,0:T(8,128)(2,1)S(1)}, u32[]{:S(2)}, u32[]{:S(2)}) collective-permute-start(bf16[256,512]{1,0:T(8,128)(2,1)S(1)} %get-tuple-element.31), channel_id=1, source_target_pairs={{0,1},{1,2},{2,3},{3,4},{4,5},{5,6},{6,7},{7,0},{8,9},{9,10},{10,1... | collective-permute-start | bytes 786440 | tf_op jit(solution)/shard_map/ppermute | solution.py:275
  89.7 4.2 %collective-permute-start.7 = (bf16[256,256]{1,0:T(8,128)(2,1)S(1)}, bf16[256,256]{1,0:T(8,128)(2,1)S(1)}, u32[]{:S(2)}, u32[]{:S(2)}) collective-permute-start(bf16[256,256]{1,0:T(8,128)(2,1)S(1)} %get-tuple-element.32), channel_id=1, source_target_pairs={{0,2},{1,3},{2,4},{3,5},{4,6},{5,7},{6,0},{7,1},{8,10},{9,11},{10,... | collective-permute-start | bytes 393224 | tf_op jit(solution)/shard_map/ppermute | solution.py:275
  93.9 3.3 %collective-permute-start.9 = (bf16[256,512]{1,0:T(8,128)(2,1)S(1)}, bf16[256,512]{1,0:T(8,128)(2,1)S(1)}, u32[]{:S(2)}, u32[]{:S(2)}) collective-permute-start(bf16[256,512]{1,0:T(8,128)(2,1)S(1)} %get-tuple-element.34), channel_id=1, source_target_pairs={{0,7},{1,0},{2,1},{3,2},{4,3},{5,4},{6,5},{7,6},{8,15},{9,8},{10,9... | collective-permute-start | bytes 786440 | tf_op jit(solution)/shard_map/ppermute | solution.py:275
  97.3 0.9 copy-done.2
  98.2 0.8 shard_map.71
  99.0 2.5 %collective-permute-start.10 = (bf16[256,256]{1,0:T(8,128)(2,1)S(1)}, bf16[256,256]{1,0:T(8,128)(2,1)S(1)}, u32[]{:S(2)}, u32[]{:S(2)}) collective-permute-start(bf16[256,256]{1,0:T(8,128)(2,1)S(1)} %get-tuple-element.35), channel_id=1, source_target_pairs={{0,6},{1,7},{2,0},{3,1},{4,2},{5,3},{6,4},{7,5},{8,14},{9,15},{10,... | collective-permute-start | bytes 393224 | tf_op jit(solution)/shard_map/ppermute | solution.py:275
  101.5 2.7 %collective-permute-start.4 = (bf16[256,512]{1,0:T(8,128)(2,1)S(1)}, bf16[256,512]{1,0:T(8,128)(2,1)S(1)}, u32[]{:S(2)}, u32[]{:S(2)}) collective-permute-start(bf16[256,512]{1,0:T(8,128)(2,1)S(1)} %get-tuple-element.28), channel_id=1, source_target_pairs={{0,1},{1,2},{2,3},{3,4},{4,5},{5,6},{6,7},{7,0},{8,9},{9,10},{10,1... | collective-permute-start | bytes 786440 | tf_op jit(solution)/shard_map/ppermute | solution.py:275
  104.2 3.9 %collective-permute-start.5 = (bf16[256,512]{1,0:T(8,128)(2,1)S(1)}, bf16[256,512]{1,0:T(8,128)(2,1)S(1)}, u32[]{:S(2)}, u32[]{:S(2)}) collective-permute-start(bf16[256,512]{1,0:T(8,128)(2,1)S(1)} %get-tuple-element.29), channel_id=1, source_target_pairs={{0,7},{1,0},{2,1},{3,2},{4,3},{5,4},{6,5},{7,6},{8,15},{9,8},{10,9... | collective-permute-start | bytes 786440 | tf_op jit(solution)/shard_map/ppermute | solution.py:275
  108.2 2.4 %collective-permute-start.8 = (bf16[256,512]{1,0:T(8,128)(2,1)S(1)}, bf16[256,512]{1,0:T(8,128)(2,1)S(1)}, u32[]{:S(2)}, u32[]{:S(2)}) collective-permute-start(bf16[256,512]{1,0:T(8,128)(2,1)S(1)} %add_convert_fusion.2), channel_id=1, source_target_pairs={{0,2},{1,3},{2,4},{3,5},{4,6},{5,7},{6,0},{7,1},{8,10},{9,11},{10,... | collective-permute-start | bytes 786440 | tf_op jit(solution)/shard_map/ppermute | solution.py:275
  110.7 0.8 collective-permute-done.10
  111.6 4.2 %collective-permute-start.11 = (bf16[256,512]{1,0:T(8,128)(2,1)S(1)}, bf16[256,512]{1,0:T(8,128)(2,1)S(1)}, u32[]{:S(2)}, u32[]{:S(2)}) collective-permute-start(bf16[256,512]{1,0:T(8,128)(2,1)S(1)} %add_convert_fusion.1), channel_id=1, source_target_pairs={{0,6},{1,7},{2,0},{3,1},{4,2},{5,3},{6,4},{7,5},{8,14},{9,15},{10,... | collective-permute-start | bytes 786440 | tf_op jit(solution)/shard_map/ppermute | solution.py:275
  115.8 9.9 %collective-permute-done.8 = bf16[256,512]{1,0:T(8,128)(2,1)S(1)} collective-permute-done((bf16[256,512]{1,0:T(8,128)(2,1)S(1)}, bf16[256,512]{1,0:T(8,128)(2,1)S(1)}, u32[]{:S(2)}, u32[]{:S(2)}) %collective-permute-start.8) | collective-permute-done | bytes 262176 | tf_op jit(solution)/shard_map/ppermute | solution.py:275
  125.7 3.8 %collective-permute-done.11 = bf16[256,512]{1,0:T(8,128)(2,1)S(1)} collective-permute-done((bf16[256,512]{1,0:T(8,128)(2,1)S(1)}, bf16[256,512]{1,0:T(8,128)(2,1)S(1)}, u32[]{:S(2)}, u32[]{:S(2)}) %collective-permute-start.11) | collective-permute-done | bytes 262176 | tf_op jit(solution)/shard_map/ppermute | solution.py:275
  129.5 0.9 add_convert_fusion
  (22 shorter events, 0.3 us)
Async XLA Ops:
  3.3 4.1 %copy-start.3 = (bf16[256,512]{1,0:T(8,128)(2,1)S(1)}, bf16[256,512]{1,0:T(8,128)(2,1)}, u32[]{:S(2)}) copy-start(bf16[256,512]{1,0:T(8,128)(2,1)} %param.5) | copy-start | bytes 786436
  3.3 26.3 %all-to-all-start = ((bf16[8,528,128]{2,1,0:T(8,128)(2,1)}), bf16[8,528,128]{2,1,0:T(8,128)(2,1)S(1)}, u32[]{:S(2)}, u32[]{:S(2)}) async-start(bf16[8,528,128]{2,1,0:T(8,128)(2,1)} %broadcast_in_dim.10), calls=%async_computation | async-start | bytes 2162688 | tf_op jit(solution)/shard_map/all_to_all | solution.py:306
  7.4 10.6 %collective-permute-start = (bf16[272,512]{1,0:T(8,128)(2,1)S(1)}, bf16[272,512]{1,0:T(8,128)(2,1)S(1)}, u32[]{:S(2)}, u32[]{:S(2)}) collective-permute-start(bf16[272,512]{1,0:T(8,128)(2,1)S(1)} %fusion.1.refs_0_), channel_id=1, source_target_pairs={{0,16},{8,24},{16,32},{24,40},{32,48},{40,56},{48,0},{56,8},{64,80... | collective-permute-start | bytes 835592 | tf_op jit(solution)/shard_map/ppermute | solution.py:300
  10.6 13.8 %collective-permute-start.1 = (bf16[272,512]{1,0:T(8,128)(2,1)S(1)}, bf16[272,512]{1,0:T(8,128)(2,1)S(1)}, u32[]{:S(2)}, u32[]{:S(2)}) collective-permute-start(bf16[272,512]{1,0:T(8,128)(2,1)S(1)} %fusion.1.refs_0_), channel_id=1, source_target_pairs={{0,32},{8,40},{16,48},{24,56},{32,0},{40,8},{48,16},{56,24},{64,96... | collective-permute-start | bytes 835592 | tf_op jit(solution)/shard_map/ppermute | solution.py:300
  14.9 10.7 %collective-permute-start.2 = (bf16[272,512]{1,0:T(8,128)(2,1)S(1)}, bf16[272,512]{1,0:T(8,128)(2,1)S(1)}, u32[]{:S(2)}, u32[]{:S(2)}) collective-permute-start(bf16[272,512]{1,0:T(8,128)(2,1)S(1)} %fusion.1.refs_0_), channel_id=1, source_target_pairs={{0,48},{8,56},{16,0},{24,8},{32,16},{40,24},{48,32},{56,40},{64,11... | collective-permute-start | bytes 835592 | tf_op jit(solution)/shard_map/ppermute | solution.py:300
  29.7 7.8 %collective-permute-start.3 = (bf16[8,528,128]{2,1,0:T(8,128)(2,1)S(1)}, bf16[8,528,128]{2,1,0:T(8,128)(2,1)S(1)}, u32[]{:S(2)}, u32[]{:S(2)}) collective-permute-start(bf16[8,528,128]{2,1,0:T(8,128)(2,1)S(1)} %all-to-all-done.kv_own), channel_id=1, source_target_pairs={{0,8},{8,0},{16,24},{24,16},{32,40},{40,32},{48,56},{56,48},{64,72... | collective-permute-start | bytes 3244040 | tf_op jit(solution)/shard_map/ppermute | solution.py:314
  60.9 22.0 %all-to-all-start.1 = ((bf16[4,144,1024]{2,1,0:T(8,128)(2,1)}), bf16[4,144,1024]{2,1,0:T(8,128)(2,1)S(1)}, u32[]{:S(2)}, u32[]{:S(2)}) async-start(bf16[4,144,1024]{2,1,0:T(8,128)(2,1)} %shard_map.69), calls=%async_computation.1 | async-start | bytes 2359296 | tf_op jit(solution)/shard_map/all_to_all | solution.py:321
  82.9 2.2 %copy-start = (bf16[512,4096]{1,0:T(8,128)(2,1)S(1)}, bf16[512,4096]{1,0:T(8,128)(2,1)}, u32[]{:S(2)}) copy-start(bf16[512,4096]{1,0:T(8,128)(2,1)} %weight.3) | copy-start | bytes 12582916
  85.1 12.2 %copy-start.1 = (bf16[512,4096]{1,0:T(8,128)(2,1)S(1)}, bf16[512,4096]{1,0:T(8,128)(2,1)}, u32[]{:S(2)}) copy-start(bf16[512,4096]{1,0:T(8,128)(2,1)} %weight.3) | copy-start | bytes 12582916
  86.5 21.6 %collective-permute-start.6 = (bf16[256,512]{1,0:T(8,128)(2,1)S(1)}, bf16[256,512]{1,0:T(8,128)(2,1)S(1)}, u32[]{:S(2)}, u32[]{:S(2)}) collective-permute-start(bf16[256,512]{1,0:T(8,128)(2,1)S(1)} %get-tuple-element.31), channel_id=1, source_target_pairs={{0,1},{1,2},{2,3},{3,4},{4,5},{5,6},{6,7},{7,0},{8,9},{9,10},{10,1... | collective-permute-start | bytes 786440 | tf_op jit(solution)/shard_map/ppermute | solution.py:275
  89.7 14.5 %collective-permute-start.7 = (bf16[256,256]{1,0:T(8,128)(2,1)S(1)}, bf16[256,256]{1,0:T(8,128)(2,1)S(1)}, u32[]{:S(2)}, u32[]{:S(2)}) collective-permute-start(bf16[256,256]{1,0:T(8,128)(2,1)S(1)} %get-tuple-element.32), channel_id=1, source_target_pairs={{0,2},{1,3},{2,4},{3,5},{4,6},{5,7},{6,0},{7,1},{8,10},{9,11},{10,... | collective-permute-start | bytes 393224 | tf_op jit(solution)/shard_map/ppermute | solution.py:275
  93.9 17.5 %collective-permute-start.9 = (bf16[256,512]{1,0:T(8,128)(2,1)S(1)}, bf16[256,512]{1,0:T(8,128)(2,1)S(1)}, u32[]{:S(2)}, u32[]{:S(2)}) collective-permute-start(bf16[256,512]{1,0:T(8,128)(2,1)S(1)} %get-tuple-element.34), channel_id=1, source_target_pairs={{0,7},{1,0},{2,1},{3,2},{4,3},{5,4},{6,5},{7,6},{8,15},{9,8},{10,9... | collective-permute-start | bytes 786440 | tf_op jit(solution)/shard_map/ppermute | solution.py:275
  97.2 1.0 copy-start.2
  99.0 12.4 %collective-permute-start.10 = (bf16[256,256]{1,0:T(8,128)(2,1)S(1)}, bf16[256,256]{1,0:T(8,128)(2,1)S(1)}, u32[]{:S(2)}, u32[]{:S(2)}) collective-permute-start(bf16[256,256]{1,0:T(8,128)(2,1)S(1)} %get-tuple-element.35), channel_id=1, source_target_pairs={{0,6},{1,7},{2,0},{3,1},{4,2},{5,3},{6,4},{7,5},{8,14},{9,15},{10,... | collective-permute-start | bytes 393224 | tf_op jit(solution)/shard_map/ppermute | solution.py:275
  101.5 14.2 %collective-permute-start.4 = (bf16[256,512]{1,0:T(8,128)(2,1)S(1)}, bf16[256,512]{1,0:T(8,128)(2,1)S(1)}, u32[]{:S(2)}, u32[]{:S(2)}) collective-permute-start(bf16[256,512]{1,0:T(8,128)(2,1)S(1)} %get-tuple-element.28), channel_id=1, source_target_pairs={{0,1},{1,2},{2,3},{3,4},{4,5},{5,6},{6,7},{7,0},{8,9},{9,10},{10,1... | collective-permute-start | bytes 786440 | tf_op jit(solution)/shard_map/ppermute | solution.py:275
  104.2 11.6 %collective-permute-start.5 = (bf16[256,512]{1,0:T(8,128)(2,1)S(1)}, bf16[256,512]{1,0:T(8,128)(2,1)S(1)}, u32[]{:S(2)}, u32[]{:S(2)}) collective-permute-start(bf16[256,512]{1,0:T(8,128)(2,1)S(1)} %get-tuple-element.29), channel_id=1, source_target_pairs={{0,7},{1,0},{2,1},{3,2},{4,3},{5,4},{6,5},{7,6},{8,15},{9,8},{10,9... | collective-permute-start | bytes 786440 | tf_op jit(solution)/shard_map/ppermute | solution.py:275
  108.2 17.5 %collective-permute-start.8 = (bf16[256,512]{1,0:T(8,128)(2,1)S(1)}, bf16[256,512]{1,0:T(8,128)(2,1)S(1)}, u32[]{:S(2)}, u32[]{:S(2)}) collective-permute-start(bf16[256,512]{1,0:T(8,128)(2,1)S(1)} %add_convert_fusion.2), channel_id=1, source_target_pairs={{0,2},{1,3},{2,4},{3,5},{4,6},{5,7},{6,0},{7,1},{8,10},{9,11},{10,... | collective-permute-start | bytes 786440 | tf_op jit(solution)/shard_map/ppermute | solution.py:275
  111.6 17.9 %collective-permute-start.11 = (bf16[256,512]{1,0:T(8,128)(2,1)S(1)}, bf16[256,512]{1,0:T(8,128)(2,1)S(1)}, u32[]{:S(2)}, u32[]{:S(2)}) collective-permute-start(bf16[256,512]{1,0:T(8,128)(2,1)S(1)} %add_convert_fusion.1), channel_id=1, source_target_pairs={{0,6},{1,7},{2,0},{3,1},{4,2},{5,3},{6,4},{7,5},{8,14},{9,15},{10,... | collective-permute-start | bytes 786440 | tf_op jit(solution)/shard_map/ppermute | solution.py:275

commit v4 on v3

--- a/solution.py
+++ b/solution.py
@@ -15,11 +15,11 @@
 NZ, NX, NC = 8, 4, 2
 NY = 8
 QCOLS = GROUP * ROWS
+FOREIGN = (2, 1, 3)
 PAD = 16
 NEG_BIG = -1e30
 SCALE = math.log2(math.e) / math.sqrt(HDIM)
 
-X_GROUPS = [[(z * NX + x) * NC + c for x in range(NX)] for z in range(NZ) for c in range(NC)]
 Z_GROUPS = [[(z * NX + x) * NC + c for z in range(NZ)] for x in range(NX) for c in range(NC)]
 
 
@@ -51,7 +51,8 @@
     shifts, place, q_ids, own_ids, other_ids, *refs
 ):
     count = len(shifts)
-    q_refs, (k_held, v_turned, out, q_held, bounds, scores, total, high, norm) = refs[:count], refs[count:]
+    q_refs, (k_held, v_turned) = refs[:count], refs[count : count + 2]
+    outs, (q_held, bounds, scores, total, high, norm) = refs[count + 2 : 2 * count + 2], refs[2 * count + 2 :]
     index = place[0]
     z, x, c = lax.div(index, NX * NC), lax.rem(lax.div(index, NC), NX), lax.rem(index, NC)
 
@@ -120,9 +121,13 @@
         third = rest - second
         row = lax.broadcasted_iota(jnp.int32, (PAD, QCOLS), 0)
         stats = jnp.where(row == 0, first, jnp.where(row == 1, second, jnp.where(row == 2, third, 0.0)))
-        at = bounds[n, 2]
-        out[at, 0:HDIM, :] = (total[...] * share).astype(jnp.bfloat16)
-        out[at, HDIM : HDIM + PAD, :] = stats.astype(jnp.bfloat16)
+        done, stats = (total[...] * share).astype(jnp.bfloat16), stats.astype(jnp.bfloat16)
+        for k, out in enumerate(outs):
+
+            @pl.when(n == k)
+            def _():
+                out[0:HDIM, :] = done
+                out[HDIM : HDIM + PAD, :] = stats
 
     def turn(slot, n, zk):
         live = n < count
@@ -182,9 +187,9 @@
     pairs = count * NZ * NC * ROWS * QCOLS // 2
     return pl.pallas_call(
         functools.partial(attend_kernel, shifts),
-        out_shape=jax.ShapeDtypeStruct((NX, HDIM + PAD, QCOLS), jnp.bfloat16),
+        out_shape=(jax.ShapeDtypeStruct((HDIM + PAD, QCOLS), jnp.bfloat16),) * count,
         in_specs=[SMEM] * 4 + [VMEM] * (count + 2),
-        out_specs=VMEM,
+        out_specs=(VMEM,) * count,
         scratch_shapes=[
             pltpu.VMEM((count, QCOLS, HDIM), jnp.bfloat16),
             pltpu.SMEM((count + 1, 4), jnp.int32),
@@ -207,69 +212,86 @@
     return jnp.dot(attended[...], picked, preferred_element_type=jnp.float32).astype(jnp.bfloat16)
 
 
-def far_kernel(y, parts, weight, attended, ahead3, behind3, ahead4, behind4):
+def far_kernel(p0, p1, p2, p3, weight, attended, kept, ahead3, behind3, ahead4, behind4):
+    views = (p0, p1, p2, p3)
     levels = []
-    for s in range(NX):
-        stats = parts[s, HDIM : HDIM + PAD, :].astype(jnp.float32)
+    for view in views:
+        stats = view[HDIM : HDIM + PAD, :].astype(jnp.float32)
         levels.append(stats[0:1, :] + stats[1:2, :] + stats[2:3, :])
     top = functools.reduce(jnp.maximum, levels)
     shares = [jnp.exp2(level - top) for level in levels]
     inverse = 1.0 / sum(shares)
     mixed = sum(
-        parts[s, 0:HDIM, :].astype(jnp.float32) * (shares[s] * inverse) for s in range(NX)
+        views[s][0:HDIM, :].astype(jnp.float32) * (shares[s] * inverse) for s in range(NX)
     )
     for h in range(GROUP):
-        block = mixed[:, h * ROWS : (h + 1) * ROWS]
-        attended[:, h * HDIM : (h + 1) * HDIM] = block.T.astype(jnp.bfloat16)
-    half = ahead4.shape[1]
-    everything = slice(0, 2 * half)
-    ahead3[...] = column_share(attended, weight, y[0], 3, everything)
-    behind3[...] = column_share(attended, weight, y[0], -3, everything)
-    ahead4[...] = column_share(attended, weight, y[0], 4, slice(0, half))
-    behind4[...] = column_share(attended, weight, y[0], 4, slice(half, 2 * half))
-
-
-def near_kernel(y, attended, weight, ahead1, behind1, ahead2, behind2, here):
-    everything = slice(0, here.shape[1])
-    for out, step in ((ahead2, 2), (behind2, -2), (ahead1, 1), (behind1, -1), (here, 0)):
-        out[...] = column_share(attended, weight, y[0], step, everything)
-
-
-def project_far(y, parts, weight):
+        block = mixed[:, h * ROWS : (h + 1) * ROWS].T.astype(jnp.bfloat16)
+        attended[:, h * HDIM : (h + 1) * HDIM] = block
+        kept[:, h * HDIM : (h + 1) * HDIM] = block
+    rows = kept[...]
+    at = 0
+    for out in (ahead3, behind3, ahead4, behind4):
+        width = out.shape[1]
+        out[...] = jnp.dot(
+            rows, weight[:, at : at + width], preferred_element_type=jnp.float32
+        ).astype(jnp.bfloat16)
+        at += width
+
+
+def near_kernel(attended, weight, ahead2, behind2, ahead1, behind1, here):
+    width = here.shape[1]
+    for n, out in enumerate((ahead2, behind2, ahead1, behind1, here)):
+        out[...] = jnp.dot(
+            attended[...], weight[:, n * width : (n + 1) * width],
+            preferred_element_type=jnp.float32,
+        ).astype(jnp.bfloat16)
+
+
+def columns_of(y, weight, steps):
     width = weight.shape[1] // NY
+    return jnp.concatenate(
+        [
+            lax.dynamic_slice_in_dim(weight, lax.rem(y + step + NY, NY) * width, width, 1)
+            for step in steps
+        ],
+        axis=1,
+    )
+
+
+def project_far(parts, weight):
+    width = weight.shape[1] // 3
+    attended = jax.ShapeDtypeStruct((ROWS, GROUP * HDIM), jnp.bfloat16)
     whole = jax.ShapeDtypeStruct((ROWS, width), jnp.bfloat16)
     half = jax.ShapeDtypeStruct((ROWS, width // 2), jnp.bfloat16)
     return pl.pallas_call(
         far_kernel,
-        out_shape=(
-            jax.ShapeDtypeStruct((ROWS, GROUP * HDIM), jnp.bfloat16), whole, whole, half, half,
+        out_shape=(attended, attended, whole, whole, half, half),
+        in_specs=[VMEM] * 5,
+        out_specs=(VMEM,) * 6,
+        compiler_params=pltpu.CompilerParams(vmem_limit_bytes=24 * 1024 * 1024),
+        cost_estimate=pl.CostEstimate(
+            flops=2 * ROWS * weight.size, bytes_accessed=2 * weight.size, transcendentals=0
         ),
-        in_specs=[SMEM, VMEM, VMEM],
+    )(*parts, weight)
+
+
+def project_near(attended, weight):
+    whole = jax.ShapeDtypeStruct((ROWS, weight.shape[1] // 5), jnp.bfloat16)
+    return pl.pallas_call(
+        near_kernel,
+        out_shape=(whole,) * 5,
+        in_specs=[VMEM] * 2,
         out_specs=(VMEM,) * 5,
         compiler_params=pltpu.CompilerParams(vmem_limit_bytes=24 * 1024 * 1024),
         cost_estimate=pl.CostEstimate(
-            flops=ROWS * weight.size, bytes_accessed=weight.size, transcendentals=0
+            flops=2 * ROWS * weight.size, bytes_accessed=2 * weight.size, transcendentals=0
         ),
-    )(y, parts, weight)
-
-
-def project_near(y, attended, weight):
-    whole = jax.ShapeDtypeStruct((ROWS, weight.shape[1] // NY), jnp.bfloat16)
-    return pl.pallas_call(
-        near_kernel,
-        out_shape=(whole,) * 5,
-        in_specs=[SMEM, VMEM, VMEM],
-        out_specs=(VMEM,) * 5,
-        compiler_params=pltpu.CompilerParams(vmem_limit_bytes=24 * 1024 * 1024),
-        cost_estimate=pl.CostEstimate(
-            flops=ROWS * weight.size, bytes_accessed=weight.size, transcendentals=0
-        ),
-    )(y, attended, weight)
+    )(attended, weight)
 
 
 def sum_over_hd(far, near):
     ahead3, behind3, ahead4, behind4 = far
-    ahead1, behind1, ahead2, behind2, here = near
+    ahead2, behind2, ahead1, behind1, here = near
 
     def move(rows, step):
         return lax.ppermute(rows, "hd", [(i, (i + step) % NY) for i in range(NY)])
@@ -310,6 +332,7 @@
         0,
         axis_index_groups=Z_GROUPS,
     )
+    y = lax.axis_index("hd")
     *q_blocks, kv_own = lax.optimization_barrier((*q_blocks, kv_own))
     kv_other = lax.ppermute(kv_own, "ctx", ctx_perm(lambda z, x, c: (z, x, 1 - c)))
 
@@ -317,11 +340,18 @@
     own_ids = kv_own[:, 2 * ROWS, 0:4].astype(jnp.int32)
     other_ids = kv_other[:, 2 * ROWS, 0:4].astype(jnp.int32)
     k_held, v_turned = hold(place, kv_own, kv_other)
-    made = attend((0, 1, 2, 3), place, q_ids, own_ids, other_ids, q_blocks, k_held, v_turned)
-    parts = lax.all_to_all(made, "ctx", 0, 0, axis_index_groups=X_GROUPS)
-    y = lax.axis_index("hd").reshape(1)
-    attended, *far = project_far(y, parts, out_weight)
-    near = project_near(y, attended, out_weight)
+    arrays = (place, q_ids, own_ids, other_ids, q_blocks, k_held, v_turned)
+    made = dict(zip(FOREIGN, attend(FOREIGN, *arrays)))
+    made[1], weight = lax.optimization_barrier((made[1], out_weight))
+    parts = {
+        r: lax.ppermute(made[r], "ctx", ctx_perm(lambda z, x, c, r=r: (z, x - r, c)))
+        for r in FOREIGN
+    }
+    (parts[0],) = attend((0,), *arrays)
+    far_weight = columns_of(y, weight, (3, -3, 4))
+    near_weight = columns_of(y, weight, (2, -2, 1, -1, 0))
+    attended, kept, *far = project_far([parts[r] for r in range(NX)], far_weight)
+    near = project_near(kept, near_weight)
     return attended, sum_over_hd(far, near)
 
 

time: 131 us -> 122 us (0.931)
  the two profiles are of different devices: /device:TPU:449 before, /device:TPU:24 now
where the time goes in v4:
time: 122 us; the launch traced here: 121 us
  starting transfers between devices  59.2 us (49%)
  waiting for transfers between devices  45.9 us (38%)
  Pallas kernels  10.9 us (9%)
  other arithmetic  2.77 us (2%)
  local copies, waits for them, and re-layouts  1.6 us (1%)
    ppermute x8, starting transfers between devices, move(): return lax.ppermute(rows, 'hd', [(i, (i + step) % NY) for i in range(NY)])  27.1 us
    ppermute x8, waiting for transfers between devices, move(): return lax.ppermute(rows, 'hd', [(i, (i + step) % NY) for i in range(NY)])  14 us
    ppermute x3, waiting for transfers between devices, per_device(): lax.ppermute(q_packed, 'ctx', ctx_perm(lambda z, x, c, r=r: (z, x + r, c)))  11.7 us
    all_to_all x1, starting transfers between devices, per_device(): lax.all_to_all(jnp.broadcast_to(kv_packed[None], (NZ,) + kv_packed.shape)...  10.3 us
    ppermute x3, waiting for transfers between devices, per_device(): lax.ppermute(made[r], 'ctx', ctx_perm(lambda z, x, c, r=r: (z, x - r, c)))  10.2 us
    ppermute x3, starting transfers between devices, per_device(): lax.ppermute(q_packed, 'ctx', ctx_perm(lambda z, x, c, r=r: (z, x + r, c)))  10.2 us
    ppermute x3, starting transfers between devices, per_device(): lax.ppermute(made[r], 'ctx', ctx_perm(lambda z, x, c, r=r: (z, x - r, c)))  9.63 us
    pallas_call x2, Pallas kernels, attend(): pl.pallas_call(functools.partial(attend_kernel, shifts), out_shape=(jax.S...  8.52 us
  transfers between devices with their start and end apart: 16, of which 11 were waited for; matrix products, arithmetic and copies ran while one was open for 1% of the time, Pallas kernels for 3%

profile of v4, /device:TPU:24, one launch (start us, length us, event | category | flops | bytes accessed | tf_op | source)
XLA Modules:
  0.0 121.4 jit_solution(18018165157822205018)
XLA Ops:
  1.3 0.9 fusion.3
  2.2 1.2 broadcast_in_dim.10
  3.4 10.3 %all-to-all-start = ((bf16[8,528,128]{2,1,0:T(8,128)(2,1)}), bf16[8,528,128]{2,1,0:T(8,128)(2,1)S(1)}, u32[]{:S(2)}, u32[]{:S(2)}) async-start(bf16[8,528,128]{2,1,0:T(8,128)(2,1)} %broadcast_in_dim.10), calls=%async_computation | async-start | bytes 2162688 | tf_op jit(solution)/shard_map/all_to_all | solution.py:328
  13.7 4.7 %collective-permute-start.2 = (bf16[272,512]{1,0:T(8,128)(2,1)S(1)}, bf16[272,512]{1,0:T(8,128)(2,1)S(1)}, u32[]{:S(2)}, u32[]{:S(2)}) collective-permute-start(bf16[272,512]{1,0:T(8,128)(2,1)S(1)} %fusion.1.refs_0_), channel_id=1, source_target_pairs={{0,48},{8,56},{16,0},{24,8},{32,16},{40,24},{48,32},{56,40},{64,11... | collective-permute-start | bytes 835592 | tf_op jit(solution)/shard_map/ppermute | solution.py:322
  18.4 2.7 %collective-permute-start.1 = (bf16[272,512]{1,0:T(8,128)(2,1)S(1)}, bf16[272,512]{1,0:T(8,128)(2,1)S(1)}, u32[]{:S(2)}, u32[]{:S(2)}) collective-permute-start(bf16[272,512]{1,0:T(8,128)(2,1)S(1)} %fusion.1.refs_0_), channel_id=1, source_target_pairs={{0,32},{8,40},{16,48},{24,56},{32,0},{40,8},{48,16},{56,24},{64,96... | collective-permute-start | bytes 835592 | tf_op jit(solution)/shard_map/ppermute | solution.py:322
  21.1 2.8 %collective-permute-start = (bf16[272,512]{1,0:T(8,128)(2,1)S(1)}, bf16[272,512]{1,0:T(8,128)(2,1)S(1)}, u32[]{:S(2)}, u32[]{:S(2)}) collective-permute-start(bf16[272,512]{1,0:T(8,128)(2,1)S(1)} %fusion.1.refs_0_), channel_id=1, source_target_pairs={{0,16},{8,24},{16,32},{24,40},{32,48},{40,56},{48,0},{56,8},{64,80... | collective-permute-start | bytes 835592 | tf_op jit(solution)/shard_map/ppermute | solution.py:322
  23.9 6.1 %collective-permute-done.2.refs_2_ = bf16[272,512]{1,0:T(8,128)(2,1)S(1)} collective-permute-done((bf16[272,512]{1,0:T(8,128)(2,1)S(1)}, bf16[272,512]{1,0:T(8,128)(2,1)S(1)}, u32[]{:S(2)}, u32[]{:S(2)}) %collective-permute-start.2) | collective-permute-done | bytes 278560 | tf_op jit(solution)/shard_map/ppermute | solution.py:322
  30.0 1.4 %collective-permute-done.1.refs_0_ = bf16[272,512]{1,0:T(8,128)(2,1)S(1)} collective-permute-done((bf16[272,512]{1,0:T(8,128)(2,1)S(1)}, bf16[272,512]{1,0:T(8,128)(2,1)S(1)}, u32[]{:S(2)}, u32[]{:S(2)}) %collective-permute-start.1) | collective-permute-done | bytes 278560 | tf_op jit(solution)/shard_map/ppermute | solution.py:322
  31.4 4.2 %collective-permute-done.refs_1_ = bf16[272,512]{1,0:T(8,128)(2,1)S(1)} collective-permute-done((bf16[272,512]{1,0:T(8,128)(2,1)S(1)}, bf16[272,512]{1,0:T(8,128)(2,1)S(1)}, u32[]{:S(2)}, u32[]{:S(2)}) %collective-permute-start) | collective-permute-done | bytes 278560 | tf_op jit(solution)/shard_map/ppermute | solution.py:322
  35.6 7.5 %all-to-all-done.kv_own = bf16[8,528,128]{2,1,0:T(8,128)(2,1)S(1)} async-done(((bf16[8,528,128]{2,1,0:T(8,128)(2,1)}), bf16[8,528,128]{2,1,0:T(8,128)(2,1)S(1)}, u32[]{:S(2)}, u32[]{:S(2)}) %all-to-all-start) | async-done | bytes 1081376 | tf_op jit(solution)/shard_map/all_to_all | solution.py:328
  43.1 1.9 %collective-permute-start.3 = (bf16[8,528,128]{2,1,0:T(8,128)(2,1)S(1)}, bf16[8,528,128]{2,1,0:T(8,128)(2,1)S(1)}, u32[]{:S(2)}, u32[]{:S(2)}) collective-permute-start(bf16[8,528,128]{2,1,0:T(8,128)(2,1)S(1)} %all-to-all-done.kv_own), channel_id=1, source_target_pairs={{0,8},{8,0},{16,24},{24,16},{32,40},{40,32},{48,56},{56,48},{64,72... | collective-permute-start | bytes 3244040 | tf_op jit(solution)/shard_map/ppermute | solution.py:337
  45.2 2.5 %collective-permute-done.3.kv_other = bf16[8,528,128]{2,1,0:T(8,128)(2,1)S(1)} collective-permute-done((bf16[8,528,128]{2,1,0:T(8,128)(2,1)S(1)}, bf16[8,528,128]{2,1,0:T(8,128)(2,1)S(1)}, u32[]{:S(2)}, u32[]{:S(2)}) %collective-permute-start.3) | collective-permute-done | bytes 1081376 | tf_op jit(solution)/shard_map/ppermute | solution.py:337
  47.8 5.8 %shard_map.70 = (bf16[144,1024]{1,0:T(8,128)(2,1)S(1)}, bf16[144,1024]{1,0:T(8,128)(2,1)S(1)}, bf16[144,1024]{1,0:T(8,128)(2,1)S(1)}) custom-call(s32[1]{0:T(128)} %bitcast.place, s32[4,4]{1,0:T(4,128)S(1)} %maximum_convert_fusion.q_ids, s32[8,4]{1,0:T(8,128)S(1)} %bitcast.5, s32[8,4]{1,0:T(8,128)S(1)} %bitcast.7, ...), custom_call_target="tpu_custom_call" | custom-call | flops 3221225472 | bytes 2097152 | tf_op jit(solution)/shard_map/pallas_call | solution.py:188
  53.7 4.7 %collective-permute-start.4 = (bf16[144,1024]{1,0:T(8,128)(2,1)S(1)}, bf16[144,1024]{1,0:T(8,128)(2,1)S(1)}, u32[]{:S(2)}, u32[]{:S(2)}) collective-permute-start(bf16[144,1024]{1,0:T(8,128)(2,1)S(1)} %get-tuple-element.33), channel_id=1, source_target_pairs={{0,48},{8,56},{16,0},{24,8},{32,16},{40,24},{48,32},{56,40},{64,11... | collective-permute-start | bytes 884744 | tf_op jit(solution)/shard_map/ppermute | solution.py:347
  58.3 2.7 %collective-permute-start.5 = (bf16[144,1024]{1,0:T(8,128)(2,1)S(1)}, bf16[144,1024]{1,0:T(8,128)(2,1)S(1)}, u32[]{:S(2)}, u32[]{:S(2)}) collective-permute-start(bf16[144,1024]{1,0:T(8,128)(2,1)S(1)} %get-tuple-element.34), channel_id=1, source_target_pairs={{0,32},{8,40},{16,48},{24,56},{32,0},{40,8},{48,16},{56,24},{64,96... | collective-permute-start | bytes 884744 | tf_op jit(solution)/shard_map/ppermute | solution.py:347
  61.0 2.3 %collective-permute-start.6 = (bf16[144,1024]{1,0:T(8,128)(2,1)S(1)}, bf16[144,1024]{1,0:T(8,128)(2,1)S(1)}, u32[]{:S(2)}, u32[]{:S(2)}) collective-permute-start(bf16[144,1024]{1,0:T(8,128)(2,1)S(1)} %get-tuple-element.35), channel_id=1, source_target_pairs={{0,16},{8,24},{16,32},{24,40},{32,48},{40,56},{48,0},{56,8},{64,80... | collective-permute-start | bytes 884744 | tf_op jit(solution)/shard_map/ppermute | solution.py:347
  63.8 2.7 %shard_map.69.p0 = bf16[144,1024]{1,0:T(8,128)(2,1)S(1)} custom-call(s32[1]{0:T(128)} %bitcast.place, s32[4,4]{1,0:T(4,128)S(1)} %maximum_convert_fusion.q_ids, s32[8,4]{1,0:T(8,128)S(1)} %bitcast.6, s32[8,4]{1,0:T(8,128)S(1)} %bitcast.8, bf16[272,512]{1,0:T(8,128)(2,1)S(1)} %fusion.1.refs_0_, bf16[8,512,128]{2,1,0:T(8,128)(2,1)S(1)} %get-tuple-element.30.refs_1_.refs_3_, ...), custom_call_target="tpu_custom_call" | custom-call | flops 1073741824 | bytes 2097152 | tf_op jit(solution)/shard_map/pallas_call | solution.py:188
  66.6 4.6 %collective-permute-done.4.p1 = bf16[144,1024]{1,0:T(8,128)(2,1)S(1)} collective-permute-done((bf16[144,1024]{1,0:T(8,128)(2,1)S(1)}, bf16[144,1024]{1,0:T(8,128)(2,1)S(1)}, u32[]{:S(2)}, u32[]{:S(2)}) %collective-permute-start.4) | collective-permute-done | bytes 294944 | tf_op jit(solution)/shard_map/ppermute | solution.py:347
  71.7 5.2 %collective-permute-done.6.p3 = bf16[144,1024]{1,0:T(8,128)(2,1)S(1)} collective-permute-done((bf16[144,1024]{1,0:T(8,128)(2,1)S(1)}, bf16[144,1024]{1,0:T(8,128)(2,1)S(1)}, u32[]{:S(2)}, u32[]{:S(2)}) %collective-permute-start.6) | collective-permute-done | bytes 294944 | tf_op jit(solution)/shard_map/ppermute | solution.py:347
  76.8 1.4 %shard_map.71 = (bf16[256,512]{1,0:T(8,128)(2,1)}, bf16[256,512]{1,0:T(8,128)(2,1)S(1)}, bf16[256,512]{1,0:T(8,128)(2,1)S(1)}, bf16[256,512]{1,0:T(8,128)(2,1)S(...) custom-call(bf16[144,1024]{1,0:T(8,128)(2,1)S(1)} %shard_map.69.p0, ...), custom_call_target="tpu_custom_call" | custom-call | flops 402653184 | bytes 1572864 | tf_op jit(solution)/shard_map/pallas_call | solution.py:266
  78.3 4.7 %collective-permute-start.9 = (bf16[256,512]{1,0:T(8,128)(2,1)S(1)}, bf16[256,512]{1,0:T(8,128)(2,1)S(1)}, u32[]{:S(2)}, u32[]{:S(2)}) collective-permute-start(bf16[256,512]{1,0:T(8,128)(2,1)S(1)} %get-tuple-element.43), channel_id=1, source_target_pairs={{0,1},{1,2},{2,3},{3,4},{4,5},{5,6},{6,7},{7,0},{8,9},{9,10},{10,1... | collective-permute-start | bytes 786440 | tf_op jit(solution)/shard_map/ppermute | solution.py:297
  83.0 2.7 %collective-permute-start.10 = (bf16[256,256]{1,0:T(8,128)(2,1)S(1)}, bf16[256,256]{1,0:T(8,128)(2,1)S(1)}, u32[]{:S(2)}, u32[]{:S(2)}) collective-permute-start(bf16[256,256]{1,0:T(8,128)(2,1)S(1)} %get-tuple-element.44), channel_id=1, source_target_pairs={{0,2},{1,3},{2,4},{3,5},{4,6},{5,7},{6,0},{7,1},{8,10},{9,11},{10,... | collective-permute-start | bytes 393224 | tf_op jit(solution)/shard_map/ppermute | solution.py:297
  85.7 4.0 %collective-permute-start.13 = (bf16[256,256]{1,0:T(8,128)(2,1)S(1)}, bf16[256,256]{1,0:T(8,128)(2,1)S(1)}, u32[]{:S(2)}, u32[]{:S(2)}) collective-permute-start(bf16[256,256]{1,0:T(8,128)(2,1)S(1)} %get-tuple-element.47), channel_id=1, source_target_pairs={{0,6},{1,7},{2,0},{3,1},{4,2},{5,3},{6,4},{7,5},{8,14},{9,15},{10,... | collective-permute-start | bytes 393224 | tf_op jit(solution)/shard_map/ppermute | solution.py:297
  89.7 1.9 %collective-permute-start.12 = (bf16[256,512]{1,0:T(8,128)(2,1)S(1)}, bf16[256,512]{1,0:T(8,128)(2,1)S(1)}, u32[]{:S(2)}, u32[]{:S(2)}) collective-permute-start(bf16[256,512]{1,0:T(8,128)(2,1)S(1)} %get-tuple-element.46), channel_id=1, source_target_pairs={{0,7},{1,0},{2,1},{3,2},{4,3},{5,4},{6,5},{7,6},{8,15},{9,8},{10,9... | collective-permute-start | bytes 786440 | tf_op jit(solution)/shard_map/ppermute | solution.py:297
  92.5 5.1 %collective-permute-start.7 = (bf16[256,512]{1,0:T(8,128)(2,1)S(1)}, bf16[256,512]{1,0:T(8,128)(2,1)S(1)}, u32[]{:S(2)}, u32[]{:S(2)}) collective-permute-start(bf16[256,512]{1,0:T(8,128)(2,1)S(1)} %get-tuple-element.40), channel_id=1, source_target_pairs={{0,1},{1,2},{2,3},{3,4},{4,5},{5,6},{6,7},{7,0},{8,9},{9,10},{10,1... | collective-permute-start | bytes 786440 | tf_op jit(solution)/shard_map/ppermute | solution.py:297
  97.6 1.9 %collective-permute-start.8 = (bf16[256,512]{1,0:T(8,128)(2,1)S(1)}, bf16[256,512]{1,0:T(8,128)(2,1)S(1)}, u32[]{:S(2)}, u32[]{:S(2)}) collective-permute-start(bf16[256,512]{1,0:T(8,128)(2,1)S(1)} %get-tuple-element.41), channel_id=1, source_target_pairs={{0,7},{1,0},{2,1},{3,2},{4,3},{5,4},{6,5},{7,6},{8,15},{9,8},{10,9... | collective-permute-start | bytes 786440 | tf_op jit(solution)/shard_map/ppermute | solution.py:297
  99.7 4.0 %collective-permute-start.11 = (bf16[256,512]{1,0:T(8,128)(2,1)S(1)}, bf16[256,512]{1,0:T(8,128)(2,1)S(1)}, u32[]{:S(2)}, u32[]{:S(2)}) collective-permute-start(bf16[256,512]{1,0:T(8,128)(2,1)S(1)} %add_convert_fusion.2), channel_id=1, source_target_pairs={{0,2},{1,3},{2,4},{3,5},{4,6},{5,7},{6,0},{7,1},{8,10},{9,11},{10,... | collective-permute-start | bytes 786440 | tf_op jit(solution)/shard_map/ppermute | solution.py:297
  103.8 2.7 %collective-permute-start.14 = (bf16[256,512]{1,0:T(8,128)(2,1)S(1)}, bf16[256,512]{1,0:T(8,128)(2,1)S(1)}, u32[]{:S(2)}, u32[]{:S(2)}) collective-permute-start(bf16[256,512]{1,0:T(8,128)(2,1)S(1)} %add_convert_fusion.1), channel_id=1, source_target_pairs={{0,6},{1,7},{2,0},{3,1},{4,2},{5,3},{6,4},{7,5},{8,14},{9,15},{10,... | collective-permute-start | bytes 786440 | tf_op jit(solution)/shard_map/ppermute | solution.py:297
  106.5 1.9 %collective-permute-done.8 = bf16[256,512]{1,0:T(8,128)(2,1)S(1)} collective-permute-done((bf16[256,512]{1,0:T(8,128)(2,1)S(1)}, bf16[256,512]{1,0:T(8,128)(2,1)S(1)}, u32[]{:S(2)}, u32[]{:S(2)}) %collective-permute-start.8) | collective-permute-done | bytes 262176 | tf_op jit(solution)/shard_map/ppermute | solution.py:297
  108.5 2.3 %collective-permute-done.11 = bf16[256,512]{1,0:T(8,128)(2,1)S(1)} collective-permute-done((bf16[256,512]{1,0:T(8,128)(2,1)S(1)}, bf16[256,512]{1,0:T(8,128)(2,1)S(1)}, u32[]{:S(2)}, u32[]{:S(2)}) %collective-permute-start.11) | collective-permute-done | bytes 262176 | tf_op jit(solution)/shard_map/ppermute | solution.py:297
  110.7 9.8 %collective-permute-done.14 = bf16[256,512]{1,0:T(8,128)(2,1)S(1)} collective-permute-done((bf16[256,512]{1,0:T(8,128)(2,1)S(1)}, bf16[256,512]{1,0:T(8,128)(2,1)S(1)}, u32[]{:S(2)}, u32[]{:S(2)}) %collective-permute-start.14) | collective-permute-done | bytes 262176 | tf_op jit(solution)/shard_map/ppermute | solution.py:297
  120.5 0.9 add_convert_fusion
  (29 shorter events, 2.8 us)
Async XLA Ops:
  0.6 13.1 %copy-start.1 = (bf16[256,512]{1,0:T(8,128)(2,1)S(1)}, bf16[256,512]{1,0:T(8,128)(2,1)}, u32[]{:S(2)}) copy-start(bf16[256,512]{1,0:T(8,128)(2,1)} %param.5) | copy-start | bytes 786436
  3.4 39.8 %all-to-all-start = ((bf16[8,528,128]{2,1,0:T(8,128)(2,1)}), bf16[8,528,128]{2,1,0:T(8,128)(2,1)S(1)}, u32[]{:S(2)}, u32[]{:S(2)}) async-start(bf16[8,528,128]{2,1,0:T(8,128)(2,1)} %broadcast_in_dim.10), calls=%async_computation | async-start | bytes 2162688 | tf_op jit(solution)/shard_map/all_to_all | solution.py:328
  13.7 16.3 %collective-permute-start.2 = (bf16[272,512]{1,0:T(8,128)(2,1)S(1)}, bf16[272,512]{1,0:T(8,128)(2,1)S(1)}, u32[]{:S(2)}, u32[]{:S(2)}) collective-permute-start(bf16[272,512]{1,0:T(8,128)(2,1)S(1)} %fusion.1.refs_0_), channel_id=1, source_target_pairs={{0,48},{8,56},{16,0},{24,8},{32,16},{40,24},{48,32},{56,40},{64,11... | collective-permute-start | bytes 835592 | tf_op jit(solution)/shard_map/ppermute | solution.py:322
  18.4 13.0 %collective-permute-start.1 = (bf16[272,512]{1,0:T(8,128)(2,1)S(1)}, bf16[272,512]{1,0:T(8,128)(2,1)S(1)}, u32[]{:S(2)}, u32[]{:S(2)}) collective-permute-start(bf16[272,512]{1,0:T(8,128)(2,1)S(1)} %fusion.1.refs_0_), channel_id=1, source_target_pairs={{0,32},{8,40},{16,48},{24,56},{32,0},{40,8},{48,16},{56,24},{64,96... | collective-permute-start | bytes 835592 | tf_op jit(solution)/shard_map/ppermute | solution.py:322
  21.1 14.5 %collective-permute-start = (bf16[272,512]{1,0:T(8,128)(2,1)S(1)}, bf16[272,512]{1,0:T(8,128)(2,1)S(1)}, u32[]{:S(2)}, u32[]{:S(2)}) collective-permute-start(bf16[272,512]{1,0:T(8,128)(2,1)S(1)} %fusion.1.refs_0_), channel_id=1, source_target_pairs={{0,16},{8,24},{16,32},{24,40},{32,48},{40,56},{48,0},{56,8},{64,80... | collective-permute-start | bytes 835592 | tf_op jit(solution)/shard_map/ppermute | solution.py:322
  43.1 4.6 %collective-permute-start.3 = (bf16[8,528,128]{2,1,0:T(8,128)(2,1)S(1)}, bf16[8,528,128]{2,1,0:T(8,128)(2,1)S(1)}, u32[]{:S(2)}, u32[]{:S(2)}) collective-permute-start(bf16[8,528,128]{2,1,0:T(8,128)(2,1)S(1)} %all-to-all-done.kv_own), channel_id=1, source_target_pairs={{0,8},{8,0},{16,24},{24,16},{32,40},{40,32},{48,56},{56,48},{64,72... | collective-permute-start | bytes 3244040 | tf_op jit(solution)/shard_map/ppermute | solution.py:337
  47.8 15.5 %copy-start = (bf16[512,4096]{1,0:T(8,128)(2,1)S(1)}, bf16[512,4096]{1,0:T(8,128)(2,1)}, u32[]{:S(2)}) copy-start(bf16[512,4096]{1,0:T(8,128)(2,1)} %param.9) | copy-start | bytes 12582916
  53.7 17.6 %collective-permute-start.4 = (bf16[144,1024]{1,0:T(8,128)(2,1)S(1)}, bf16[144,1024]{1,0:T(8,128)(2,1)S(1)}, u32[]{:S(2)}, u32[]{:S(2)}) collective-permute-start(bf16[144,1024]{1,0:T(8,128)(2,1)S(1)} %get-tuple-element.33), channel_id=1, source_target_pairs={{0,48},{8,56},{16,0},{24,8},{32,16},{40,24},{48,32},{56,40},{64,11... | collective-permute-start | bytes 884744 | tf_op jit(solution)/shard_map/ppermute | solution.py:347
  58.3 13.3 %collective-permute-start.5 = (bf16[144,1024]{1,0:T(8,128)(2,1)S(1)}, bf16[144,1024]{1,0:T(8,128)(2,1)S(1)}, u32[]{:S(2)}, u32[]{:S(2)}) collective-permute-start(bf16[144,1024]{1,0:T(8,128)(2,1)S(1)} %get-tuple-element.34), channel_id=1, source_target_pairs={{0,32},{8,40},{16,48},{24,56},{32,0},{40,8},{48,16},{56,24},{64,96... | collective-permute-start | bytes 884744 | tf_op jit(solution)/shard_map/ppermute | solution.py:347
  61.0 15.8 %collective-permute-start.6 = (bf16[144,1024]{1,0:T(8,128)(2,1)S(1)}, bf16[144,1024]{1,0:T(8,128)(2,1)S(1)}, u32[]{:S(2)}, u32[]{:S(2)}) collective-permute-start(bf16[144,1024]{1,0:T(8,128)(2,1)S(1)} %get-tuple-element.35), channel_id=1, source_target_pairs={{0,16},{8,24},{16,32},{24,40},{32,48},{40,56},{48,0},{56,8},{64,80... | collective-permute-start | bytes 884744 | tf_op jit(solution)/shard_map/ppermute | solution.py:347
  78.3 21.3 %collective-permute-start.9 = (bf16[256,512]{1,0:T(8,128)(2,1)S(1)}, bf16[256,512]{1,0:T(8,128)(2,1)S(1)}, u32[]{:S(2)}, u32[]{:S(2)}) collective-permute-start(bf16[256,512]{1,0:T(8,128)(2,1)S(1)} %get-tuple-element.43), channel_id=1, source_target_pairs={{0,1},{1,2},{2,3},{3,4},{4,5},{5,6},{6,7},{7,0},{8,9},{9,10},{10,1... | collective-permute-start | bytes 786440 | tf_op jit(solution)/shard_map/ppermute | solution.py:297
  83.0 14.7 %collective-permute-start.10 = (bf16[256,256]{1,0:T(8,128)(2,1)S(1)}, bf16[256,256]{1,0:T(8,128)(2,1)S(1)}, u32[]{:S(2)}, u32[]{:S(2)}) collective-permute-start(bf16[256,256]{1,0:T(8,128)(2,1)S(1)} %get-tuple-element.44), channel_id=1, source_target_pairs={{0,2},{1,3},{2,4},{3,5},{4,6},{5,7},{6,0},{7,1},{8,10},{9,11},{10,... | collective-permute-start | bytes 393224 | tf_op jit(solution)/shard_map/ppermute | solution.py:297
  85.7 18.0 %collective-permute-start.13 = (bf16[256,256]{1,0:T(8,128)(2,1)S(1)}, bf16[256,256]{1,0:T(8,128)(2,1)S(1)}, u32[]{:S(2)}, u32[]{:S(2)}) collective-permute-start(bf16[256,256]{1,0:T(8,128)(2,1)S(1)} %get-tuple-element.47), channel_id=1, source_target_pairs={{0,6},{1,7},{2,0},{3,1},{4,2},{5,3},{6,4},{7,5},{8,14},{9,15},{10,... | collective-permute-start | bytes 393224 | tf_op jit(solution)/shard_map/ppermute | solution.py:297
  89.7 14.0 %collective-permute-start.12 = (bf16[256,512]{1,0:T(8,128)(2,1)S(1)}, bf16[256,512]{1,0:T(8,128)(2,1)S(1)}, u32[]{:S(2)}, u32[]{:S(2)}) collective-permute-start(bf16[256,512]{1,0:T(8,128)(2,1)S(1)} %get-tuple-element.46), channel_id=1, source_target_pairs={{0,7},{1,0},{2,1},{3,2},{4,3},{5,4},{6,5},{7,6},{8,15},{9,8},{10,9... | collective-permute-start | bytes 786440 | tf_op jit(solution)/shard_map/ppermute | solution.py:297
  92.5 14.1 %collective-permute-start.7 = (bf16[256,512]{1,0:T(8,128)(2,1)S(1)}, bf16[256,512]{1,0:T(8,128)(2,1)S(1)}, u32[]{:S(2)}, u32[]{:S(2)}) collective-permute-start(bf16[256,512]{1,0:T(8,128)(2,1)S(1)} %get-tuple-element.40), channel_id=1, source_target_pairs={{0,1},{1,2},{2,3},{3,4},{4,5},{5,6},{6,7},{7,0},{8,9},{9,10},{10,1... | collective-permute-start | bytes 786440 | tf_op jit(solution)/shard_map/ppermute | solution.py:297
  97.6 10.9 %collective-permute-start.8 = (bf16[256,512]{1,0:T(8,128)(2,1)S(1)}, bf16[256,512]{1,0:T(8,128)(2,1)S(1)}, u32[]{:S(2)}, u32[]{:S(2)}) collective-permute-start(bf16[256,512]{1,0:T(8,128)(2,1)S(1)} %get-tuple-element.41), channel_id=1, source_target_pairs={{0,7},{1,0},{2,1},{3,2},{4,3},{5,4},{6,5},{7,6},{8,15},{9,8},{10,9... | collective-permute-start | bytes 786440 | tf_op jit(solution)/shard_map/ppermute | solution.py:297
  99.7 11.1 %collective-permute-start.11 = (bf16[256,512]{1,0:T(8,128)(2,1)S(1)}, bf16[256,512]{1,0:T(8,128)(2,1)S(1)}, u32[]{:S(2)}, u32[]{:S(2)}) collective-permute-start(bf16[256,512]{1,0:T(8,128)(2,1)S(1)} %add_convert_fusion.2), channel_id=1, source_target_pairs={{0,2},{1,3},{2,4},{3,5},{4,6},{5,7},{6,0},{7,1},{8,10},{9,11},{10,... | collective-permute-start | bytes 786440 | tf_op jit(solution)/shard_map/ppermute | solution.py:297
  103.8 16.7 %collective-permute-start.14 = (bf16[256,512]{1,0:T(8,128)(2,1)S(1)}, bf16[256,512]{1,0:T(8,128)(2,1)S(1)}, u32[]{:S(2)}, u32[]{:S(2)}) collective-permute-start(bf16[256,512]{1,0:T(8,128)(2,1)S(1)} %add_convert_fusion.1), channel_id=1, source_target_pairs={{0,6},{1,7},{2,0},{3,1},{4,2},{5,3},{6,4},{7,5},{8,14},{9,15},{10,... | collective-permute-start | bytes 786440 | tf_op jit(solution)/shard_map/ppermute | solution.py:297

commit v5 on v4

--- a/solution.py
+++ b/solution.py
@@ -15,7 +15,7 @@
 NZ, NX, NC = 8, 4, 2
 NY = 8
 QCOLS = GROUP * ROWS
-FOREIGN = (2, 1, 3)
+FOREIGN = (2, 3, 1)
 PAD = 16
 NEG_BIG = -1e30
 SCALE = math.log2(math.e) / math.sqrt(HDIM)
@@ -313,18 +313,16 @@
 
 def per_device(query_rows, key_rows, value_rows, doc_ids, out_weight):
     place = lax.axis_index("ctx").reshape(1)
-    ids = doc_ids.astype(jnp.bfloat16)[None, :]
-
-    q_packed = jnp.concatenate(
-        [query_rows, jnp.pad(ids, ((0, PAD - 1), (0, query_rows.shape[1] - 4)))], axis=0
-    )
+
+    def id_rows(columns):
+        return jnp.pad(doc_ids[None, :], ((0, PAD - 1), (0, columns - 4))).astype(jnp.bfloat16)
+
+    q_packed = jnp.concatenate([query_rows, id_rows(query_rows.shape[1])], axis=0)
     q_blocks = [q_packed] + [
         lax.ppermute(q_packed, "ctx", ctx_perm(lambda z, x, c, r=r: (z, x + r, c)))
         for r in range(1, NX)
     ]
-    kv_packed = jnp.concatenate(
-        [key_rows, value_rows, jnp.pad(ids, ((0, PAD - 1), (0, HDIM - 4)))], axis=0
-    )
+    kv_packed = jnp.concatenate([key_rows, value_rows, id_rows(HDIM)], axis=0)
     kv_own = lax.all_to_all(
         jnp.broadcast_to(kv_packed[None], (NZ,) + kv_packed.shape),
         "ctx",
@@ -342,7 +340,7 @@
     k_held, v_turned = hold(place, kv_own, kv_other)
     arrays = (place, q_ids, own_ids, other_ids, q_blocks, k_held, v_turned)
     made = dict(zip(FOREIGN, attend(FOREIGN, *arrays)))
-    made[1], weight = lax.optimization_barrier((made[1], out_weight))
+    made[2], weight = lax.optimization_barrier((made[2], out_weight))
     parts = {
         r: lax.ppermute(made[r], "ctx", ctx_perm(lambda z, x, c, r=r: (z, x - r, c)))
         for r in FOREIGN
@@ -350,7 +348,7 @@
     (parts[0],) = attend((0,), *arrays)
     far_weight = columns_of(y, weight, (3, -3, 4))
     near_weight = columns_of(y, weight, (2, -2, 1, -1, 0))
-    attended, kept, *far = project_far([parts[r] for r in range(NX)], far_weight)
+    attended, kept, *far = project_far([parts[r] for r in (0, 2, 3, 1)], far_weight)
     near = project_near(kept, near_weight)
     return attended, sum_over_hd(far, near)
 

time: 122 us -> 119 us (0.975)
  the two profiles are of different devices: /device:TPU:24 before, /device:TPU:6 now
where the time goes in v5:
time: 119 us; the launch traced here: 117 us
  starting transfers between devices  60.2 us (51%)
  waiting for transfers between devices  40.5 us (34%)
  Pallas kernels  10.9 us (9%)
  other arithmetic  2.77 us (2%)
  local copies, waits for them, and re-layouts  1.6 us (1%)
    ppermute x8, starting transfers between devices, move(): return lax.ppermute(rows, 'hd', [(i, (i + step) % NY) for i in range(NY)])  29 us
    ppermute x8, waiting for transfers between devices, move(): return lax.ppermute(rows, 'hd', [(i, (i + step) % NY) for i in range(NY)])  11.6 us
    all_to_all x1, starting transfers between devices, per_device(): lax.all_to_all(jnp.broadcast_to(kv_packed[None], (NZ,) + kv_packed.shape)...  10.3 us
    ppermute x3, waiting for transfers between devices, per_device(): lax.ppermute(q_packed, 'ctx', ctx_perm(lambda z, x, c, r=r: (z, x + r, c)))  9.94 us
    ppermute x3, starting transfers between devices, per_device(): lax.ppermute(q_packed, 'ctx', ctx_perm(lambda z, x, c, r=r: (z, x + r, c)))  9.76 us
    all_to_all x1, waiting for transfers between devices, per_device(): lax.all_to_all(jnp.broadcast_to(kv_packed[None], (NZ,) + kv_packed.shape)...  9.69 us
    ppermute x3, starting transfers between devices, per_device(): lax.ppermute(made[r], 'ctx', ctx_perm(lambda z, x, c, r=r: (z, x - r, c)))  9.15 us
    pallas_call x2, Pallas kernels, attend(): pl.pallas_call(functools.partial(attend_kernel, shifts), out_shape=(jax.S...  8.51 us
  transfers between devices with their start and end apart: 16, of which 9 were waited for; matrix products, arithmetic and copies ran while one was open for 1% of the time, Pallas kernels for 3%

profile of v5, /device:TPU:6, one launch (start us, length us, event | category | flops | bytes accessed | tf_op | source)
XLA Modules:
  0.0 117.0 jit_solution(10443113541535011248)
XLA Ops:
  1.3 0.9 fusion.3
  2.2 1.2 broadcast_in_dim.5
  3.4 10.3 %all-to-all-start = ((bf16[8,528,128]{2,1,0:T(8,128)(2,1)}), bf16[8,528,128]{2,1,0:T(8,128)(2,1)S(1)}, u32[]{:S(2)}, u32[]{:S(2)}) async-start(bf16[8,528,128]{2,1,0:T(8,128)(2,1)} %broadcast_in_dim.5), calls=%async_computation | async-start | bytes 2162688 | tf_op jit(solution)/shard_map/all_to_all | solution.py:326
  13.7 2.7 %collective-permute-start.2 = (bf16[272,512]{1,0:T(8,128)(2,1)S(1)}, bf16[272,512]{1,0:T(8,128)(2,1)S(1)}, u32[]{:S(2)}, u32[]{:S(2)}) collective-permute-start(bf16[272,512]{1,0:T(8,128)(2,1)S(1)} %fusion.1.refs_0_), channel_id=1, source_target_pairs={{0,48},{8,56},{16,0},{24,8},{32,16},{40,24},{48,32},{56,40},{64,11... | collective-permute-start | bytes 835592 | tf_op jit(solution)/shard_map/ppermute | solution.py:322
  16.5 3.0 %collective-permute-start.1 = (bf16[272,512]{1,0:T(8,128)(2,1)S(1)}, bf16[272,512]{1,0:T(8,128)(2,1)S(1)}, u32[]{:S(2)}, u32[]{:S(2)}) collective-permute-start(bf16[272,512]{1,0:T(8,128)(2,1)S(1)} %fusion.1.refs_0_), channel_id=1, source_target_pairs={{0,32},{8,40},{16,48},{24,56},{32,0},{40,8},{48,16},{56,24},{64,96... | collective-permute-start | bytes 835592 | tf_op jit(solution)/shard_map/ppermute | solution.py:322
  19.5 4.0 %collective-permute-start = (bf16[272,512]{1,0:T(8,128)(2,1)S(1)}, bf16[272,512]{1,0:T(8,128)(2,1)S(1)}, u32[]{:S(2)}, u32[]{:S(2)}) collective-permute-start(bf16[272,512]{1,0:T(8,128)(2,1)S(1)} %fusion.1.refs_0_), channel_id=1, source_target_pairs={{0,16},{8,24},{16,32},{24,40},{32,48},{40,56},{48,0},{56,8},{64,80... | collective-permute-start | bytes 835592 | tf_op jit(solution)/shard_map/ppermute | solution.py:322
  23.5 7.4 %collective-permute-done.2.refs_1_ = bf16[272,512]{1,0:T(8,128)(2,1)S(1)} collective-permute-done((bf16[272,512]{1,0:T(8,128)(2,1)S(1)}, bf16[272,512]{1,0:T(8,128)(2,1)S(1)}, u32[]{:S(2)}, u32[]{:S(2)}) %collective-permute-start.2) | collective-permute-done | bytes 278560 | tf_op jit(solution)/shard_map/ppermute | solution.py:322
  30.9 2.5 %collective-permute-done.refs_2_ = bf16[272,512]{1,0:T(8,128)(2,1)S(1)} collective-permute-done((bf16[272,512]{1,0:T(8,128)(2,1)S(1)}, bf16[272,512]{1,0:T(8,128)(2,1)S(1)}, u32[]{:S(2)}, u32[]{:S(2)}) %collective-permute-start) | collective-permute-done | bytes 278560 | tf_op jit(solution)/shard_map/ppermute | solution.py:322
  33.5 9.7 %all-to-all-done.kv_own = bf16[8,528,128]{2,1,0:T(8,128)(2,1)S(1)} async-done(((bf16[8,528,128]{2,1,0:T(8,128)(2,1)}), bf16[8,528,128]{2,1,0:T(8,128)(2,1)S(1)}, u32[]{:S(2)}, u32[]{:S(2)}) %all-to-all-start) | async-done | bytes 1081376 | tf_op jit(solution)/shard_map/all_to_all | solution.py:326
  43.1 1.9 %collective-permute-start.3 = (bf16[8,528,128]{2,1,0:T(8,128)(2,1)S(1)}, bf16[8,528,128]{2,1,0:T(8,128)(2,1)S(1)}, u32[]{:S(2)}, u32[]{:S(2)}) collective-permute-start(bf16[8,528,128]{2,1,0:T(8,128)(2,1)S(1)} %all-to-all-done.kv_own), channel_id=1, source_target_pairs={{0,8},{8,0},{16,24},{24,16},{32,40},{40,32},{48,56},{56,48},{64,72... | collective-permute-start | bytes 3244040 | tf_op jit(solution)/shard_map/ppermute | solution.py:335
  45.2 2.5 %collective-permute-done.3.kv_other = bf16[8,528,128]{2,1,0:T(8,128)(2,1)S(1)} collective-permute-done((bf16[8,528,128]{2,1,0:T(8,128)(2,1)S(1)}, bf16[8,528,128]{2,1,0:T(8,128)(2,1)S(1)}, u32[]{:S(2)}, u32[]{:S(2)}) %collective-permute-start.3) | collective-permute-done | bytes 1081376 | tf_op jit(solution)/shard_map/ppermute | solution.py:335
  47.8 5.8 %shard_map.70 = (bf16[144,1024]{1,0:T(8,128)(2,1)S(1)}, bf16[144,1024]{1,0:T(8,128)(2,1)S(1)}, bf16[144,1024]{1,0:T(8,128)(2,1)S(1)}) custom-call(s32[1]{0:T(128)} %bitcast.place, s32[4,4]{1,0:T(4,128)S(1)} %maximum_convert_fusion.q_ids, s32[8,4]{1,0:T(8,128)S(1)} %bitcast.5, s32[8,4]{1,0:T(8,128)S(1)} %bitcast.7, ...), custom_call_target="tpu_custom_call" | custom-call | flops 3221225472 | bytes 2097152 | tf_op jit(solution)/shard_map/pallas_call | solution.py:188
  53.7 3.3 %collective-permute-start.4 = (bf16[144,1024]{1,0:T(8,128)(2,1)S(1)}, bf16[144,1024]{1,0:T(8,128)(2,1)S(1)}, u32[]{:S(2)}, u32[]{:S(2)}) collective-permute-start(bf16[144,1024]{1,0:T(8,128)(2,1)S(1)} %get-tuple-element.33), channel_id=1, source_target_pairs={{0,32},{8,40},{16,48},{24,56},{32,0},{40,8},{48,16},{56,24},{64,96... | collective-permute-start | bytes 884744 | tf_op jit(solution)/shard_map/ppermute | solution.py:345
  57.0 3.5 %collective-permute-start.5 = (bf16[144,1024]{1,0:T(8,128)(2,1)S(1)}, bf16[144,1024]{1,0:T(8,128)(2,1)S(1)}, u32[]{:S(2)}, u32[]{:S(2)}) collective-permute-start(bf16[144,1024]{1,0:T(8,128)(2,1)S(1)} %get-tuple-element.34), channel_id=1, source_target_pairs={{0,16},{8,24},{16,32},{24,40},{32,48},{40,56},{48,0},{56,8},{64,80... | collective-permute-start | bytes 884744 | tf_op jit(solution)/shard_map/ppermute | solution.py:345
  60.4 2.4 %collective-permute-start.6 = (bf16[144,1024]{1,0:T(8,128)(2,1)S(1)}, bf16[144,1024]{1,0:T(8,128)(2,1)S(1)}, u32[]{:S(2)}, u32[]{:S(2)}) collective-permute-start(bf16[144,1024]{1,0:T(8,128)(2,1)S(1)} %get-tuple-element.35), channel_id=1, source_target_pairs={{0,48},{8,56},{16,0},{24,8},{32,16},{40,24},{48,32},{56,40},{64,11... | collective-permute-start | bytes 884744 | tf_op jit(solution)/shard_map/ppermute | solution.py:345
  63.3 2.7 %shard_map.69.p0 = bf16[144,1024]{1,0:T(8,128)(2,1)S(1)} custom-call(s32[1]{0:T(128)} %bitcast.place, s32[4,4]{1,0:T(4,128)S(1)} %maximum_convert_fusion.q_ids, s32[8,4]{1,0:T(8,128)S(1)} %bitcast.6, s32[8,4]{1,0:T(8,128)S(1)} %bitcast.8, bf16[272,512]{1,0:T(8,128)(2,1)S(1)} %fusion.1.refs_0_, bf16[8,512,128]{2,1,0:T(8,128)(2,1)S(1)} %get-tuple-element.30.refs_1_.refs_3_, ...), custom_call_target="tpu_custom_call" | custom-call | flops 1073741824 | bytes 2097152 | tf_op jit(solution)/shard_map/pallas_call | solution.py:188
  66.1 0.8 collective-permute-done.4.p1
  66.9 3.3 %collective-permute-done.5.p2 = bf16[144,1024]{1,0:T(8,128)(2,1)S(1)} collective-permute-done((bf16[144,1024]{1,0:T(8,128)(2,1)S(1)}, bf16[144,1024]{1,0:T(8,128)(2,1)S(1)}, u32[]{:S(2)}, u32[]{:S(2)}) %collective-permute-start.5) | collective-permute-done | bytes 294944 | tf_op jit(solution)/shard_map/ppermute | solution.py:345
  70.2 2.7 %collective-permute-done.6.p3 = bf16[144,1024]{1,0:T(8,128)(2,1)S(1)} collective-permute-done((bf16[144,1024]{1,0:T(8,128)(2,1)S(1)}, bf16[144,1024]{1,0:T(8,128)(2,1)S(1)}, u32[]{:S(2)}, u32[]{:S(2)}) %collective-permute-start.6) | collective-permute-done | bytes 294944 | tf_op jit(solution)/shard_map/ppermute | solution.py:345
  72.9 1.4 %shard_map.71 = (bf16[256,512]{1,0:T(8,128)(2,1)}, bf16[256,512]{1,0:T(8,128)(2,1)S(1)}, bf16[256,512]{1,0:T(8,128)(2,1)S(1)}, bf16[256,512]{1,0:T(8,128)(2,1)S(...) custom-call(bf16[144,1024]{1,0:T(8,128)(2,1)S(1)} %shard_map.69.p0, ...), custom_call_target="tpu_custom_call" | custom-call | flops 402653184 | bytes 1572864 | tf_op jit(solution)/shard_map/pallas_call | solution.py:266
  74.4 3.5 %collective-permute-start.9 = (bf16[256,512]{1,0:T(8,128)(2,1)S(1)}, bf16[256,512]{1,0:T(8,128)(2,1)S(1)}, u32[]{:S(2)}, u32[]{:S(2)}) collective-permute-start(bf16[256,512]{1,0:T(8,128)(2,1)S(1)} %get-tuple-element.43), channel_id=1, source_target_pairs={{0,1},{1,2},{2,3},{3,4},{4,5},{5,6},{6,7},{7,0},{8,9},{9,10},{10,1... | collective-permute-start | bytes 786440 | tf_op jit(solution)/shard_map/ppermute | solution.py:297
  77.8 4.5 %collective-permute-start.10 = (bf16[256,256]{1,0:T(8,128)(2,1)S(1)}, bf16[256,256]{1,0:T(8,128)(2,1)S(1)}, u32[]{:S(2)}, u32[]{:S(2)}) collective-permute-start(bf16[256,256]{1,0:T(8,128)(2,1)S(1)} %get-tuple-element.44), channel_id=1, source_target_pairs={{0,2},{1,3},{2,4},{3,5},{4,6},{5,7},{6,0},{7,1},{8,10},{9,11},{10,... | collective-permute-start | bytes 393224 | tf_op jit(solution)/shard_map/ppermute | solution.py:297
  82.3 3.5 %collective-permute-start.13 = (bf16[256,256]{1,0:T(8,128)(2,1)S(1)}, bf16[256,256]{1,0:T(8,128)(2,1)S(1)}, u32[]{:S(2)}, u32[]{:S(2)}) collective-permute-start(bf16[256,256]{1,0:T(8,128)(2,1)S(1)} %get-tuple-element.47), channel_id=1, source_target_pairs={{0,6},{1,7},{2,0},{3,1},{4,2},{5,3},{6,4},{7,5},{8,14},{9,15},{10,... | collective-permute-start | bytes 393224 | tf_op jit(solution)/shard_map/ppermute | solution.py:297
  85.8 2.6 %collective-permute-start.12 = (bf16[256,512]{1,0:T(8,128)(2,1)S(1)}, bf16[256,512]{1,0:T(8,128)(2,1)S(1)}, u32[]{:S(2)}, u32[]{:S(2)}) collective-permute-start(bf16[256,512]{1,0:T(8,128)(2,1)S(1)} %get-tuple-element.46), channel_id=1, source_target_pairs={{0,7},{1,0},{2,1},{3,2},{4,3},{5,4},{6,5},{7,6},{8,15},{9,8},{10,9... | collective-permute-start | bytes 786440 | tf_op jit(solution)/shard_map/ppermute | solution.py:297
  88.4 0.8 shard_map.72
  89.3 3.2 %collective-permute-start.7 = (bf16[256,512]{1,0:T(8,128)(2,1)S(1)}, bf16[256,512]{1,0:T(8,128)(2,1)S(1)}, u32[]{:S(2)}, u32[]{:S(2)}) collective-permute-start(bf16[256,512]{1,0:T(8,128)(2,1)S(1)} %get-tuple-element.40), channel_id=1, source_target_pairs={{0,1},{1,2},{2,3},{3,4},{4,5},{5,6},{6,7},{7,0},{8,9},{9,10},{10,1... | collective-permute-start | bytes 786440 | tf_op jit(solution)/shard_map/ppermute | solution.py:297
  92.5 3.8 %collective-permute-start.8 = (bf16[256,512]{1,0:T(8,128)(2,1)S(1)}, bf16[256,512]{1,0:T(8,128)(2,1)S(1)}, u32[]{:S(2)}, u32[]{:S(2)}) collective-permute-start(bf16[256,512]{1,0:T(8,128)(2,1)S(1)} %get-tuple-element.41), channel_id=1, source_target_pairs={{0,7},{1,0},{2,1},{3,2},{4,3},{5,4},{6,5},{7,6},{8,15},{9,8},{10,9... | collective-permute-start | bytes 786440 | tf_op jit(solution)/shard_map/ppermute | solution.py:297
  96.5 3.0 %collective-permute-start.11 = (bf16[256,512]{1,0:T(8,128)(2,1)S(1)}, bf16[256,512]{1,0:T(8,128)(2,1)S(1)}, u32[]{:S(2)}, u32[]{:S(2)}) collective-permute-start(bf16[256,512]{1,0:T(8,128)(2,1)S(1)} %add_convert_fusion.2), channel_id=1, source_target_pairs={{0,2},{1,3},{2,4},{3,5},{4,6},{5,7},{6,0},{7,1},{8,10},{9,11},{10,... | collective-permute-start | bytes 786440 | tf_op jit(solution)/shard_map/ppermute | solution.py:297
  99.6 4.9 %collective-permute-start.14 = (bf16[256,512]{1,0:T(8,128)(2,1)S(1)}, bf16[256,512]{1,0:T(8,128)(2,1)S(1)}, u32[]{:S(2)}, u32[]{:S(2)}) collective-permute-start(bf16[256,512]{1,0:T(8,128)(2,1)S(1)} %add_convert_fusion.1), channel_id=1, source_target_pairs={{0,6},{1,7},{2,0},{3,1},{4,2},{5,3},{6,4},{7,5},{8,14},{9,15},{10,... | collective-permute-start | bytes 786440 | tf_op jit(solution)/shard_map/ppermute | solution.py:297
  104.6 7.8 %collective-permute-done.11 = bf16[256,512]{1,0:T(8,128)(2,1)S(1)} collective-permute-done((bf16[256,512]{1,0:T(8,128)(2,1)S(1)}, bf16[256,512]{1,0:T(8,128)(2,1)S(1)}, u32[]{:S(2)}, u32[]{:S(2)}) %collective-permute-start.11) | collective-permute-done | bytes 262176 | tf_op jit(solution)/shard_map/ppermute | solution.py:297
  112.3 3.8 %collective-permute-done.14 = bf16[256,512]{1,0:T(8,128)(2,1)S(1)} collective-permute-done((bf16[256,512]{1,0:T(8,128)(2,1)S(1)}, bf16[256,512]{1,0:T(8,128)(2,1)S(1)}, u32[]{:S(2)}, u32[]{:S(2)}) %collective-permute-start.14) | collective-permute-done | bytes 262176 | tf_op jit(solution)/shard_map/ppermute | solution.py:297
  116.2 0.9 add_convert_fusion
  (29 shorter events, 1.6 us)
Async XLA Ops:
  0.6 13.1 %copy-start.1 = (bf16[256,512]{1,0:T(8,128)(2,1)S(1)}, bf16[256,512]{1,0:T(8,128)(2,1)}, u32[]{:S(2)}) copy-start(bf16[256,512]{1,0:T(8,128)(2,1)} %param.5) | copy-start | bytes 786436
  3.4 39.8 %all-to-all-start = ((bf16[8,528,128]{2,1,0:T(8,128)(2,1)}), bf16[8,528,128]{2,1,0:T(8,128)(2,1)S(1)}, u32[]{:S(2)}, u32[]{:S(2)}) async-start(bf16[8,528,128]{2,1,0:T(8,128)(2,1)} %broadcast_in_dim.5), calls=%async_computation | async-start | bytes 2162688 | tf_op jit(solution)/shard_map/all_to_all | solution.py:326
  13.7 17.2 %collective-permute-start.2 = (bf16[272,512]{1,0:T(8,128)(2,1)S(1)}, bf16[272,512]{1,0:T(8,128)(2,1)S(1)}, u32[]{:S(2)}, u32[]{:S(2)}) collective-permute-start(bf16[272,512]{1,0:T(8,128)(2,1)S(1)} %fusion.1.refs_0_), channel_id=1, source_target_pairs={{0,48},{8,56},{16,0},{24,8},{32,16},{40,24},{48,32},{56,40},{64,11... | collective-permute-start | bytes 835592 | tf_op jit(solution)/shard_map/ppermute | solution.py:322
  16.5 14.4 %collective-permute-start.1 = (bf16[272,512]{1,0:T(8,128)(2,1)S(1)}, bf16[272,512]{1,0:T(8,128)(2,1)S(1)}, u32[]{:S(2)}, u32[]{:S(2)}) collective-permute-start(bf16[272,512]{1,0:T(8,128)(2,1)S(1)} %fusion.1.refs_0_), channel_id=1, source_target_pairs={{0,32},{8,40},{16,48},{24,56},{32,0},{40,8},{48,16},{56,24},{64,96... | collective-permute-start | bytes 835592 | tf_op jit(solution)/shard_map/ppermute | solution.py:322
  19.5 14.0 %collective-permute-start = (bf16[272,512]{1,0:T(8,128)(2,1)S(1)}, bf16[272,512]{1,0:T(8,128)(2,1)S(1)}, u32[]{:S(2)}, u32[]{:S(2)}) collective-permute-start(bf16[272,512]{1,0:T(8,128)(2,1)S(1)} %fusion.1.refs_0_), channel_id=1, source_target_pairs={{0,16},{8,24},{16,32},{24,40},{32,48},{40,56},{48,0},{56,8},{64,80... | collective-permute-start | bytes 835592 | tf_op jit(solution)/shard_map/ppermute | solution.py:322
  43.1 4.6 %collective-permute-start.3 = (bf16[8,528,128]{2,1,0:T(8,128)(2,1)S(1)}, bf16[8,528,128]{2,1,0:T(8,128)(2,1)S(1)}, u32[]{:S(2)}, u32[]{:S(2)}) collective-permute-start(bf16[8,528,128]{2,1,0:T(8,128)(2,1)S(1)} %all-to-all-done.kv_own), channel_id=1, source_target_pairs={{0,8},{8,0},{16,24},{24,16},{32,40},{40,32},{48,56},{56,48},{64,72... | collective-permute-start | bytes 3244040 | tf_op jit(solution)/shard_map/ppermute | solution.py:335
  47.8 15.0 %copy-start = (bf16[512,4096]{1,0:T(8,128)(2,1)S(1)}, bf16[512,4096]{1,0:T(8,128)(2,1)}, u32[]{:S(2)}) copy-start(bf16[512,4096]{1,0:T(8,128)(2,1)} %param.9) | copy-start | bytes 12582916
  53.7 13.2 %collective-permute-start.4 = (bf16[144,1024]{1,0:T(8,128)(2,1)S(1)}, bf16[144,1024]{1,0:T(8,128)(2,1)S(1)}, u32[]{:S(2)}, u32[]{:S(2)}) collective-permute-start(bf16[144,1024]{1,0:T(8,128)(2,1)S(1)} %get-tuple-element.33), channel_id=1, source_target_pairs={{0,32},{8,40},{16,48},{24,56},{32,0},{40,8},{48,16},{56,24},{64,96... | collective-permute-start | bytes 884744 | tf_op jit(solution)/shard_map/ppermute | solution.py:345
  57.0 13.3 %collective-permute-start.5 = (bf16[144,1024]{1,0:T(8,128)(2,1)S(1)}, bf16[144,1024]{1,0:T(8,128)(2,1)S(1)}, u32[]{:S(2)}, u32[]{:S(2)}) collective-permute-start(bf16[144,1024]{1,0:T(8,128)(2,1)S(1)} %get-tuple-element.34), channel_id=1, source_target_pairs={{0,16},{8,24},{16,32},{24,40},{32,48},{40,56},{48,0},{56,8},{64,80... | collective-permute-start | bytes 884744 | tf_op jit(solution)/shard_map/ppermute | solution.py:345
  60.4 12.5 %collective-permute-start.6 = (bf16[144,1024]{1,0:T(8,128)(2,1)S(1)}, bf16[144,1024]{1,0:T(8,128)(2,1)S(1)}, u32[]{:S(2)}, u32[]{:S(2)}) collective-permute-start(bf16[144,1024]{1,0:T(8,128)(2,1)S(1)} %get-tuple-element.35), channel_id=1, source_target_pairs={{0,48},{8,56},{16,0},{24,8},{32,16},{40,24},{48,32},{56,40},{64,11... | collective-permute-start | bytes 884744 | tf_op jit(solution)/shard_map/ppermute | solution.py:345
  74.4 22.0 %collective-permute-start.9 = (bf16[256,512]{1,0:T(8,128)(2,1)S(1)}, bf16[256,512]{1,0:T(8,128)(2,1)S(1)}, u32[]{:S(2)}, u32[]{:S(2)}) collective-permute-start(bf16[256,512]{1,0:T(8,128)(2,1)S(1)} %get-tuple-element.43), channel_id=1, source_target_pairs={{0,1},{1,2},{2,3},{3,4},{4,5},{5,6},{6,7},{7,0},{8,9},{9,10},{10,1... | collective-permute-start | bytes 786440 | tf_op jit(solution)/shard_map/ppermute | solution.py:297
  77.8 14.7 %collective-permute-start.10 = (bf16[256,256]{1,0:T(8,128)(2,1)S(1)}, bf16[256,256]{1,0:T(8,128)(2,1)S(1)}, u32[]{:S(2)}, u32[]{:S(2)}) collective-permute-start(bf16[256,256]{1,0:T(8,128)(2,1)S(1)} %get-tuple-element.44), channel_id=1, source_target_pairs={{0,2},{1,3},{2,4},{3,5},{4,6},{5,7},{6,0},{7,1},{8,10},{9,11},{10,... | collective-permute-start | bytes 393224 | tf_op jit(solution)/shard_map/ppermute | solution.py:297
  82.3 17.2 %collective-permute-start.13 = (bf16[256,256]{1,0:T(8,128)(2,1)S(1)}, bf16[256,256]{1,0:T(8,128)(2,1)S(1)}, u32[]{:S(2)}, u32[]{:S(2)}) collective-permute-start(bf16[256,256]{1,0:T(8,128)(2,1)S(1)} %get-tuple-element.47), channel_id=1, source_target_pairs={{0,6},{1,7},{2,0},{3,1},{4,2},{5,3},{6,4},{7,5},{8,14},{9,15},{10,... | collective-permute-start | bytes 393224 | tf_op jit(solution)/shard_map/ppermute | solution.py:297
  85.8 13.7 %collective-permute-start.12 = (bf16[256,512]{1,0:T(8,128)(2,1)S(1)}, bf16[256,512]{1,0:T(8,128)(2,1)S(1)}, u32[]{:S(2)}, u32[]{:S(2)}) collective-permute-start(bf16[256,512]{1,0:T(8,128)(2,1)S(1)} %get-tuple-element.46), channel_id=1, source_target_pairs={{0,7},{1,0},{2,1},{3,2},{4,3},{5,4},{6,5},{7,6},{8,15},{9,8},{10,9... | collective-permute-start | bytes 786440 | tf_op jit(solution)/shard_map/ppermute | solution.py:297
  89.3 15.3 %collective-permute-start.7 = (bf16[256,512]{1,0:T(8,128)(2,1)S(1)}, bf16[256,512]{1,0:T(8,128)(2,1)S(1)}, u32[]{:S(2)}, u32[]{:S(2)}) collective-permute-start(bf16[256,512]{1,0:T(8,128)(2,1)S(1)} %get-tuple-element.40), channel_id=1, source_target_pairs={{0,1},{1,2},{2,3},{3,4},{4,5},{5,6},{6,7},{7,0},{8,9},{9,10},{10,1... | collective-permute-start | bytes 786440 | tf_op jit(solution)/shard_map/ppermute | solution.py:297
  92.5 12.0 %collective-permute-start.8 = (bf16[256,512]{1,0:T(8,128)(2,1)S(1)}, bf16[256,512]{1,0:T(8,128)(2,1)S(1)}, u32[]{:S(2)}, u32[]{:S(2)}) collective-permute-start(bf16[256,512]{1,0:T(8,128)(2,1)S(1)} %get-tuple-element.41), channel_id=1, source_target_pairs={{0,7},{1,0},{2,1},{3,2},{4,3},{5,4},{6,5},{7,6},{8,15},{9,8},{10,9... | collective-permute-start | bytes 786440 | tf_op jit(solution)/shard_map/ppermute | solution.py:297
  96.5 15.9 %collective-permute-start.11 = (bf16[256,512]{1,0:T(8,128)(2,1)S(1)}, bf16[256,512]{1,0:T(8,128)(2,1)S(1)}, u32[]{:S(2)}, u32[]{:S(2)}) collective-permute-start(bf16[256,512]{1,0:T(8,128)(2,1)S(1)} %add_convert_fusion.2), channel_id=1, source_target_pairs={{0,2},{1,3},{2,4},{3,5},{4,6},{5,7},{6,0},{7,1},{8,10},{9,11},{10,... | collective-permute-start | bytes 786440 | tf_op jit(solution)/shard_map/ppermute | solution.py:297
  99.6 16.5 %collective-permute-start.14 = (bf16[256,512]{1,0:T(8,128)(2,1)S(1)}, bf16[256,512]{1,0:T(8,128)(2,1)S(1)}, u32[]{:S(2)}, u32[]{:S(2)}) collective-permute-start(bf16[256,512]{1,0:T(8,128)(2,1)S(1)} %add_convert_fusion.1), channel_id=1, source_target_pairs={{0,6},{1,7},{2,0},{3,1},{4,2},{5,3},{6,4},{7,5},{8,14},{9,15},{10,... | collective-permute-start | bytes 786440 | tf_op jit(solution)/shard_map/ppermute | solution.py:297

commit v6 on v5

--- a/solution.py
+++ b/solution.py
@@ -15,7 +15,7 @@
 NZ, NX, NC = 8, 4, 2
 NY = 8
 QCOLS = GROUP * ROWS
-FOREIGN = (2, 3, 1)
+FOREIGN = (2, 1, 3)
 PAD = 16
 NEG_BIG = -1e30
 SCALE = math.log2(math.e) / math.sqrt(HDIM)
@@ -348,7 +348,7 @@
     (parts[0],) = attend((0,), *arrays)
     far_weight = columns_of(y, weight, (3, -3, 4))
     near_weight = columns_of(y, weight, (2, -2, 1, -1, 0))
-    attended, kept, *far = project_far([parts[r] for r in (0, 2, 3, 1)], far_weight)
+    attended, kept, *far = project_far([parts[r] for r in (0, 2, 1, 3)], far_weight)
     near = project_near(kept, near_weight)
     return attended, sum_over_hd(far, near)
 

time: 119 us -> 119 us (level)
  transfers between devices with their start and end apart: 16 -> 16, of which waited for: 9 -> 8; matrix products, arithmetic and copies ran while one was open for 1% -> 1% of each run, Pallas kernels for 3% -> 3%
where the time goes in v6:
time: 119 us; the launch traced here: 117 us
  starting transfers between devices  60.3 us (51%)
  waiting for transfers between devices  40.4 us (34%)
  Pallas kernels  10.9 us (9%)
  other arithmetic  2.77 us (2%)
  local copies, waits for them, and re-layouts  1.6 us (1%)
    ppermute x8, starting transfers between devices, move(): return lax.ppermute(rows, 'hd', [(i, (i + step) % NY) for i in range(NY)])  29 us
    ppermute x8, waiting for transfers between devices, move(): return lax.ppermute(rows, 'hd', [(i, (i + step) % NY) for i in range(NY)])  12 us
    all_to_all x1, starting transfers between devices, per_device(): lax.all_to_all(jnp.broadcast_to(kv_packed[None], (NZ,) + kv_packed.shape)...  10.3 us
    ppermute x3, waiting for transfers between devices, per_device(): lax.ppermute(q_packed, 'ctx', ctx_perm(lambda z, x, c, r=r: (z, x + r, c)))  9.94 us
    ppermute x3, starting transfers between devices, per_device(): lax.ppermute(q_packed, 'ctx', ctx_perm(lambda z, x, c, r=r: (z, x + r, c)))  9.76 us
    all_to_all x1, waiting for transfers between devices, per_device(): lax.all_to_all(jnp.broadcast_to(kv_packed[None], (NZ,) + kv_packed.shape)...  9.69 us
    ppermute x3, starting transfers between devices, per_device(): lax.ppermute(made[r], 'ctx', ctx_perm(lambda z, x, c, r=r: (z, x - r, c)))  9.29 us
    pallas_call x2, Pallas kernels, attend(): pl.pallas_call(functools.partial(attend_kernel, shifts), out_shape=(jax.S...  8.51 us
  transfers between devices with their start and end apart: 16, of which 8 were waited for; matrix products, arithmetic and copies ran while one was open for 1% of the time, Pallas kernels for 3%

profile of v6, /device:TPU:6, one launch (start us, length us, event | category | flops | bytes accessed | tf_op | source)
XLA Modules:
  0.0 117.0 jit_solution(16563977159447928072)
XLA Ops:
  0.6 0.7 convert_bitcast_fusion
  1.3 0.9 fusion.3
  2.2 1.2 broadcast_in_dim.5
  3.4 10.3 %all-to-all-start = ((bf16[8,528,128]{2,1,0:T(8,128)(2,1)}), bf16[8,528,128]{2,1,0:T(8,128)(2,1)S(1)}, u32[]{:S(2)}, u32[]{:S(2)}) async-start(bf16[8,528,128]{2,1,0:T(8,128)(2,1)} %broadcast_in_dim.5), calls=%async_computation | async-start | bytes 2162688 | tf_op jit(solution)/shard_map/all_to_all | solution.py:326
  13.7 2.7 %collective-permute-start.2 = (bf16[272,512]{1,0:T(8,128)(2,1)S(1)}, bf16[272,512]{1,0:T(8,128)(2,1)S(1)}, u32[]{:S(2)}, u32[]{:S(2)}) collective-permute-start(bf16[272,512]{1,0:T(8,128)(2,1)S(1)} %fusion.1.refs_0_), channel_id=1, source_target_pairs={{0,48},{8,56},{16,0},{24,8},{32,16},{40,24},{48,32},{56,40},{64,11... | collective-permute-start | bytes 835592 | tf_op jit(solution)/shard_map/ppermute | solution.py:322
  16.5 3.0 %collective-permute-start.1 = (bf16[272,512]{1,0:T(8,128)(2,1)S(1)}, bf16[272,512]{1,0:T(8,128)(2,1)S(1)}, u32[]{:S(2)}, u32[]{:S(2)}) collective-permute-start(bf16[272,512]{1,0:T(8,128)(2,1)S(1)} %fusion.1.refs_0_), channel_id=1, source_target_pairs={{0,32},{8,40},{16,48},{24,56},{32,0},{40,8},{48,16},{56,24},{64,96... | collective-permute-start | bytes 835592 | tf_op jit(solution)/shard_map/ppermute | solution.py:322
  19.5 4.0 %collective-permute-start = (bf16[272,512]{1,0:T(8,128)(2,1)S(1)}, bf16[272,512]{1,0:T(8,128)(2,1)S(1)}, u32[]{:S(2)}, u32[]{:S(2)}) collective-permute-start(bf16[272,512]{1,0:T(8,128)(2,1)S(1)} %fusion.1.refs_0_), channel_id=1, source_target_pairs={{0,16},{8,24},{16,32},{24,40},{32,48},{40,56},{48,0},{56,8},{64,80... | collective-permute-start | bytes 835592 | tf_op jit(solution)/shard_map/ppermute | solution.py:322
  23.5 7.4 %collective-permute-done.2.refs_2_ = bf16[272,512]{1,0:T(8,128)(2,1)S(1)} collective-permute-done((bf16[272,512]{1,0:T(8,128)(2,1)S(1)}, bf16[272,512]{1,0:T(8,128)(2,1)S(1)}, u32[]{:S(2)}, u32[]{:S(2)}) %collective-permute-start.2) | collective-permute-done | bytes 278560 | tf_op jit(solution)/shard_map/ppermute | solution.py:322
  30.9 2.5 %collective-permute-done.refs_1_ = bf16[272,512]{1,0:T(8,128)(2,1)S(1)} collective-permute-done((bf16[272,512]{1,0:T(8,128)(2,1)S(1)}, bf16[272,512]{1,0:T(8,128)(2,1)S(1)}, u32[]{:S(2)}, u32[]{:S(2)}) %collective-permute-start) | collective-permute-done | bytes 278560 | tf_op jit(solution)/shard_map/ppermute | solution.py:322
  33.5 9.7 %all-to-all-done.kv_own = bf16[8,528,128]{2,1,0:T(8,128)(2,1)S(1)} async-done(((bf16[8,528,128]{2,1,0:T(8,128)(2,1)}), bf16[8,528,128]{2,1,0:T(8,128)(2,1)S(1)}, u32[]{:S(2)}, u32[]{:S(2)}) %all-to-all-start) | async-done | bytes 1081376 | tf_op jit(solution)/shard_map/all_to_all | solution.py:326
  43.1 1.9 %collective-permute-start.3 = (bf16[8,528,128]{2,1,0:T(8,128)(2,1)S(1)}, bf16[8,528,128]{2,1,0:T(8,128)(2,1)S(1)}, u32[]{:S(2)}, u32[]{:S(2)}) collective-permute-start(bf16[8,528,128]{2,1,0:T(8,128)(2,1)S(1)} %all-to-all-done.kv_own), channel_id=1, source_target_pairs={{0,8},{8,0},{16,24},{24,16},{32,40},{40,32},{48,56},{56,48},{64,72... | collective-permute-start | bytes 3244040 | tf_op jit(solution)/shard_map/ppermute | solution.py:335
  45.2 2.5 %collective-permute-done.3.kv_other = bf16[8,528,128]{2,1,0:T(8,128)(2,1)S(1)} collective-permute-done((bf16[8,528,128]{2,1,0:T(8,128)(2,1)S(1)}, bf16[8,528,128]{2,1,0:T(8,128)(2,1)S(1)}, u32[]{:S(2)}, u32[]{:S(2)}) %collective-permute-start.3) | collective-permute-done | bytes 1081376 | tf_op jit(solution)/shard_map/ppermute | solution.py:335
  47.8 5.8 %shard_map.70 = (bf16[144,1024]{1,0:T(8,128)(2,1)S(1)}, bf16[144,1024]{1,0:T(8,128)(2,1)S(1)}, bf16[144,1024]{1,0:T(8,128)(2,1)S(1)}) custom-call(s32[1]{0:T(128)} %bitcast.place, s32[4,4]{1,0:T(4,128)S(1)} %maximum_convert_fusion.q_ids, s32[8,4]{1,0:T(8,128)S(1)} %bitcast.5, s32[8,4]{1,0:T(8,128)S(1)} %bitcast.7, ...), custom_call_target="tpu_custom_call" | custom-call | flops 3221225472 | bytes 2097152 | tf_op jit(solution)/shard_map/pallas_call | solution.py:188
  53.7 2.2 %collective-permute-start.4 = (bf16[144,1024]{1,0:T(8,128)(2,1)S(1)}, bf16[144,1024]{1,0:T(8,128)(2,1)S(1)}, u32[]{:S(2)}, u32[]{:S(2)}) collective-permute-start(bf16[144,1024]{1,0:T(8,128)(2,1)S(1)} %get-tuple-element.33), channel_id=1, source_target_pairs={{0,32},{8,40},{16,48},{24,56},{32,0},{40,8},{48,16},{56,24},{64,96... | collective-permute-start | bytes 884744 | tf_op jit(solution)/shard_map/ppermute | solution.py:345
  55.9 2.9 %collective-permute-start.5 = (bf16[144,1024]{1,0:T(8,128)(2,1)S(1)}, bf16[144,1024]{1,0:T(8,128)(2,1)S(1)}, u32[]{:S(2)}, u32[]{:S(2)}) collective-permute-start(bf16[144,1024]{1,0:T(8,128)(2,1)S(1)} %get-tuple-element.34), channel_id=1, source_target_pairs={{0,48},{8,56},{16,0},{24,8},{32,16},{40,24},{48,32},{56,40},{64,11... | collective-permute-start | bytes 884744 | tf_op jit(solution)/shard_map/ppermute | solution.py:345
  58.8 4.1 %collective-permute-start.6 = (bf16[144,1024]{1,0:T(8,128)(2,1)S(1)}, bf16[144,1024]{1,0:T(8,128)(2,1)S(1)}, u32[]{:S(2)}, u32[]{:S(2)}) collective-permute-start(bf16[144,1024]{1,0:T(8,128)(2,1)S(1)} %get-tuple-element.35), channel_id=1, source_target_pairs={{0,16},{8,24},{16,32},{24,40},{32,48},{40,56},{48,0},{56,8},{64,80... | collective-permute-start | bytes 884744 | tf_op jit(solution)/shard_map/ppermute | solution.py:345
  63.4 2.7 %shard_map.69.p0 = bf16[144,1024]{1,0:T(8,128)(2,1)S(1)} custom-call(s32[1]{0:T(128)} %bitcast.place, s32[4,4]{1,0:T(4,128)S(1)} %maximum_convert_fusion.q_ids, s32[8,4]{1,0:T(8,128)S(1)} %bitcast.6, s32[8,4]{1,0:T(8,128)S(1)} %bitcast.8, bf16[272,512]{1,0:T(8,128)(2,1)S(1)} %fusion.1.refs_0_, bf16[8,512,128]{2,1,0:T(8,128)(2,1)S(1)} %get-tuple-element.30.refs_1_.refs_3_, ...), custom_call_target="tpu_custom_call" | custom-call | flops 1073741824 | bytes 2097152 | tf_op jit(solution)/shard_map/pallas_call | solution.py:188
  66.3 0.7 collective-permute-done.4.p1
  67.0 5.5 %collective-permute-done.5.p2 = bf16[144,1024]{1,0:T(8,128)(2,1)S(1)} collective-permute-done((bf16[144,1024]{1,0:T(8,128)(2,1)S(1)}, bf16[144,1024]{1,0:T(8,128)(2,1)S(1)}, u32[]{:S(2)}, u32[]{:S(2)}) %collective-permute-start.5) | collective-permute-done | bytes 294944 | tf_op jit(solution)/shard_map/ppermute | solution.py:345
  72.4 1.4 %shard_map.71 = (bf16[256,512]{1,0:T(8,128)(2,1)}, bf16[256,512]{1,0:T(8,128)(2,1)S(1)}, bf16[256,512]{1,0:T(8,128)(2,1)S(1)}, bf16[256,512]{1,0:T(8,128)(2,1)S(...) custom-call(bf16[144,1024]{1,0:T(8,128)(2,1)S(1)} %shard_map.69.p0, ...), custom_call_target="tpu_custom_call" | custom-call | flops 402653184 | bytes 1572864 | tf_op jit(solution)/shard_map/pallas_call | solution.py:266
  73.9 3.5 %collective-permute-start.9 = (bf16[256,512]{1,0:T(8,128)(2,1)S(1)}, bf16[256,512]{1,0:T(8,128)(2,1)S(1)}, u32[]{:S(2)}, u32[]{:S(2)}) collective-permute-start(bf16[256,512]{1,0:T(8,128)(2,1)S(1)} %get-tuple-element.43), channel_id=1, source_target_pairs={{0,1},{1,2},{2,3},{3,4},{4,5},{5,6},{6,7},{7,0},{8,9},{9,10},{10,1... | collective-permute-start | bytes 786440 | tf_op jit(solution)/shard_map/ppermute | solution.py:297
  77.4 4.5 %collective-permute-start.10 = (bf16[256,256]{1,0:T(8,128)(2,1)S(1)}, bf16[256,256]{1,0:T(8,128)(2,1)S(1)}, u32[]{:S(2)}, u32[]{:S(2)}) collective-permute-start(bf16[256,256]{1,0:T(8,128)(2,1)S(1)} %get-tuple-element.44), channel_id=1, source_target_pairs={{0,2},{1,3},{2,4},{3,5},{4,6},{5,7},{6,0},{7,1},{8,10},{9,11},{10,... | collective-permute-start | bytes 393224 | tf_op jit(solution)/shard_map/ppermute | solution.py:297
  81.9 3.5 %collective-permute-start.13 = (bf16[256,256]{1,0:T(8,128)(2,1)S(1)}, bf16[256,256]{1,0:T(8,128)(2,1)S(1)}, u32[]{:S(2)}, u32[]{:S(2)}) collective-permute-start(bf16[256,256]{1,0:T(8,128)(2,1)S(1)} %get-tuple-element.47), channel_id=1, source_target_pairs={{0,6},{1,7},{2,0},{3,1},{4,2},{5,3},{6,4},{7,5},{8,14},{9,15},{10,... | collective-permute-start | bytes 393224 | tf_op jit(solution)/shard_map/ppermute | solution.py:297
  85.3 2.6 %collective-permute-start.12 = (bf16[256,512]{1,0:T(8,128)(2,1)S(1)}, bf16[256,512]{1,0:T(8,128)(2,1)S(1)}, u32[]{:S(2)}, u32[]{:S(2)}) collective-permute-start(bf16[256,512]{1,0:T(8,128)(2,1)S(1)} %get-tuple-element.46), channel_id=1, source_target_pairs={{0,7},{1,0},{2,1},{3,2},{4,3},{5,4},{6,5},{7,6},{8,15},{9,8},{10,9... | collective-permute-start | bytes 786440 | tf_op jit(solution)/shard_map/ppermute | solution.py:297
  87.9 0.8 shard_map.72
  88.8 3.3 %collective-permute-start.7 = (bf16[256,512]{1,0:T(8,128)(2,1)S(1)}, bf16[256,512]{1,0:T(8,128)(2,1)S(1)}, u32[]{:S(2)}, u32[]{:S(2)}) collective-permute-start(bf16[256,512]{1,0:T(8,128)(2,1)S(1)} %get-tuple-element.40), channel_id=1, source_target_pairs={{0,1},{1,2},{2,3},{3,4},{4,5},{5,6},{6,7},{7,0},{8,9},{9,10},{10,1... | collective-permute-start | bytes 786440 | tf_op jit(solution)/shard_map/ppermute | solution.py:297
  92.1 3.8 %collective-permute-start.8 = (bf16[256,512]{1,0:T(8,128)(2,1)S(1)}, bf16[256,512]{1,0:T(8,128)(2,1)S(1)}, u32[]{:S(2)}, u32[]{:S(2)}) collective-permute-start(bf16[256,512]{1,0:T(8,128)(2,1)S(1)} %get-tuple-element.41), channel_id=1, source_target_pairs={{0,7},{1,0},{2,1},{3,2},{4,3},{5,4},{6,5},{7,6},{8,15},{9,8},{10,9... | collective-permute-start | bytes 786440 | tf_op jit(solution)/shard_map/ppermute | solution.py:297
  96.0 3.0 %collective-permute-start.11 = (bf16[256,512]{1,0:T(8,128)(2,1)S(1)}, bf16[256,512]{1,0:T(8,128)(2,1)S(1)}, u32[]{:S(2)}, u32[]{:S(2)}) collective-permute-start(bf16[256,512]{1,0:T(8,128)(2,1)S(1)} %add_convert_fusion.2), channel_id=1, source_target_pairs={{0,2},{1,3},{2,4},{3,5},{4,6},{5,7},{6,0},{7,1},{8,10},{9,11},{10,... | collective-permute-start | bytes 786440 | tf_op jit(solution)/shard_map/ppermute | solution.py:297
  99.1 4.9 %collective-permute-start.14 = (bf16[256,512]{1,0:T(8,128)(2,1)S(1)}, bf16[256,512]{1,0:T(8,128)(2,1)S(1)}, u32[]{:S(2)}, u32[]{:S(2)}) collective-permute-start(bf16[256,512]{1,0:T(8,128)(2,1)S(1)} %add_convert_fusion.1), channel_id=1, source_target_pairs={{0,6},{1,7},{2,0},{3,1},{4,2},{5,3},{6,4},{7,5},{8,14},{9,15},{10,... | collective-permute-start | bytes 786440 | tf_op jit(solution)/shard_map/ppermute | solution.py:297
  104.1 8.4 %collective-permute-done.11 = bf16[256,512]{1,0:T(8,128)(2,1)S(1)} collective-permute-done((bf16[256,512]{1,0:T(8,128)(2,1)S(1)}, bf16[256,512]{1,0:T(8,128)(2,1)S(1)}, u32[]{:S(2)}, u32[]{:S(2)}) %collective-permute-start.11) | collective-permute-done | bytes 262176 | tf_op jit(solution)/shard_map/ppermute | solution.py:297
  112.4 3.6 %collective-permute-done.14 = bf16[256,512]{1,0:T(8,128)(2,1)S(1)} collective-permute-done((bf16[256,512]{1,0:T(8,128)(2,1)S(1)}, bf16[256,512]{1,0:T(8,128)(2,1)S(1)}, u32[]{:S(2)}, u32[]{:S(2)}) %collective-permute-start.14) | collective-permute-done | bytes 262176 | tf_op jit(solution)/shard_map/ppermute | solution.py:297
  116.1 0.9 add_convert_fusion
  (29 shorter events, 0.9 us)
Async XLA Ops:
  0.6 13.1 %copy-start.1 = (bf16[256,512]{1,0:T(8,128)(2,1)S(1)}, bf16[256,512]{1,0:T(8,128)(2,1)}, u32[]{:S(2)}) copy-start(bf16[256,512]{1,0:T(8,128)(2,1)} %param.5) | copy-start | bytes 786436
  3.4 39.8 %all-to-all-start = ((bf16[8,528,128]{2,1,0:T(8,128)(2,1)}), bf16[8,528,128]{2,1,0:T(8,128)(2,1)S(1)}, u32[]{:S(2)}, u32[]{:S(2)}) async-start(bf16[8,528,128]{2,1,0:T(8,128)(2,1)} %broadcast_in_dim.5), calls=%async_computation | async-start | bytes 2162688 | tf_op jit(solution)/shard_map/all_to_all | solution.py:326
  13.7 17.2 %collective-permute-start.2 = (bf16[272,512]{1,0:T(8,128)(2,1)S(1)}, bf16[272,512]{1,0:T(8,128)(2,1)S(1)}, u32[]{:S(2)}, u32[]{:S(2)}) collective-permute-start(bf16[272,512]{1,0:T(8,128)(2,1)S(1)} %fusion.1.refs_0_), channel_id=1, source_target_pairs={{0,48},{8,56},{16,0},{24,8},{32,16},{40,24},{48,32},{56,40},{64,11... | collective-permute-start | bytes 835592 | tf_op jit(solution)/shard_map/ppermute | solution.py:322
  16.5 14.4 %collective-permute-start.1 = (bf16[272,512]{1,0:T(8,128)(2,1)S(1)}, bf16[272,512]{1,0:T(8,128)(2,1)S(1)}, u32[]{:S(2)}, u32[]{:S(2)}) collective-permute-start(bf16[272,512]{1,0:T(8,128)(2,1)S(1)} %fusion.1.refs_0_), channel_id=1, source_target_pairs={{0,32},{8,40},{16,48},{24,56},{32,0},{40,8},{48,16},{56,24},{64,96... | collective-permute-start | bytes 835592 | tf_op jit(solution)/shard_map/ppermute | solution.py:322
  19.5 14.0 %collective-permute-start = (bf16[272,512]{1,0:T(8,128)(2,1)S(1)}, bf16[272,512]{1,0:T(8,128)(2,1)S(1)}, u32[]{:S(2)}, u32[]{:S(2)}) collective-permute-start(bf16[272,512]{1,0:T(8,128)(2,1)S(1)} %fusion.1.refs_0_), channel_id=1, source_target_pairs={{0,16},{8,24},{16,32},{24,40},{32,48},{40,56},{48,0},{56,8},{64,80... | collective-permute-start | bytes 835592 | tf_op jit(solution)/shard_map/ppermute | solution.py:322
  43.1 4.6 %collective-permute-start.3 = (bf16[8,528,128]{2,1,0:T(8,128)(2,1)S(1)}, bf16[8,528,128]{2,1,0:T(8,128)(2,1)S(1)}, u32[]{:S(2)}, u32[]{:S(2)}) collective-permute-start(bf16[8,528,128]{2,1,0:T(8,128)(2,1)S(1)} %all-to-all-done.kv_own), channel_id=1, source_target_pairs={{0,8},{8,0},{16,24},{24,16},{32,40},{40,32},{48,56},{56,48},{64,72... | collective-permute-start | bytes 3244040 | tf_op jit(solution)/shard_map/ppermute | solution.py:335
  47.8 15.1 %copy-start = (bf16[512,4096]{1,0:T(8,128)(2,1)S(1)}, bf16[512,4096]{1,0:T(8,128)(2,1)}, u32[]{:S(2)}) copy-start(bf16[512,4096]{1,0:T(8,128)(2,1)} %param.9) | copy-start | bytes 12582916
  53.7 13.3 %collective-permute-start.4 = (bf16[144,1024]{1,0:T(8,128)(2,1)S(1)}, bf16[144,1024]{1,0:T(8,128)(2,1)S(1)}, u32[]{:S(2)}, u32[]{:S(2)}) collective-permute-start(bf16[144,1024]{1,0:T(8,128)(2,1)S(1)} %get-tuple-element.33), channel_id=1, source_target_pairs={{0,32},{8,40},{16,48},{24,56},{32,0},{40,8},{48,16},{56,24},{64,96... | collective-permute-start | bytes 884744 | tf_op jit(solution)/shard_map/ppermute | solution.py:345
  55.9 16.5 %collective-permute-start.5 = (bf16[144,1024]{1,0:T(8,128)(2,1)S(1)}, bf16[144,1024]{1,0:T(8,128)(2,1)S(1)}, u32[]{:S(2)}, u32[]{:S(2)}) collective-permute-start(bf16[144,1024]{1,0:T(8,128)(2,1)S(1)} %get-tuple-element.34), channel_id=1, source_target_pairs={{0,48},{8,56},{16,0},{24,8},{32,16},{40,24},{48,32},{56,40},{64,11... | collective-permute-start | bytes 884744 | tf_op jit(solution)/shard_map/ppermute | solution.py:345
  58.8 13.6 %collective-permute-start.6 = (bf16[144,1024]{1,0:T(8,128)(2,1)S(1)}, bf16[144,1024]{1,0:T(8,128)(2,1)S(1)}, u32[]{:S(2)}, u32[]{:S(2)}) collective-permute-start(bf16[144,1024]{1,0:T(8,128)(2,1)S(1)} %get-tuple-element.35), channel_id=1, source_target_pairs={{0,16},{8,24},{16,32},{24,40},{32,48},{40,56},{48,0},{56,8},{64,80... | collective-permute-start | bytes 884744 | tf_op jit(solution)/shard_map/ppermute | solution.py:345
  73.9 22.0 %collective-permute-start.9 = (bf16[256,512]{1,0:T(8,128)(2,1)S(1)}, bf16[256,512]{1,0:T(8,128)(2,1)S(1)}, u32[]{:S(2)}, u32[]{:S(2)}) collective-permute-start(bf16[256,512]{1,0:T(8,128)(2,1)S(1)} %get-tuple-element.43), channel_id=1, source_target_pairs={{0,1},{1,2},{2,3},{3,4},{4,5},{5,6},{6,7},{7,0},{8,9},{9,10},{10,1... | collective-permute-start | bytes 786440 | tf_op jit(solution)/shard_map/ppermute | solution.py:297
  77.4 14.7 %collective-permute-start.10 = (bf16[256,256]{1,0:T(8,128)(2,1)S(1)}, bf16[256,256]{1,0:T(8,128)(2,1)S(1)}, u32[]{:S(2)}, u32[]{:S(2)}) collective-permute-start(bf16[256,256]{1,0:T(8,128)(2,1)S(1)} %get-tuple-element.44), channel_id=1, source_target_pairs={{0,2},{1,3},{2,4},{3,5},{4,6},{5,7},{6,0},{7,1},{8,10},{9,11},{10,... | collective-permute-start | bytes 393224 | tf_op jit(solution)/shard_map/ppermute | solution.py:297
  81.9 17.2 %collective-permute-start.13 = (bf16[256,256]{1,0:T(8,128)(2,1)S(1)}, bf16[256,256]{1,0:T(8,128)(2,1)S(1)}, u32[]{:S(2)}, u32[]{:S(2)}) collective-permute-start(bf16[256,256]{1,0:T(8,128)(2,1)S(1)} %get-tuple-element.47), channel_id=1, source_target_pairs={{0,6},{1,7},{2,0},{3,1},{4,2},{5,3},{6,4},{7,5},{8,14},{9,15},{10,... | collective-permute-start | bytes 393224 | tf_op jit(solution)/shard_map/ppermute | solution.py:297
  85.3 13.7 %collective-permute-start.12 = (bf16[256,512]{1,0:T(8,128)(2,1)S(1)}, bf16[256,512]{1,0:T(8,128)(2,1)S(1)}, u32[]{:S(2)}, u32[]{:S(2)}) collective-permute-start(bf16[256,512]{1,0:T(8,128)(2,1)S(1)} %get-tuple-element.46), channel_id=1, source_target_pairs={{0,7},{1,0},{2,1},{3,2},{4,3},{5,4},{6,5},{7,6},{8,15},{9,8},{10,9... | collective-permute-start | bytes 786440 | tf_op jit(solution)/shard_map/ppermute | solution.py:297
  88.8 15.3 %collective-permute-start.7 = (bf16[256,512]{1,0:T(8,128)(2,1)S(1)}, bf16[256,512]{1,0:T(8,128)(2,1)S(1)}, u32[]{:S(2)}, u32[]{:S(2)}) collective-permute-start(bf16[256,512]{1,0:T(8,128)(2,1)S(1)} %get-tuple-element.40), channel_id=1, source_target_pairs={{0,1},{1,2},{2,3},{3,4},{4,5},{5,6},{6,7},{7,0},{8,9},{9,10},{10,1... | collective-permute-start | bytes 786440 | tf_op jit(solution)/shard_map/ppermute | solution.py:297
  92.1 12.0 %collective-permute-start.8 = (bf16[256,512]{1,0:T(8,128)(2,1)S(1)}, bf16[256,512]{1,0:T(8,128)(2,1)S(1)}, u32[]{:S(2)}, u32[]{:S(2)}) collective-permute-start(bf16[256,512]{1,0:T(8,128)(2,1)S(1)} %get-tuple-element.41), channel_id=1, source_target_pairs={{0,7},{1,0},{2,1},{3,2},{4,3},{5,4},{6,5},{7,6},{8,15},{9,8},{10,9... | collective-permute-start | bytes 786440 | tf_op jit(solution)/shard_map/ppermute | solution.py:297
  96.0 16.5 %collective-permute-start.11 = (bf16[256,512]{1,0:T(8,128)(2,1)S(1)}, bf16[256,512]{1,0:T(8,128)(2,1)S(1)}, u32[]{:S(2)}, u32[]{:S(2)}) collective-permute-start(bf16[256,512]{1,0:T(8,128)(2,1)S(1)} %add_convert_fusion.2), channel_id=1, source_target_pairs={{0,2},{1,3},{2,4},{3,5},{4,6},{5,7},{6,0},{7,1},{8,10},{9,11},{10,... | collective-permute-start | bytes 786440 | tf_op jit(solution)/shard_map/ppermute | solution.py:297
  99.1 17.0 %collective-permute-start.14 = (bf16[256,512]{1,0:T(8,128)(2,1)S(1)}, bf16[256,512]{1,0:T(8,128)(2,1)S(1)}, u32[]{:S(2)}, u32[]{:S(2)}) collective-permute-start(bf16[256,512]{1,0:T(8,128)(2,1)S(1)} %add_convert_fusion.1), channel_id=1, source_target_pairs={{0,6},{1,7},{2,0},{3,1},{4,2},{5,3},{6,4},{7,5},{8,14},{9,15},{10,... | collective-permute-start | bytes 786440 | tf_op jit(solution)/shard_map/ppermute | solution.py:297
